TPU v7x, 256 devices: a whole 4x4x8 slice. The times are simulated.
256 devices in a mesh: dp: 32 (over y, x, core), mp: 8 (over z).
Axes of the slice: x: 4, y: 4, z: 8, core: 2. Of those that a mesh axis runs over, the one named last changes fastest.
Arguments:
- tokens: bfloat16 [32768, 2048], P(('dp', 'mp')), may hold values from -6 to 6
- out_grad: bfloat16 [32768, 7168], P('dp', 'mp'), may hold values from -0.1875 to 0.1875
- error: bfloat16 [32, 2048, 7168], P('dp', None, 'mp'), may hold values from -6 to 6
- q_prev: float32 [8, 7168], P(None, 'mp'), may hold values from -6 to 6
Outputs:
- p_factor: float32 [8, 2048], replicated
- q_factor: float32 [8, 7168], P(None, 'mp')
- new_error: bfloat16 [32, 2048, 7168], P('dp', None, 'mp')
All inputs are finite; a program needn't handle non-finite values.
Results may differ from a plain program's by a relative error of at most 0.0004.
Values may be sent and summed in bfloat16 or wider, within the bound.
No kernel may reach another device: no remote copies, remote signals or barrier semaphores. Data moves between devices by JAX's collectives and lax.ppermute only.
A program may use at most 64 MiB of HBM per device.

v0:
```python
import jax
import jax.numpy as jnp
from jax import lax
from jax.sharding import PartitionSpec as P


def orthonormal(rows):
    done = []
    for index in range(rows.shape[0]):
        vector = rows[index]
        for earlier in done:
            vector = vector - jnp.sum(vector * earlier) * earlier
        vector = vector / jnp.sqrt(jnp.sum(vector * vector) + 1e-06)
        done.append(vector)
    return jnp.stack(done)


def on_device(tokens, out_grad, error, q_prev):
    high = lax.Precision.HIGHEST
    inner = (((0,), (0,)), ((), ()))
    across = (((1,), (1,)), ((), ()))
    err_local = error[0].astype(jnp.float32)
    grad = lax.dot_general(
        lax.all_gather(tokens, "mp", axis=0, tiled=True),
        out_grad,
        inner,
        preferred_element_type=jnp.float32,
    )
    merged = grad + err_local
    partial_value = lax.dot_general(q_prev, merged, across, precision=high)
    summed = lax.psum(partial_value, "mp")
    summed = lax.psum(summed, "dp")
    p_factor = orthonormal(summed)
    q_local = jnp.dot(p_factor, merged, precision=high)
    q_factor = lax.psum(q_local, "dp") / lax.axis_size("dp")
    new_error = (merged - jnp.dot(p_factor.T, q_factor, precision=high)).astype(jnp.bfloat16)
    return (p_factor, q_factor, new_error[None])


def solution(mesh):
    placed = (P(("dp", "mp"), None), P("dp", "mp"), P("dp", None, "mp"), P(None, "mp"))
    return jax.shard_map(
        on_device,
        mesh=mesh,
        in_specs=placed,
        out_specs=(P(), P(None, "mp"), P("dp", None, "mp")),
        check_vma=False,
    )
```

profile of v0, /device:TPU:1, one launch (start us, length us, event | category | flops | bytes accessed | tf_op | source)
XLA Modules:
  0.0 473.9 jit_solution(13876447468016021796)
XLA Ops:
  7.2 0.0 copy-start
  7.2 0.0 all-gather.2.cloned.1.call-start
  7.2 0.7 all-gather.2.cloned.1.call-update
  7.9 0.0 copy-start.4
  7.9 0.0 all-reduce.3.cloned.1.call-start
  8.0 60.5 %all-gather.2.cloned.1.call-done = bf16[1024,2048]{1,0:T(8,128)(2,1)} async-done(((bf16[128,2048]{1,0:T(8,128)(2,1)}), bf16[1024,2048]{1,0:T(8,128)(2,1)}) %all-gather.2.cloned.1.call-update) | async-done | bytes 4194320 | tf_op jit(solution)/shard_map/all_gather | solution.py:24
  68.5 0.0 copy-done
  68.5 8.2 %convert_add_fusion = f32[2048,896]{1,0:T(8,128)S(1)} fusion(bf16[1,2048,896]{2,1,0:T(8,128)(2,1)} %param.6, bf16[1024,2048]{1,0:T(8,128)(2,1)} %all-gather.2.cloned.1.call-done, bf16[1024,896]{1,0:T(8,128)(2,1)S(1)} %copy-done), kind=kOutput, calls=%fused_computation | convolution fusion | flops 3761766400 | bytes 17039360 | tf_op jit(solution)/shard_map/dot_general | solution.py:23
  76.6 0.0 copy-start.1
  76.6 3.0 copy-done.1
  79.6 0.0 copy-done.4
  79.6 6.9 %convolution_bitcast_fusion = f32[8,2048]{1,0:T(8,128)} fusion(f32[2048,896]{1,0:T(8,128)S(1)} %convert_add_fusion, f32[8,896]{1,0:T(8,128)S(1)} %copy-done.4), kind=kOutput, calls=%fused_computation.3 | convolution fusion | flops 176160768 | bytes 7434240 | tf_op jit(solution)/shard_map/dot_general | solution.py:30
  86.5 0.0 all-reduce.3.cloned.1.call-update
  86.5 0.2 all-reduce.5.cloned.1.call-start
  86.7 64.9 %all-reduce.3.cloned.1.call-done = f32[8,2048]{1,0:T(8,128)} async-done(((f32[8,2048]{1,0:T(8,128)}), f32[8,2048]{1,0:T(8,128)}) %all-reduce.3.cloned.1.call-update) | async-done | bytes 65552 | tf_op jit(solution)/shard_map/psum | solution.py:31
  151.6 0.0 all-reduce.5.cloned.1.call-update
  151.7 113.0 %all-reduce.5.cloned.1.call-done = f32[8,2048]{1,0:T(8,128)} async-done(((f32[8,2048]{1,0:T(8,128)}), f32[8,2048]{1,0:T(8,128)}) %all-reduce.5.cloned.1.call-update) | async-done | bytes 65552 | tf_op jit(solution)/shard_map/psum | solution.py:32
  264.6 1.5 multiply_reduce_fusion.35
  266.8 1.3 fusion.1
  268.1 0.6 multiply_reduce_fusion.34
  268.7 1.3 multiply_reduce_fusion.7
  270.8 5.1 %multiply_reduce_fusion.6 = (f32[]{:T(128)}, f32[]{:T(128)}, f32[]{:T(128)}, f32[]{:T(128)}, f32[]{:T(128)}, /*index=5*/f32[]{:T(128)}, f32[2048]{0:T(1024)S(1)}) fusion(f32[2048]{0:T(1024)S(1)} %bitcast.30, f32[2048]{0:T(1024)S(1)} %bitcast.25, f32[]{:T(128)} %get-tuple-element.23, f32[2048]{0:T(1024)S(1)} %bitcast.33, f32[]{:T(128)} %get-tuple-element.24, ...), kind=kLoop, calls=%fused_computation.17 | loop fusion | flops 55290 | bytes 73784 | tf_op jit(solution)/shard_map/reduce_sum | solution.py:12
  275.9 2.0 multiply_reduce_fusion.30
  278.6 1.9 multiply_reduce_fusion.27
  280.5 6.4 %multiply_reduce_fusion.5 = (f32[]{:T(128)}, f32[]{:T(128)}, f32[]{:T(128)}, f32[]{:T(128)}, f32[]{:T(128)}, /*index=5*/f32[2048]{0:T(1024)S(1)}, f32[2048]{0:T(1024)S(1)}, f32[2048]{0:T(1024)S(1)}, f32[2048]{0:T(1024)S(1)}) fusion(f32[2048]{0:T(1024)S(1)} %get-tuple-element.54, f32[]{:T(128)S(6)} %sqrt.26, f32[2048]{0:T(1024)S(1)} %get-tuple-element.52, ...), kind=kLoop, calls=%fused_computation.15 | loop fusion | flops 59387 | bytes 98364 | tf_op jit(solution)/shard_map/reduce_sum | solution.py:12
  287.6 3.8 multiply_reduce_fusion.4
  291.4 2.7 multiply_reduce_fusion.21
  294.8 2.6 multiply_reduce_fusion.16
  297.4 4.4 multiply_reduce_fusion.3
  302.5 2.6 multiply_reduce_fusion.2
  305.1 2.6 multiply_reduce_fusion.8
  308.4 2.7 multiply_reduce_fusion.1
  311.1 1.3 multiply_reduce_fusion
  313.0 19.0 %subtract_divide_fusion = (f32[1,2048]{1,0:T(1,128)S(1)}, f32[1,2048]{1,0:T(1,128)S(1)}, f32[1,2048]{1,0:T(1,128)S(1)}, f32[1,2048]{1,0:T(1,128)S(1)}, f32[1,204...) fusion(f32[1,2048]{1,0:T(1,128)S(1)} %get-tuple-element.57, f32[]{:T(128)S(6)} %sqrt.31, ...), kind=kLoop, calls=%fused_computation.6 | loop fusion | flops 129024 | bytes 123020 | tf_op jit(solution)/shard_map/div | solution.py:13
  332.1 0.1 stack.2
  332.2 0.0 copy-start.2
  332.2 5.6 %fusion.2 = f32[8,896]{1,0:T(8,128)S(1)} fusion(f32[8,2048]{1,0:T(8,128)S(1)} %stack.2, f32[2048,896]{1,0:T(8,128)} %copy-done.1), kind=kOutput, calls=%fused_computation.83 | convolution fusion | flops 176160768 | bytes 7434240 | tf_op jit(solution)/shard_map/dot_general | solution.py:34
  337.8 120.0 %psum.23 = f32[8,896]{1,0:T(8,128)S(1)} all-reduce(f32[8,896]{1,0:T(8,128)S(1)} %fusion.2), channel_id=1, replica_groups=mesh['dp'=32,'mp'=8] {'dp'}, use_global_device_ids=true, to_apply=%region_38.0 | all-reduce | flops 7168 | bytes 57344 | tf_op jit(solution)/shard_map/psum | solution.py:35
  457.8 0.0 copy-start.3
  457.9 9.5 %fusion = bf16[1,2048,896]{2,1,0:T(8,128)(2,1)} fusion(f32[2048,896]{1,0:T(8,128)} %copy-done.1, f32[8,2048]{1,0:T(8,128)S(1)} %stack.2, f32[8,896]{1,0:T(8,128)S(1)} %broadcast_multiply_fusion), kind=kOutput, calls=%fused_computation.2 | convolution fusion | flops 179830784 | bytes 11104256 | tf_op jit(solution)/shard_map/dot_general | solution.py:36
  467.3 0.0 copy-done.2
  467.3 0.0 copy-done.3
  (1 shorter events, 0.0 us)
Async XLA Ops:
  7.2 61.3 %copy-start = (bf16[1024,896]{1,0:T(8,128)(2,1)S(1)}, bf16[1024,896]{1,0:T(8,128)(2,1)}, u32[]{:S(2)}) copy-start(bf16[1024,896]{1,0:T(8,128)(2,1)} %param.5) | copy-start | bytes 5505028
  7.2 61.3 %all-gather.2.cloned.1.call-start = ((), (), s32[]{:S(2)}) async-start(), calls=%async_computation | async-start | bytes 4718592 | tf_op jit(solution)/shard_map/all_gather | solution.py:24
  7.9 71.7 %copy-start.4 = (f32[8,896]{1,0:T(8,128)S(1)}, f32[8,896]{1,0:T(8,128)}, u32[]{:S(2)}) copy-start(f32[8,896]{1,0:T(8,128)} %param.7) | copy-start | bytes 86020
  7.9 143.7 %all-reduce.3.cloned.1.call-start = ((), (), s32[]{:S(2)}) async-start(), calls=%async_computation.1 | async-start | bytes 131072 | tf_op jit(solution)/shard_map/psum | solution.py:31
  76.6 3.0 copy-start.1
  86.5 178.2 %all-reduce.5.cloned.1.call-start = ((), (), s32[]{:S(2)}) async-start(), calls=%async_computation.2 | async-start | bytes 131072 | tf_op jit(solution)/shard_map/psum | solution.py:32
  332.2 135.2 %copy-start.2 = (f32[8,2048]{1,0:T(8,128)}, f32[8,2048]{1,0:T(8,128)S(1)}, u32[]{:S(2)}) copy-start(f32[8,2048]{1,0:T(8,128)S(1)} %stack.2) | copy-start | bytes 196612
  457.8 9.5 %copy-start.3 = (f32[8,896]{1,0:T(8,128)}, f32[8,896]{1,0:T(8,128)S(1)}, u32[]{:S(2)}) copy-start(f32[8,896]{1,0:T(8,128)S(1)} %broadcast_multiply_fusion) | copy-start | bytes 86020
Sparse Core Ops, SparseCore 0:
  9.8 58.6 all-gather.1
  86.6 64.9 all-reduce.2
  155.2 109.3 all-reduce.4
where the time goes:
time: 479 us; the launch traced here: 474 us
  waiting for transfers between devices  239 us (50%)
  blocking collectives  120 us (25%)
  other arithmetic  61.9 us (13%)
  matrix products  30.1 us (6%)
  between operations  19.4 us (4%)
    psum x1, blocking collectives, on_device(): q_factor = lax.psum(q_local, 'dp') / lax.axis_size('dp')  120 us
    psum x1, waiting for transfers between devices, on_device(): summed = lax.psum(summed, 'dp')  113 us
    psum x1, waiting for transfers between devices, on_device(): summed = lax.psum(partial_value, 'mp')  64.9 us
    all_gather x1, waiting for transfers between devices, on_device(): lax.all_gather(tokens, 'mp', axis=0, tiled=True)  60.5 us
    reduce_sum x10, other arithmetic, orthonormal(): vector = vector - jnp.sum(vector * earlier) * earlier  31.5 us
    div x1, other arithmetic, orthonormal(): vector = vector / jnp.sqrt(jnp.sum(vector * vector) + 1e-06)  19 us
    reduce_sum x5, other arithmetic, orthonormal(): vector = vector / jnp.sqrt(jnp.sum(vector * vector) + 1e-06)  9.97 us
  transfers between devices with their start and end apart: 3, of which 3 were waited for; matrix products, arithmetic and copies ran while one was open for 0% of the time, Pallas kernels for 0%

commit v1 on v0

v1 whole, which is shorter than its diff:
```python
import functools

import jax
import jax.numpy as jnp
from jax import lax
from jax.experimental import pallas as pl
from jax.experimental.pallas import tpu as pltpu
from jax.sharding import PartitionSpec as P

MP = 8
DP = 32
R = 8


def shift(size, step):
    return [(i, (i + step) % size) for i in range(size)]


CORES = [(i, i ^ 1) for i in range(DP)]
CHIPS = [[2 * i for i in range(DP // 2)], [2 * i + 1 for i in range(DP // 2)]]


def split3(x):
    first = lax.reduce_precision(x, 8, 7)
    rest = x - first
    second = lax.reduce_precision(rest, 8, 7)
    third = rest - second
    return jnp.concatenate([first, second, third], axis=0).astype(jnp.bfloat16)


def fold3(x):
    rows = x.shape[0] // 3
    return (x[2 * rows :] + x[rows : 2 * rows]) + x[:rows]


def dot(a, b, contract):
    return lax.dot_general(a, b, (contract, ((), ())), preferred_element_type=jnp.float32)


def gram_schmidt_kernel(rows_ref, out_ref):
    rows = rows_ref[...]
    index = lax.broadcasted_iota(jnp.int32, (R, 1), 0)
    for i in range(R):
        vector = rows[i : i + 1]
        norm = jnp.sqrt(jnp.sum(vector * vector, axis=1, keepdims=True) + 1e-06)
        vector = vector / norm
        products = jnp.sum(rows * vector, axis=1, keepdims=True)
        rows = jnp.where(index > i, rows - products * vector, jnp.where(index == i, vector, rows))
    out_ref[...] = rows


def gram_schmidt(rows):
    return pl.pallas_call(
        gram_schmidt_kernel,
        out_shape=jax.ShapeDtypeStruct(rows.shape, rows.dtype),
        in_specs=[pl.BlockSpec(memory_space=pltpu.VMEM)],
        out_specs=pl.BlockSpec(memory_space=pltpu.VMEM),
    )(rows)


def spread(x, axis, size, groups=None):
    wide = jnp.broadcast_to(x[None], (size,) + x.shape)
    return lax.all_to_all(wide, axis, 0, 0, axis_index_groups=groups)


def on_device(tokens, out_grad, error, q_prev):
    err = error[0]
    me = lax.axis_index("mp")
    core = lax.axis_index("dp") % 2
    half = tokens.shape[0] // 2
    rows = tokens.shape[0]

    blocks, order = [tokens], [me]
    right = left = tokens
    for step in range(1, 4):
        right = lax.ppermute(right, "mp", shift(MP, 1))
        left = lax.ppermute(left, "mp", shift(MP, -1))
        blocks += [right, left]
        order += [(me - step) % MP, (me + step) % MP]
    top = lax.ppermute(right[:half], "mp", shift(MP, 1))
    bottom = lax.ppermute(left[half:], "mp", shift(MP, -1))
    blocks += [top, bottom]
    order += [(me + 4) % MP]
    gathered = jnp.concatenate(blocks, axis=0)
    grads = jnp.concatenate([lax.dynamic_slice_in_dim(out_grad, o * rows, rows, 0) for o in order], axis=0)

    q_terms = split3(q_prev)
    reduced = fold3(dot(q_terms, out_grad, ((1,), (1,))))
    reduced = reduced.reshape(R, MP, rows).transpose(1, 0, 2)
    reduced = jnp.sum(lax.all_to_all(reduced, "mp", 0, 0), axis=0)
    part = fold3(dot(split3(reduced), tokens, ((1,), (0,)))) + fold3(dot(q_terms, err, ((1,), (1,))))
    width = part.shape[1] // MP
    part = part.reshape(R, MP, width).transpose(1, 0, 2)
    part = jnp.sum(lax.all_to_all(part, "mp", 0, 0), axis=0)
    part = jnp.sum(spread(part, "dp", DP), axis=0)
    p_sum = spread(part, "mp", MP).transpose(1, 0, 2).reshape(R, MP * width)
    p_factor = gram_schmidt(p_sum)

    p_terms = split3(p_factor)
    projected = fold3(dot(p_terms, gathered, ((1,), (1,))))
    q_local = fold3(dot(split3(projected), grads, ((1,), (0,)))) + fold3(dot(p_terms, err, ((1,), (0,))))
    columns = q_local.shape[1]
    wide = jnp.pad(q_local, ((0, 0), (0, 1024 - columns))).reshape(R, 2, 512).transpose(1, 0, 2)
    keep = lax.dynamic_index_in_dim(wide, core, 0, False)
    send = lax.dynamic_index_in_dim(wide, 1 - core, 0, False)
    mine = keep + lax.ppermute(send, "dp", CORES)
    mine = jnp.sum(spread(mine, "dp", DP // 2, CHIPS), axis=0) / DP
    other = lax.ppermute(mine, "dp", CORES)
    first = jnp.where(core == 0, mine, other)
    second = jnp.where(core == 0, other, mine)
    q_factor = jnp.concatenate([first, second], axis=1)[:, :columns]

    grad = dot(gathered, grads, ((0,), (0,)))
    q_terms = split3(q_factor)
    left_terms = jnp.concatenate([p_terms[:8], p_terms[:8], p_terms[:8], p_terms[8:16], p_terms[8:16], p_terms[16:]], axis=0)
    right_terms = jnp.concatenate([q_terms, q_terms[:16], q_terms[:8]], axis=0)
    new_error = (grad + err.astype(jnp.float32) - dot(left_terms, right_terms, ((0,), (0,)))).astype(jnp.bfloat16)
    return (p_factor, q_factor, new_error[None])


def solution(mesh):
    placed = (P(("dp", "mp"), None), P("dp", "mp"), P("dp", None, "mp"), P(None, "mp"))
    return jax.shard_map(
        on_device,
        mesh=mesh,
        in_specs=placed,
        out_specs=(P(), P(None, "mp"), P("dp", None, "mp")),
        check_vma=False,
    )
```

time: 479 us -> 131 us (0.27)
  waiting for transfers between devices: 239 us -> 31.8 us
  blocking collectives: 120 us -> 11.7 us
  other arithmetic: 61.9 us -> 5.24 us
  starting transfers between devices: 0.3 us -> 44.9 us
  between operations: 19.4 us -> 0.95 us
  matrix products: 30.1 us -> 17 us
  local copies, waits for them, and re-layouts: 3.09 us -> 15.6 us
    psum x2 -> x0, waiting for transfers between devices: 178 us -> none  [the longest x1 113 us: on_device(): summed = lax.psum(summed, 'dp')]
    psum x1 -> x0, blocking collectives: 120 us -> none  [on_device(): q_factor = lax.psum(q_local, 'dp') / lax.axis_size('dp')]
    all_gather x1 -> x0, waiting for transfers between devices: 60.5 us -> none  [on_device(): lax.all_gather(tokens, 'mp', axis=0, tiled=True)]
    reduce_sum x15 -> x4, other arithmetic: 41.5 us -> 0.08 us  [the longest x1 0.04 us: on_device(): part = jnp.sum(spread(part, 'dp', DP), axis=0)]
    all_to_all x0 -> x4, starting transfers between devices: none -> 25.5 us  [the longest x2 13.7 us: spread(): return lax.all_to_all(wide, axis, 0, 0, axis_index_groups=groups)]
    ppermute x0 -> x10, starting transfers between devices: none -> 19.4 us  [the longest x3 8.12 us: on_device(): left = lax.ppermute(left, 'mp', shift(MP, -1))]
    div x2 -> x1, other arithmetic: 19 us -> 0.01 us  [on_device(): mine = jnp.sum(spread(mine, 'dp', DP // 2, CHIPS), axis=0) / DP]
    ppermute x0 -> x10, waiting for transfers between devices: none -> 16.4 us  [the longest x3 10.5 us: on_device(): right = lax.ppermute(right, 'mp', shift(MP, 1))]
  transfers between devices with their start and end apart: 3 -> 14, of which waited for: 3 -> 8; matrix products, arithmetic and copies ran while one was open for 0% -> 18% of each run, Pallas kernels for 0% -> 2%
where the time goes in v1:
time: 131 us; the launch traced here: 130 us
  starting transfers between devices  44.9 us (34%)
  waiting for transfers between devices  31.8 us (24%)
  matrix products  17 us (13%)
  local copies, waits for them, and re-layouts  15.6 us (12%)
  blocking collectives  11.7 us (9%)
  other arithmetic  5.24 us (4%)
  Pallas kernels  3.01 us (2%)
    dot_general x8, matrix products, dot(): lax.dot_general(a, b, (contract, ((), ())), preferred_element_type=jnp.fl...  17 us
    all_to_all x2, starting transfers between devices, spread(): return lax.all_to_all(wide, axis, 0, 0, axis_index_groups=groups)  13.7 us
    unnamed x36, local copies, waits for them, and re-layouts  13.5 us
    all_to_all x1, blocking collectives, spread(): return lax.all_to_all(wide, axis, 0, 0, axis_index_groups=groups)  11.7 us
    ppermute x3, waiting for transfers between devices, on_device(): right = lax.ppermute(right, 'mp', shift(MP, 1))  10.5 us
    all_to_all x2, waiting for transfers between devices, spread(): return lax.all_to_all(wide, axis, 0, 0, axis_index_groups=groups)  8.89 us
    ppermute x3, starting transfers between devices, on_device(): left = lax.ppermute(left, 'mp', shift(MP, -1))  8.12 us
    all_to_all x1, starting transfers between devices, on_device(): part = jnp.sum(lax.all_to_all(part, 'mp', 0, 0), axis=0)  6.65 us
  transfers between devices with their start and end apart: 14, of which 8 were waited for; matrix products, arithmetic and copies ran while one was open for 18% of the time, Pallas kernels for 2%

profile of v1, /device:TPU:1, one launch (start us, length us, event | category | flops | bytes accessed | tf_op | source)
XLA Modules:
  0.0 130.2 jit_solution(1121155550134366311)
XLA Ops:
  0.6 0.0 copy-start.1
  0.6 2.5 %collective-permute-start = (bf16[128,2048]{1,0:T(8,128)(2,1)}, bf16[128,2048]{1,0:T(8,128)(2,1)}, u32[]{:S(2)}, u32[]{:S(2)}) collective-permute-start(bf16[128,2048]{1,0:T(8,128)(2,1)} %param.4), channel_id=1, source_target_pairs={{0,1},{1,2},{2,3},{3,4},{4,5},{5,6},{6,7},{7,0},{8,9},{9,10},{10,1... | collective-permute-start | bytes 1572872 | tf_op jit(solution)/shard_map/ppermute | solution.py:76
  3.2 4.0 %collective-permute-start.1 = (bf16[128,2048]{1,0:T(8,128)(2,1)}, bf16[128,2048]{1,0:T(8,128)(2,1)S(1)}, u32[]{:S(2)}, u32[]{:S(2)}) collective-permute-start(bf16[128,2048]{1,0:T(8,128)(2,1)} %param.4), channel_id=1, source_target_pairs={{0,7},{1,0},{2,1},{3,2},{4,3},{5,4},{6,5},{7,6},{8,15},{9,8},{10,9... | collective-permute-start | bytes 1572872 | tf_op jit(solution)/shard_map/ppermute | solution.py:77
  7.2 0.8 reduce-precision_convert_fusion.7
  8.0 2.1 %fusion.19 = f32[24,1024]{1,0:T(8,128)S(1)} fusion(bf16[1024,896]{1,0:T(8,128)(2,1)} %param.5, bf16[8,896]{1,0:T(8,128)(2,1)S(1)} %get-tuple-element.18, bf16[8,896]{1,0:T(8,128)(2,1)S(1)} %get-tuple-element.19, bf16[8,896]{1,0:T(8,128)(2,1)S(1)} %get-tuple-element.17), kind=kOutput, calls=%fused_computation.80 | convolution fusion | flops 44169216 | bytes 1976320 | tf_op jit(solution)/shard_map/dot_general | solution.py:37
  10.1 0.6 fusion.15
  10.8 5.2 %all-to-all-start = ((f32[8,8,128]{2,1,0:T(8,128)}), f32[8,8,128]{2,1,0:T(8,128)S(1)}, u32[]{:S(2)}, u32[]{:S(2)}) async-start(f32[8,8,128]{2,1,0:T(8,128)} %fusion.15), calls=%async_computation | async-start | bytes 65536 | tf_op jit(solution)/shard_map/all_to_all | solution.py:90
  16.0 3.2 %fusion.3 = f32[24,2048]{1,0:T(8,128)S(1)} fusion(bf16[1,2048,896]{2,1,0:T(8,128)(2,1)} %param.6, bf16[8,896]{1,0:T(8,128)(2,1)S(1)} %get-tuple-element.18, bf16[8,896]{1,0:T(8,128)(2,1)S(1)} %get-tuple-element.19, bf16[8,896]{1,0:T(8,128)(2,1)S(1)} %get-tuple-element.17), kind=kOutput, calls=%fused_computation.4 | convolution fusion | flops 88209408 | bytes 3909632 | tf_op jit(solution)/shard_map/dot_general | solution.py:37
  19.2 0.7 dynamic-slice_dynamic-update-slice_fusion.7
  19.9 0.7 dynamic-slice_dynamic-update-slice_fusion.6
  20.6 0.7 dynamic-slice_dynamic-update-slice_fusion.5
  21.3 0.7 dynamic-slice_dynamic-update-slice_fusion.4
  22.0 0.7 dynamic-slice_dynamic-update-slice_fusion.3
  22.7 0.7 dynamic-slice_dynamic-update-slice_fusion.2
  23.4 0.0 all-to-all-done
  23.5 0.2 fusion.20
  23.7 0.7 fusion.6
  24.3 6.6 %all-to-all-start.1 = ((f32[8,8,256]{2,1,0:T(8,128)}), f32[8,8,256]{2,1,0:T(8,128)S(1)}, u32[]{:S(2)}, u32[]{:S(2)}) async-start(f32[8,8,256]{2,1,0:T(8,128)} %bitcast.4), calls=%async_computation.1 | async-start | bytes 131072 | tf_op jit(solution)/shard_map/all_to_all | solution.py:94
  31.0 0.7 dynamic-slice_dynamic-update-slice_fusion.1
  31.7 6.5 %all-to-all-done.1 = f32[8,8,256]{2,1,0:T(8,128)S(1)} async-done(((f32[8,8,256]{2,1,0:T(8,128)}), f32[8,8,256]{2,1,0:T(8,128)S(1)}, u32[]{:S(2)}, u32[]{:S(2)}) %all-to-all-start.1) | async-done | bytes 65568 | tf_op jit(solution)/shard_map/all_to_all | solution.py:94
  38.2 0.7 broadcast_in_dim.8
  38.9 10.3 %all-to-all-start.2 = ((f32[32,8,256]{2,1,0:T(8,128)}), f32[32,8,256]{2,1,0:T(8,128)S(1)}, u32[]{:S(2)}, u32[]{:S(2)}) async-start(f32[32,8,256]{2,1,0:T(8,128)} %broadcast_in_dim.8), calls=%async_computation.2 | async-start | bytes 524288 | tf_op jit(solution)/shard_map/all_to_all | solution.py:63
  49.2 0.7 dynamic-slice_dynamic-update-slice_fusion
  50.0 0.9 constant_dynamic-update-slice_fusion.8
  50.8 7.3 %all-to-all-done.2 = f32[32,8,256]{2,1,0:T(8,128)S(1)} async-done(((f32[32,8,256]{2,1,0:T(8,128)}), f32[32,8,256]{2,1,0:T(8,128)S(1)}, u32[]{:S(2)}, u32[]{:S(2)}) %all-to-all-start.2) | async-done | bytes 262176 | tf_op jit(solution)/shard_map/all_to_all | solution.py:63
  58.2 0.6 broadcast_in_dim.9
  58.8 3.4 %all-to-all-start.3 = ((f32[8,8,256]{2,1,0:T(8,128)}), f32[8,8,256]{2,1,0:T(8,128)S(1)}, u32[]{:S(2)}, u32[]{:S(2)}) async-start(f32[8,8,256]{2,1,0:T(8,128)} %broadcast_in_dim.9), calls=%async_computation.3 | async-start | bytes 131072 | tf_op jit(solution)/shard_map/all_to_all | solution.py:63
  62.2 1.4 %collective-permute-start.2 = (bf16[128,2048]{1,0:T(8,128)(2,1)}, bf16[128,2048]{1,0:T(8,128)(2,1)S(1)}, u32[]{:S(2)}, u32[]{:S(2)}) collective-permute-start(bf16[128,2048]{1,0:T(8,128)(2,1)} %collective-permute-done), channel_id=1, source_target_pairs={{0,1},{1,2},{2,3},{3,4},{4,5},{5,6},{6,7},{7,0},{8,9},{9,10},{10,1... | collective-permute-start | bytes 1572872 | tf_op jit(solution)/shard_map/ppermute | solution.py:76
  63.5 0.0 collective-permute-done.1
  63.5 1.4 %collective-permute-start.3 = (bf16[128,2048]{1,0:T(8,128)(2,1)S(1)}, bf16[128,2048]{1,0:T(8,128)(2,1)S(1)}, u32[]{:S(2)}, u32[]{:S(2)}) collective-permute-start(bf16[128,2048]{1,0:T(8,128)(2,1)S(1)} %collective-permute-done.1), channel_id=1, source_target_pairs={{0,7},{1,0},{2,1},{3,2},{4,3},{5,4},{6,5},{7,6},{8,15},{9,8},{10,9... | collective-permute-start | bytes 1572872 | tf_op jit(solution)/shard_map/ppermute | solution.py:77
  65.0 1.9 %constant_dynamic-update-slice_fusion.7 = bf16[1024,2048]{1,0:T(8,128)(2,1)} fusion(bf16[1024,2048]{1,0:T(8,128)(2,1)} %constant_dynamic-update-slice_fusion.8, bf16[128,2048]{1,0:T(8,128)(2,1)} %collective-permute-done), kind=kLoop, calls=%fused_computation.32 | loop fusion | bytes 1048576
  66.9 0.8 constant_dynamic-update-slice_fusion.6
  67.7 1.6 %all-to-all-done.3 = f32[8,8,256]{2,1,0:T(8,128)S(1)} async-done(((f32[8,8,256]{2,1,0:T(8,128)}), f32[8,8,256]{2,1,0:T(8,128)S(1)}, u32[]{:S(2)}, u32[]{:S(2)}) %all-to-all-start.3) | async-done | bytes 65568 | tf_op jit(solution)/shard_map/all_to_all | solution.py:63
  69.2 0.6 copy-done.8
  69.9 3.0 %shard_map.67 = f32[8,2048]{1,0:T(8,128)} custom-call(f32[8,2048]{1,0:T(8,128)} %bitcast.31), custom_call_target="tpu_custom_call" | custom-call | tf_op jit(solution)/shard_map/pallas_call | solution.py:53
  72.9 1.0 constant_dynamic-update-slice_fusion.14
  73.9 1.1 constant_dynamic-update-slice_fusion.11
  75.0 0.9 constant_dynamic-update-slice_fusion.9
  75.9 2.3 %collective-permute-done.2 = bf16[128,2048]{1,0:T(8,128)(2,1)S(1)} collective-permute-done((bf16[128,2048]{1,0:T(8,128)(2,1)}, bf16[128,2048]{1,0:T(8,128)(2,1)S(1)}, u32[]{:S(2)}, u32[]{:S(2)}) %collective-permute-start.2) | collective-permute-done | bytes 524320 | tf_op jit(solution)/shard_map/ppermute | solution.py:76
  78.2 0.0 collective-permute-start.4
  78.2 0.0 collective-permute-done.3
  78.2 2.7 %collective-permute-start.5 = (bf16[128,2048]{1,0:T(8,128)(2,1)S(1)}, bf16[128,2048]{1,0:T(8,128)(2,1)S(1)}, u32[]{:S(2)}, u32[]{:S(2)}) collective-permute-start(bf16[128,2048]{1,0:T(8,128)(2,1)S(1)} %collective-permute-done.3), channel_id=1, source_target_pairs={{0,7},{1,0},{2,1},{3,2},{4,3},{5,4},{6,5},{7,6},{8,15},{9,8},{10,9... | collective-permute-start | bytes 1572872 | tf_op jit(solution)/shard_map/ppermute | solution.py:77
  80.9 2.6 %fusion.1 = f32[24,896]{1,0:T(8,128)S(1)} fusion(bf16[1,2048,896]{2,1,0:T(8,128)(2,1)} %param.6, bf16[8,2048]{1,0:T(8,128)(2,1)S(1)} %get-tuple-element.6, bf16[8,2048]{1,0:T(8,128)(2,1)S(1)} %get-tuple-element.8, bf16[8,2048]{1,0:T(8,128)(2,1)S(1)} %get-tuple-element.10), kind=kOutput, calls=%fused_computation.2 | convolution fusion | flops 88375296 | bytes 3854336 | tf_op jit(solution)/shard_map/dot_general | solution.py:37
  83.5 0.0 copy-done.2
  83.6 8.2 %collective-permute-done.4 = bf16[128,2048]{1,0:T(8,128)(2,1)S(1)} collective-permute-done((bf16[128,2048]{1,0:T(8,128)(2,1)S(1)}, bf16[128,2048]{1,0:T(8,128)(2,1)S(1)}, u32[]{:S(2)}, u32[]{:S(2)}) %collective-permute-start.4) | collective-permute-done | bytes 524320 | tf_op jit(solution)/shard_map/ppermute | solution.py:76
  91.8 0.1 collective-permute-start.6
  92.0 0.0 copy-start.5
  92.0 2.7 %collective-permute-start.7 = (bf16[64,2048]{1,0:T(8,128)(2,1)S(1)}, bf16[64,2048]{1,0:T(8,128)(2,1)S(1)}, u32[]{:S(2)}, u32[]{:S(2)}) collective-permute-start(bf16[64,2048]{1,0:T(8,128)(2,1)S(1)} %slice.113), channel_id=1, source_target_pairs={{0,7},{1,0},{2,1},{3,2},{4,3},{5,4},{6,5},{7,6},{8,15},{9,8},{10,9... | collective-permute-start | bytes 786440 | tf_op jit(solution)/shard_map/ppermute | solution.py:81
  94.8 4.2 %collective-permute-done.6 = bf16[64,2048]{1,0:T(8,128)(2,1)S(1)} collective-permute-done((bf16[64,2048]{1,0:T(8,128)(2,1)S(1)}, bf16[64,2048]{1,0:T(8,128)(2,1)S(1)}, u32[]{:S(2)}, u32[]{:S(2)}) %collective-permute-start.6) | collective-permute-done | bytes 262176 | tf_op jit(solution)/shard_map/ppermute | solution.py:80
  99.0 0.0 collective-permute-done.7
  99.0 1.9 %copy-done.3 = bf16[1024,2048]{1,0:T(8,128)(2,1)} copy-done((bf16[1024,2048]{1,0:T(8,128)(2,1)}, bf16[1024,2048]{1,0:T(8,128)(2,1)S(1)}, u32[]{:S(2)}) %copy-start.3) | copy-done | bytes 4194328
  100.9 1.2 fusion.13
  102.2 0.3 fusion.7
  102.6 3.0 %collective-permute-start.8 = (f32[8,512]{1,0:T(8,128)S(1)}, f32[8,512]{1,0:T(8,128)S(1)}, u32[]{:S(2)}, u32[]{:S(2)}) collective-permute-start(f32[8,512]{1,0:T(8,128)S(1)} %dynamic-slice_bitcast_fusion), channel_id=1, source_target_pairs={{0,8},{8,0},{16,24},{24,16},{32,40},{40,32},{48,56},{56,48},{64,72... | collective-permute-start | bytes 49160 | tf_op jit(solution)/shard_map/ppermute | solution.py:106
  105.6 0.8 collective-permute-done.8
  106.5 11.7 %all_to_all.25 = f32[16,8,512]{2,1,0:T(8,128)S(1)} all-to-all(f32[16,8,512]{2,1,0:T(8,128)S(1)} %broadcast_in_dim.10), channel_id=1, replica_groups={{0,16,32,48,64,80,96,112,128,144,160,176,192,208,224,240},{8,24,40,56,7..., dimensions={0} | all-to-all | bytes 524288 | tf_op jit(solution)/shard_map/all_to_all | solution.py:63
  118.2 1.6 %collective-permute-start.9 = (f32[8,512]{1,0:T(8,128)S(1)}, f32[8,512]{1,0:T(8,128)S(1)}, u32[]{:S(2)}, u32[]{:S(2)}) collective-permute-start(f32[8,512]{1,0:T(8,128)S(1)} %broadcast_multiply_fusion), channel_id=1, source_target_pairs={{0,8},{8,0},{16,24},{24,16},{32,40},{40,32},{48,56},{56,48},{64,72... | collective-permute-start | bytes 49160 | tf_op jit(solution)/shard_map/ppermute | solution.py:108
  119.8 0.8 collective-permute-done.9
  120.6 0.0 copy-start.7
  120.7 0.0 copy-start
  120.8 1.2 fusion.34
  121.9 0.8 copy-done
  122.8 1.3 copy-done.4
  124.0 6.1 %fusion = bf16[1,2048,896]{2,1,0:T(8,128)(2,1)} fusion(f32[2048,896]{1,0:T(8,128)S(1)} %fusion.34, bf16[1,2048,896]{2,1,0:T(8,128)(2,1)S(1)} %copy-done, bf16[1024,2048]{1,0:T(8,128)(2,1)S(1)} %copy-done.4, bf16[1024,896]{1,0:T(8,128)(2,1)S(1)} %copy-done.5), kind=kOutput, calls=%fused_computation.1 | convolution fusion | flops 3765436416 | bytes 20709376 | tf_op jit(solution)/shard_map/dot_general | solution.py:37
  (42 shorter events, 0.5 us)
Async XLA Ops:
  0.6 18.5 %copy-start.1 = (bf16[1024,896]{1,0:T(8,128)(2,1)S(1)}, bf16[1024,896]{1,0:T(8,128)(2,1)}, u32[]{:S(2)}) copy-start(bf16[1024,896]{1,0:T(8,128)(2,1)} %param.5) | copy-start | bytes 5505028
  0.6 61.5 %collective-permute-start = (bf16[128,2048]{1,0:T(8,128)(2,1)}, bf16[128,2048]{1,0:T(8,128)(2,1)}, u32[]{:S(2)}, u32[]{:S(2)}) collective-permute-start(bf16[128,2048]{1,0:T(8,128)(2,1)} %param.4), channel_id=1, source_target_pairs={{0,1},{1,2},{2,3},{3,4},{4,5},{5,6},{6,7},{7,0},{8,9},{9,10},{10,1... | collective-permute-start | bytes 1572872 | tf_op jit(solution)/shard_map/ppermute | solution.py:76
  3.2 60.4 %collective-permute-start.1 = (bf16[128,2048]{1,0:T(8,128)(2,1)}, bf16[128,2048]{1,0:T(8,128)(2,1)S(1)}, u32[]{:S(2)}, u32[]{:S(2)}) collective-permute-start(bf16[128,2048]{1,0:T(8,128)(2,1)} %param.4), channel_id=1, source_target_pairs={{0,7},{1,0},{2,1},{3,2},{4,3},{5,4},{6,5},{7,6},{8,15},{9,8},{10,9... | collective-permute-start | bytes 1572872 | tf_op jit(solution)/shard_map/ppermute | solution.py:77
  10.1 13.3 %copy-start.6 = (bf16[128,2048]{1,0:T(8,128)(2,1)S(1)}, bf16[128,2048]{1,0:T(8,128)(2,1)}, u32[]{:S(2)}) copy-start(bf16[128,2048]{1,0:T(8,128)(2,1)} %param.4) | copy-start | bytes 1572868
  10.8 12.7 %all-to-all-start = ((f32[8,8,128]{2,1,0:T(8,128)}), f32[8,8,128]{2,1,0:T(8,128)S(1)}, u32[]{:S(2)}, u32[]{:S(2)}) async-start(f32[8,8,128]{2,1,0:T(8,128)} %fusion.15), calls=%async_computation | async-start | bytes 65536 | tf_op jit(solution)/shard_map/all_to_all | solution.py:90
  24.3 13.9 %all-to-all-start.1 = ((f32[8,8,256]{2,1,0:T(8,128)}), f32[8,8,256]{2,1,0:T(8,128)S(1)}, u32[]{:S(2)}, u32[]{:S(2)}) async-start(f32[8,8,256]{2,1,0:T(8,128)} %bitcast.4), calls=%async_computation.1 | async-start | bytes 131072 | tf_op jit(solution)/shard_map/all_to_all | solution.py:94
  38.9 19.2 %all-to-all-start.2 = ((f32[32,8,256]{2,1,0:T(8,128)}), f32[32,8,256]{2,1,0:T(8,128)S(1)}, u32[]{:S(2)}, u32[]{:S(2)}) async-start(f32[32,8,256]{2,1,0:T(8,128)} %broadcast_in_dim.8), calls=%async_computation.2 | async-start | bytes 524288 | tf_op jit(solution)/shard_map/all_to_all | solution.py:63
  58.8 10.4 %all-to-all-start.3 = ((f32[8,8,256]{2,1,0:T(8,128)}), f32[8,8,256]{2,1,0:T(8,128)S(1)}, u32[]{:S(2)}, u32[]{:S(2)}) async-start(f32[8,8,256]{2,1,0:T(8,128)} %broadcast_in_dim.9), calls=%async_computation.3 | async-start | bytes 131072 | tf_op jit(solution)/shard_map/all_to_all | solution.py:63
  62.2 16.0 %collective-permute-start.2 = (bf16[128,2048]{1,0:T(8,128)(2,1)}, bf16[128,2048]{1,0:T(8,128)(2,1)S(1)}, u32[]{:S(2)}, u32[]{:S(2)}) collective-permute-start(bf16[128,2048]{1,0:T(8,128)(2,1)} %collective-permute-done), channel_id=1, source_target_pairs={{0,1},{1,2},{2,3},{3,4},{4,5},{5,6},{6,7},{7,0},{8,9},{9,10},{10,1... | collective-permute-start | bytes 1572872 | tf_op jit(solution)/shard_map/ppermute | solution.py:76
  63.5 14.7 %collective-permute-start.3 = (bf16[128,2048]{1,0:T(8,128)(2,1)S(1)}, bf16[128,2048]{1,0:T(8,128)(2,1)S(1)}, u32[]{:S(2)}, u32[]{:S(2)}) collective-permute-start(bf16[128,2048]{1,0:T(8,128)(2,1)S(1)} %collective-permute-done.1), channel_id=1, source_target_pairs={{0,7},{1,0},{2,1},{3,2},{4,3},{5,4},{6,5},{7,6},{8,15},{9,8},{10,9... | collective-permute-start | bytes 1572872 | tf_op jit(solution)/shard_map/ppermute | solution.py:77
  69.2 0.6 copy-start.8
  72.9 10.7 %copy-start.2 = (bf16[1024,2048]{1,0:T(8,128)(2,1)S(1)}, bf16[1024,2048]{1,0:T(8,128)(2,1)}, u32[]{:S(2)}) copy-start(bf16[1024,2048]{1,0:T(8,128)(2,1)} %constant_dynamic-update-slice_fusion.6) | copy-start | bytes 12582916
  78.2 13.6 %collective-permute-start.4 = (bf16[128,2048]{1,0:T(8,128)(2,1)S(1)}, bf16[128,2048]{1,0:T(8,128)(2,1)S(1)}, u32[]{:S(2)}, u32[]{:S(2)}) collective-permute-start(bf16[128,2048]{1,0:T(8,128)(2,1)S(1)} %collective-permute-done.2), channel_id=1, source_target_pairs={{0,1},{1,2},{2,3},{3,4},{4,5},{5,6},{6,7},{7,0},{8,9},{9,10},{10,1... | collective-permute-start | bytes 1572872 | tf_op jit(solution)/shard_map/ppermute | solution.py:76
  78.2 13.7 %collective-permute-start.5 = (bf16[128,2048]{1,0:T(8,128)(2,1)S(1)}, bf16[128,2048]{1,0:T(8,128)(2,1)S(1)}, u32[]{:S(2)}, u32[]{:S(2)}) collective-permute-start(bf16[128,2048]{1,0:T(8,128)(2,1)S(1)} %collective-permute-done.3), channel_id=1, source_target_pairs={{0,7},{1,0},{2,1},{3,2},{4,3},{5,4},{6,5},{7,6},{8,15},{9,8},{10,9... | collective-permute-start | bytes 1572872 | tf_op jit(solution)/shard_map/ppermute | solution.py:77
  91.8 7.1 %collective-permute-start.6 = (bf16[64,2048]{1,0:T(8,128)(2,1)S(1)}, bf16[64,2048]{1,0:T(8,128)(2,1)S(1)}, u32[]{:S(2)}, u32[]{:S(2)}) collective-permute-start(bf16[64,2048]{1,0:T(8,128)(2,1)S(1)} %slice.112), channel_id=1, source_target_pairs={{0,1},{1,2},{2,3},{3,4},{4,5},{5,6},{6,7},{7,0},{8,9},{9,10},{10,1... | collective-permute-start | bytes 786440 | tf_op jit(solution)/shard_map/ppermute | solution.py:80
  92.0 10.2 %copy-start.5 = (bf16[1024,896]{1,0:T(8,128)(2,1)S(1)}, bf16[1024,896]{1,0:T(8,128)(2,1)}, u32[]{:S(2)}) copy-start(bf16[1024,896]{1,0:T(8,128)(2,1)} %dynamic-slice_dynamic-update-slice_fusion) | copy-start | bytes 5505028
  92.0 7.0 %collective-permute-start.7 = (bf16[64,2048]{1,0:T(8,128)(2,1)S(1)}, bf16[64,2048]{1,0:T(8,128)(2,1)S(1)}, u32[]{:S(2)}, u32[]{:S(2)}) collective-permute-start(bf16[64,2048]{1,0:T(8,128)(2,1)S(1)} %slice.113), channel_id=1, source_target_pairs={{0,7},{1,0},{2,1},{3,2},{4,3},{5,4},{6,5},{7,6},{8,15},{9,8},{10,9... | collective-permute-start | bytes 786440 | tf_op jit(solution)/shard_map/ppermute | solution.py:81
  99.0 1.9 %copy-start.3 = (bf16[1024,2048]{1,0:T(8,128)(2,1)}, bf16[1024,2048]{1,0:T(8,128)(2,1)S(1)}, u32[]{:S(2)}) copy-start(bf16[1024,2048]{1,0:T(8,128)(2,1)S(1)} %constant_dynamic-update-slice_fusion) | copy-start | bytes 12582916
  102.6 3.8 %collective-permute-start.8 = (f32[8,512]{1,0:T(8,128)S(1)}, f32[8,512]{1,0:T(8,128)S(1)}, u32[]{:S(2)}, u32[]{:S(2)}) collective-permute-start(f32[8,512]{1,0:T(8,128)S(1)} %dynamic-slice_bitcast_fusion), channel_id=1, source_target_pairs={{0,8},{8,0},{16,24},{24,16},{32,40},{40,32},{48,56},{56,48},{64,72... | collective-permute-start | bytes 49160 | tf_op jit(solution)/shard_map/ppermute | solution.py:106
  118.2 2.4 %collective-permute-start.9 = (f32[8,512]{1,0:T(8,128)S(1)}, f32[8,512]{1,0:T(8,128)S(1)}, u32[]{:S(2)}, u32[]{:S(2)}) collective-permute-start(f32[8,512]{1,0:T(8,128)S(1)} %broadcast_multiply_fusion), channel_id=1, source_target_pairs={{0,8},{8,0},{16,24},{24,16},{32,40},{40,32},{48,56},{56,48},{64,72... | collective-permute-start | bytes 49160 | tf_op jit(solution)/shard_map/ppermute | solution.py:108
  120.6 1.3 copy-start.7
  120.7 2.0 %copy-start = (bf16[1,2048,896]{2,1,0:T(8,128)(2,1)S(1)}, bf16[1,2048,896]{2,1,0:T(8,128)(2,1)}, u32[]{:S(2)}) copy-start(bf16[1,2048,896]{2,1,0:T(8,128)(2,1)} %param.6) | copy-start | bytes 11010052
  120.7 3.3 %copy-start.4 = (bf16[1024,2048]{1,0:T(8,128)(2,1)S(1)}, bf16[1024,2048]{1,0:T(8,128)(2,1)}, u32[]{:S(2)}) copy-start(bf16[1024,2048]{1,0:T(8,128)(2,1)} %copy-done.3) | copy-start | bytes 12582916

commit v2 on v0

v2 whole, which is shorter than its diff:
```python
import jax
import jax.numpy as jnp
from jax import lax
from jax.experimental import pallas as pl
from jax.experimental.pallas import tpu as pltpu
from jax.sharding import PartitionSpec as P

MP = 8
DP = 32
R = 8
HALF = 512
TOKENS = 1024
F32 = jnp.float32
BF16 = jnp.bfloat16
VMEM = pltpu.MemorySpace.VMEM


def shift(size, step):
    return [(i, (i + step) % size) for i in range(size)]


CORES = [(i, i ^ 1) for i in range(DP)]
CHIPS = [[2 * i for i in range(DP // 2)], [2 * i + 1 for i in range(DP // 2)]]


def after(x, *others):
    return lax.optimization_barrier((x,) + others)[0]


def terms(x):
    first = x.astype(BF16).astype(F32)
    rest = x - first
    second = rest.astype(BF16).astype(F32)
    return first, second, rest - second


def split3(x):
    return jnp.concatenate(terms(x), axis=0).astype(BF16)


def fold3(x):
    rows = x.shape[0] // 3
    return (x[2 * rows :] + x[rows : 2 * rows]) + x[:rows]


def dot(a, b, left, right):
    return lax.dot_general(a, b, (((left,), (right,)), ((), ())), preferred_element_type=F32)


def local(kernel, out, *args, spaces=None, mib=8, scratch=(), **kw):
    spaces = spaces or [VMEM] * len(args)
    return pl.pallas_call(
        kernel,
        out_shape=out,
        in_specs=[pl.BlockSpec(memory_space=s) for s in spaces],
        out_specs=jax.tree.map(lambda _: pl.BlockSpec(memory_space=VMEM), out),
        scratch_shapes=scratch,
        compiler_params=pltpu.CompilerParams(vmem_limit_bytes=mib << 20),
        **kw,
    )(*args)


def shape(*dims, dtype=F32):
    return jax.ShapeDtypeStruct(dims, dtype)


def pieces(size, count):
    step = size // count
    return [slice(i * step, (i + 1) * step) for i in range(count)]


def far(x):
    return pltpu.with_memory_space_constraint(x, pltpu.MemorySpace.HBM)


def reduce_kernel(q_ref, g_ref, out_ref, q_held, held, sems):
    first = pltpu.make_async_copy(q_ref, q_held, sems.at[0])
    first.start()
    copies = [pltpu.make_async_copy(g_ref.at[at], held.at[at], sems.at[1 + i]) for i, at in enumerate(pieces(TOKENS, 4))]
    for copy in copies:
        copy.start()
    first.wait()
    q = split3(q_held[...])
    for i, (copy, at) in enumerate(zip(copies, pieces(TOKENS, 4))):
        copy.wait()
        value = fold3(dot(q, held[at], 1, 1))
        out_ref[2 * i] = value[:, :128]
        out_ref[2 * i + 1] = value[:, 128:]


def error_left_kernel(q_ref, err_ref, out_ref, q_held, held, sems):
    depth = err_ref.shape[0]
    first = pltpu.make_async_copy(q_ref, q_held, sems.at[0])
    first.start()
    copies = [pltpu.make_async_copy(err_ref.at[at], held.at[at], sems.at[1 + i]) for i, at in enumerate(pieces(depth, 4))]
    for copy in copies:
        copy.start()
    first.wait()
    q = split3(q_held[...])
    for copy, at in zip(copies, pieces(depth, 4)):
        copy.wait()
        out_ref[:, at] = fold3(dot(q, held[at], 1, 1))


def left_kernel(parts_ref, x_ref, more_ref, out_ref):
    reduced = jnp.sum(parts_ref[...], axis=0)
    value = fold3(dot(split3(reduced), x_ref[...], 1, 0)) + more_ref[...]
    for z in range(MP):
        out_ref[z] = value[:, z * 256 : (z + 1) * 256]


def sum_spread_kernel(parts_ref, out_ref):
    value = jnp.sum(parts_ref[...], axis=0)
    out_ref[...] = jnp.broadcast_to(value[None], out_ref.shape)


def gram_schmidt_kernel(parts_ref, out_ref):
    rows = jnp.concatenate([parts_ref[z] for z in range(MP)], axis=1)
    index = lax.broadcasted_iota(jnp.int32, (R, 1), 0)
    for i in range(R):
        vector = rows[i : i + 1]
        products = jnp.sum(rows * vector, axis=1, keepdims=True)
        scale = 1.0 / jnp.sqrt(products[i : i + 1] + 1e-06)
        vector = vector * scale
        rows = jnp.where(index > i, rows - (products * scale) * vector, jnp.where(index == i, vector, rows))
    out_ref[...] = rows


def right_kernel(p_ref, err_ref, g_ref, *refs):
    blocks, (keep_ref, send_ref, rows_ref, grads_ref, held, sems) = refs[:9], refs[9:]
    me = lax.axis_index("mp")
    starts = [me * 128]
    for step in range(1, 4):
        starts += [lax.rem(me + MP - step, MP) * 128, lax.rem(me + step, MP) * 128]
    last = lax.rem(me + 4, MP) * 128
    starts += [last, last + 64]
    copies = [pltpu.make_async_copy(g_ref, grads_ref.at[pl.ds(0, TOKENS)], sems.at[9])]
    for i, (block, start) in enumerate(zip(blocks, starts)):
        size = block.shape[0]
        copies.append(pltpu.make_async_copy(block, rows_ref.at[pl.ds(pl.multiple_of(start, size), size)], sems.at[i]))
    copies.append(pltpu.make_async_copy(err_ref, held, sems.at[10]))
    for copy in copies[1:] + copies[:1]:
        copy.start()
    a, b, c = terms(p_ref[...])
    left = jnp.concatenate([a, b, c], axis=0).astype(BF16)
    rows_ref[TOKENS:] = jnp.concatenate([a, a, a, b, b, c, jnp.zeros((2 * R, a.shape[1]), F32)], axis=0).astype(BF16)
    grads_ref[TOKENS:] = jnp.zeros((8 * R, grads_ref.shape[1]), BF16)
    for copy in copies[1:10]:
        copy.wait()
    projected = fold3(dot(left, rows_ref[:TOKENS], 1, 1))
    copies[0].wait()
    value = fold3(dot(split3(projected), grads_ref[:TOKENS], 1, 0))
    copies[10].wait()
    value = value + fold3(dot(left, held[...], 1, 0))
    first = value[:, :HALF]
    second = jnp.concatenate([value[:, HALF:], jnp.zeros((R, 2 * HALF - value.shape[1]), F32)], axis=1)
    core = lax.rem(lax.axis_index("dp"), 2)
    keep_ref[...] = jnp.where(core == 0, first, second)
    send_ref[...] = jnp.where(core == 0, second, first)


def add_spread_kernel(a_ref, b_ref, out_ref):
    out_ref[...] = jnp.broadcast_to((a_ref[...] + b_ref[...])[None], out_ref.shape)


def mean_kernel(parts_ref, out_ref):
    out_ref[...] = jnp.sum(parts_ref[...], axis=0) / DP


def right_factor_kernel(mine_ref, other_ref, grads_ref, q_ref, out_ref):
    core = lax.rem(lax.axis_index("dp"), 2)
    mine, other = mine_ref[...], other_ref[...]
    first = jnp.where(core == 0, mine, other)
    second = jnp.where(core == 0, other, mine)
    q = jnp.concatenate([first, second[:, : q_ref.shape[1] - HALF]], axis=1)
    q_ref[...] = q
    a, b, c = terms(-q)
    out_ref[TOKENS:] = jnp.concatenate([a, b, c, a, b, a, jnp.zeros((2 * R, a.shape[1]), F32)], axis=0).astype(BF16)


def exchange(x, axis, groups=None):
    return lax.all_to_all(x, axis, 0, 0, axis_index_groups=groups)


def on_device(tokens, out_grad, error, q_prev):
    err = error[0]
    depth, columns = err.shape
    half = tokens.shape[0] // 2

    def pass_on(right, left):
        return lax.ppermute(right, "mp", shift(MP, 1)), lax.ppermute(left, "mp", shift(MP, -1))

    right1, left1 = pass_on(tokens, tokens)
    hbm = pltpu.MemorySpace.HBM
    dma = pltpu.SemaphoreType.DMA
    held = pltpu.VMEM((R, columns), F32)
    reduced = local(
        reduce_kernel, shape(MP, R, 128), far(q_prev), far(out_grad), spaces=[hbm, hbm], scratch=[held, pltpu.VMEM(out_grad.shape, BF16), dma((5,))]
    )
    more = local(
        error_left_kernel, shape(R, depth), far(q_prev), far(err), spaces=[hbm, hbm], scratch=[held, pltpu.VMEM(err.shape, BF16), dma((5,))]
    )
    reduced = exchange(reduced, "mp")
    part = local(left_kernel, shape(MP, R, 256), reduced, tokens, more)
    right2, left2 = pass_on(after(right1, part), after(left1, part))
    part = exchange(after(part, right1, left1), "mp")
    part = local(sum_spread_kernel, shape(DP, R, 256), part)
    right3, left3 = pass_on(after(right2, part), after(left2, part))
    part = exchange(after(part, right2, left2), "dp")
    part = local(sum_spread_kernel, shape(MP, R, 256), part)
    right4, left4 = pass_on(after(right3, part)[:half], after(left3, part)[half:])
    part = exchange(after(part, right3, left3), "mp")
    p_factor = local(gram_schmidt_kernel, pltpu.VMEM((R, depth), F32), part)
    blocks = (tokens, right1, left1, right2, left2, right3, left3, right4, left4)

    keep, send, rows, grads = local(
        right_kernel,
        (
            shape(R, HALF),
            shape(R, HALF),
            pltpu.VMEM((TOKENS + 8 * R, depth), BF16),
            pltpu.VMEM((TOKENS + 8 * R, columns), BF16),
        ),
        pltpu.with_memory_space_constraint(p_factor, VMEM),
        far(err),
        far(out_grad),
        *blocks,
        spaces=[VMEM, hbm, hbm] + [pl.ANY] * 9,
        scratch=[pltpu.VMEM(err.shape, BF16), dma((11,))],
    )
    wide = local(add_spread_kernel, shape(DP // 2, R, HALF), keep, lax.ppermute(send, "dp", CORES))
    mine = local(mean_kernel, shape(R, HALF), exchange(wide, "dp", CHIPS))
    other = lax.ppermute(mine, "dp", CORES)
    q_factor, grads = local(
        right_factor_kernel,
        (shape(R, columns), pltpu.VMEM(grads.shape, BF16)),
        mine,
        other,
        pltpu.with_memory_space_constraint(grads, VMEM),
        input_output_aliases={2: 1},
    )
    new_error = (dot(rows, grads, 0, 0) + err.astype(F32)).astype(BF16)
    return (p_factor, q_factor, new_error[None])


def solution(mesh):
    placed = (P(("dp", "mp"), None), P("dp", "mp"), P("dp", None, "mp"), P(None, "mp"))
    return jax.shard_map(
        on_device,
        mesh=mesh,
        in_specs=placed,
        out_specs=(P(), P(None, "mp"), P("dp", None, "mp")),
        check_vma=False,
    )
```

time: 479 us -> 101 us (0.21); the launches traced: 474 us -> 101 us
  waiting for transfers between devices: 239 us -> 5.39 us
  blocking collectives: 120 us -> 55 us
  other arithmetic: 61.9 us -> 0 us
  matrix products: 30.1 us -> 7 us
  starting transfers between devices: 0.3 us -> 20.1 us
  between operations: 19.4 us -> 0.77 us
  Pallas kernels: 0 us -> 12.1 us
    psum x2 -> x0, waiting for transfers between devices: 178 us -> none  [the longest x1 113 us: on_device(): summed = lax.psum(summed, 'dp')]
    psum x1 -> x0, blocking collectives: 120 us -> none  [on_device(): q_factor = lax.psum(q_local, 'dp') / lax.axis_size('dp')]
    all_gather x1 -> x0, waiting for transfers between devices: 60.5 us -> none  [on_device(): lax.all_gather(tokens, 'mp', axis=0, tiled=True)]
    all_to_all x0 -> x4, blocking collectives: none -> 55 us  [exchange(): return lax.all_to_all(x, axis, 0, 0, axis_index_groups=groups)]
    reduce_sum x15 -> x0, other arithmetic: 41.5 us -> none  [the longest x10 31.5 us: orthonormal(): vector = vector - jnp.sum(vector * earlier) * earlier]
    dot_general x4 -> x1, matrix products: 30.1 us -> 7 us  [dot(): lax.dot_general(a, b, (((left,), (right,)), ((), ())), preferred_element_...]
    div x2 -> x0, other arithmetic: 19 us -> none  [the longest x1 19 us: orthonormal(): vector = vector / jnp.sqrt(jnp.sum(vector * vector) + 1e-06)]
    ppermute x0 -> x10, starting transfers between devices: none -> 16 us  [the longest x4 9.89 us: pass_on(): lax.ppermute(left, 'mp', shift(MP, -1))]
  transfers between devices with their start and end apart: 3 -> 11, of which waited for: 3 -> 3; matrix products, arithmetic and copies ran while one was open for 0% -> 1% of each run, Pallas kernels for 0% -> 7%
where the time goes in v2:
time: 101 us
  blocking collectives  55 us (54%)
  starting transfers between devices  20.1 us (20%)
  Pallas kernels  12.1 us (12%)
  matrix products  7 us (7%)
  waiting for transfers between devices  5.39 us (5%)
    all_to_all x4, blocking collectives, exchange(): return lax.all_to_all(x, axis, 0, 0, axis_index_groups=groups)  55 us
    pallas_call x10, Pallas kernels, local(): pl.pallas_call(kernel, out_shape=out, in_specs=[pl.BlockSpec(memory_space...  12.1 us
    ppermute x4, starting transfers between devices, pass_on(): lax.ppermute(left, 'mp', shift(MP, -1))  9.89 us
    dot_general x1, matrix products, dot(): lax.dot_general(a, b, (((left,), (right,)), ((), ())), preferred_element_...  7 us
    all_to_all x1, waiting for transfers between devices, exchange(): return lax.all_to_all(x, axis, 0, 0, axis_index_groups=groups)  4.32 us
    all_to_all x1, starting transfers between devices, exchange(): return lax.all_to_all(x, axis, 0, 0, axis_index_groups=groups)  4.09 us
    ppermute x1, starting transfers between devices, on_device(): lax.ppermute(send, 'dp', CORES)  2.3 us
    ppermute x4, starting transfers between devices, pass_on(): lax.ppermute(right, 'mp', shift(MP, 1))  2.1 us
  transfers between devices with their start and end apart: 11, of which 3 were waited for; matrix products, arithmetic and copies ran while one was open for 1% of the time, Pallas kernels for 7%

profile of v2, /device:TPU:1, one launch (start us, length us, event | category | flops | bytes accessed | tf_op | source)
XLA Modules:
  0.0 101.1 jit_solution(13266499498903544435)
XLA Ops:
  0.6 0.0 copy-start
  0.6 6.5 %collective-permute-start.1 = (bf16[128,2048]{1,0:T(8,128)(2,1)}, bf16[128,2048]{1,0:T(8,128)(2,1)S(1)}, u32[]{:S(2)}, u32[]{:S(2)}) collective-permute-start(bf16[128,2048]{1,0:T(8,128)(2,1)} %refs_0_.1), channel_id=1, source_target_pairs={{0,7},{1,0},{2,1},{3,2},{4,3},{5,4},{6,5},{7,6},{8,15},{9,8},{10,9... | collective-permute-start | bytes 1572872 | tf_op jit(solution)/shard_map/ppermute | solution.py:191
  7.1 0.0 collective-permute-start
  7.1 3.1 %shard_map.67 = f32[8,8,128]{2,1,0:T(8,128)} custom-call(f32[8,896]{1,0:T(8,128)} %q_ref.3, bf16[1024,896]{1,0:T(8,128)(2,1)} %g_ref.3), custom_call_target="tpu_custom_call" | custom-call | tf_op jit(solution)/shard_map/pallas_call | solution.py:52
  10.3 4.1 %all-to-all-start = ((f32[8,8,128]{2,1,0:T(8,128)}), f32[8,8,128]{2,1,0:T(8,128)S(1)}, u32[]{:S(2)}, u32[]{:S(2)}) async-start(f32[8,8,128]{2,1,0:T(8,128)} %shard_map.67), calls=%async_computation | async-start | bytes 65536 | tf_op jit(solution)/shard_map/all_to_all | solution.py:182
  14.3 2.8 %shard_map.68.more_ref = f32[8,2048]{1,0:T(8,128)S(1)} custom-call(f32[8,896]{1,0:T(8,128)} %q_ref.3, bf16[2048,896]{1,0:T(8,128)(2,1)} %bitcast.6), custom_call_target="tpu_custom_call" | custom-call | tf_op jit(solution)/shard_map/pallas_call | solution.py:52
  17.1 4.3 %all-to-all-done.parts_ref = f32[8,8,128]{2,1,0:T(8,128)S(1)} async-done(((f32[8,8,128]{2,1,0:T(8,128)}), f32[8,8,128]{2,1,0:T(8,128)S(1)}, u32[]{:S(2)}, u32[]{:S(2)}) %all-to-all-start) | async-done | bytes 32800 | tf_op jit(solution)/shard_map/all_to_all | solution.py:182
  21.5 0.0 copy-done
  21.5 0.2 shard_map.69
  21.7 0.0 collective-permute-done.1.refs_2_
  21.7 0.3 collective-permute-start.3
  21.9 0.0 collective-permute-done.refs_1_
  21.9 1.3 %collective-permute-start.2 = (bf16[128,2048]{1,0:T(8,128)(2,1)S(1)}, bf16[128,2048]{1,0:T(8,128)(2,1)S(1)}, u32[]{:S(2)}, u32[]{:S(2)}) collective-permute-start(bf16[128,2048]{1,0:T(8,128)(2,1)S(1)} %collective-permute-done.refs_1_), channel_id=1, source_target_pairs={{0,1},{1,2},{2,3},{3,4},{4,5},{5,6},{6,7},{7,0},{8,9},{9,10},{10,1... | collective-permute-start | bytes 1572872 | tf_op jit(solution)/shard_map/ppermute | solution.py:191
  23.2 12.9 %all_to_all.25.parts_ref = f32[8,8,256]{2,1,0:T(8,128)S(1)} all-to-all(f32[8,8,256]{2,1,0:T(8,128)S(1)} %shard_map.69), channel_id=1, replica_groups=mesh['dp'=32,'mp'=8] {'mp'}, dimensions={0} | all-to-all | bytes 131072 | tf_op jit(solution)/shard_map/all_to_all | solution.py:182
  36.1 0.0 collective-permute-done.3.refs_4_
  36.1 0.8 collective-permute-start.5
  37.0 0.0 collective-permute-done.2.refs_3_
  37.0 0.7 collective-permute-start.4
  37.7 20.1 %all_to_all.26.parts_ref = f32[32,8,256]{2,1,0:T(8,128)S(1)} all-to-all(f32[32,8,256]{2,1,0:T(8,128)S(1)} %shard_map.70), channel_id=1, replica_groups=mesh['dp'=32,'mp'=8] {'dp'}, dimensions={0} | all-to-all | bytes 524288 | tf_op jit(solution)/shard_map/all_to_all | solution.py:182
  57.8 0.0 collective-permute-done.5.refs_6_
  57.8 2.3 %collective-permute-start.7 = (bf16[64,2048]{1,0:T(8,128)(2,1)S(1)}, bf16[64,2048]{1,0:T(8,128)(2,1)S(1)}, u32[]{:S(2)}, u32[]{:S(2)}) collective-permute-start(bf16[64,2048]{1,0:T(8,128)(2,1)S(1)} %slice.7), channel_id=1, source_target_pairs={{0,7},{1,0},{2,1},{3,2},{4,3},{5,4},{6,5},{7,6},{8,15},{9,8},{10,9... | collective-permute-start | bytes 786440 | tf_op jit(solution)/shard_map/ppermute | solution.py:191
  60.1 0.0 collective-permute-done.4.refs_5_
  60.2 0.1 collective-permute-start.6
  60.3 10.9 %all_to_all.27.parts_ref = f32[8,8,256]{2,1,0:T(8,128)S(1)} all-to-all(f32[8,8,256]{2,1,0:T(8,128)S(1)} %shard_map.71), channel_id=1, replica_groups=mesh['dp'=32,'mp'=8] {'mp'}, dimensions={0} | all-to-all | bytes 131072 | tf_op jit(solution)/shard_map/all_to_all | solution.py:182
  71.1 0.9 shard_map.72.p_ref
  72.1 0.0 copy-start.1
  72.1 0.0 collective-permute-done.7.refs_8_
  72.1 0.0 collective-permute-done.6.refs_7_
  72.1 4.4 %shard_map.73 = (f32[8,512]{1,0:T(8,128)S(1)}, f32[8,512]{1,0:T(8,128)S(1)}, bf16[1088,2048]{1,0:T(8,128)(2,1)S(1)}, bf16[1088,896]{1,0:T(8,128)(2,1)S(1)}) custom-call(f32[8,2048]{1,0:T(8,128)S(1)} %shard_map.72.p_ref, bf16[2048,896]{1,0:T(8,128)(2,1)} %bitcast.7, bf16[1024,896]{1,0:T(8,128)(2,1)} %g_ref.3, bf16[128,2048]{1,0:T(8,128)(2,1)S(1)} %copy-done, ...), custom_call_target="tpu_custom_call" | custom-call | tf_op jit(solution)/shard_map/pallas_call | solution.py:52
  76.5 2.3 %collective-permute-start.8 = (f32[8,512]{1,0:T(8,128)S(1)}, f32[8,512]{1,0:T(8,128)S(1)}, u32[]{:S(2)}, u32[]{:S(2)}) collective-permute-start(f32[8,512]{1,0:T(8,128)S(1)} %get-tuple-element.28), channel_id=1, source_target_pairs={{0,8},{8,0},{16,24},{24,16},{32,40},{40,32},{48,56},{56,48},{64,72... | collective-permute-start | bytes 49160 | tf_op jit(solution)/shard_map/ppermute | solution.py:231
  78.8 0.8 collective-permute-done.8.b_ref
  79.7 11.2 %all_to_all.28.parts_ref = f32[16,8,512]{2,1,0:T(8,128)S(1)} all-to-all(f32[16,8,512]{2,1,0:T(8,128)S(1)} %shard_map.74), channel_id=1, replica_groups={{0,16,32,48,64,80,96,112,128,144,160,176,192,208,224,240},{8,24,40,56,7..., dimensions={0} | all-to-all | bytes 524288 | tf_op jit(solution)/shard_map/all_to_all | solution.py:182
  90.9 1.8 %collective-permute-start.9 = (f32[8,512]{1,0:T(8,128)S(1)}, f32[8,512]{1,0:T(8,128)S(1)}, u32[]{:S(2)}, u32[]{:S(2)}) collective-permute-start(f32[8,512]{1,0:T(8,128)S(1)} %shard_map.75.mine_ref), channel_id=1, source_target_pairs={{0,8},{8,0},{16,24},{24,16},{32,40},{40,32},{48,56},{56,48},{64,72... | collective-permute-start | bytes 49160 | tf_op jit(solution)/shard_map/ppermute | solution.py:233
  92.7 0.6 copy.9
  93.3 0.2 collective-permute-done.9.other_ref
  93.5 0.6 shard_map.76
  94.1 0.0 copy-done.1
  94.1 7.0 %fusion = bf16[1,2048,896]{2,1,0:T(8,128)(2,1)} fusion(bf16[1088,2048]{1,0:T(8,128)(2,1)S(1)} %get-tuple-element.31, bf16[1088,896]{1,0:T(8,128)(2,1)S(1)} %get-tuple-element.32, bf16[1,2048,896]{2,1,0:T(8,128)(2,1)S(1)} %copy-done.1), kind=kOutput, calls=%fused_computation.1 | convolution fusion | flops 3998482432 | bytes 13746176 | tf_op jit(solution)/shard_map/dot_general | solution.py:47
  (6 shorter events, 0.1 us)
Async XLA Ops:
  0.6 20.8 %copy-start = (bf16[128,2048]{1,0:T(8,128)(2,1)S(1)}, bf16[128,2048]{1,0:T(8,128)(2,1)}, u32[]{:S(2)}) copy-start(bf16[128,2048]{1,0:T(8,128)(2,1)} %refs_0_.1) | copy-start | bytes 1572868
  0.6 21.0 %collective-permute-start.1 = (bf16[128,2048]{1,0:T(8,128)(2,1)}, bf16[128,2048]{1,0:T(8,128)(2,1)S(1)}, u32[]{:S(2)}, u32[]{:S(2)}) collective-permute-start(bf16[128,2048]{1,0:T(8,128)(2,1)} %refs_0_.1), channel_id=1, source_target_pairs={{0,7},{1,0},{2,1},{3,2},{4,3},{5,4},{6,5},{7,6},{8,15},{9,8},{10,9... | collective-permute-start | bytes 1572872 | tf_op jit(solution)/shard_map/ppermute | solution.py:191
  7.1 14.8 %collective-permute-start = (bf16[128,2048]{1,0:T(8,128)(2,1)}, bf16[128,2048]{1,0:T(8,128)(2,1)S(1)}, u32[]{:S(2)}, u32[]{:S(2)}) collective-permute-start(bf16[128,2048]{1,0:T(8,128)(2,1)} %refs_0_.1), channel_id=1, source_target_pairs={{0,1},{1,2},{2,3},{3,4},{4,5},{5,6},{6,7},{7,0},{8,9},{9,10},{10,1... | collective-permute-start | bytes 1572872 | tf_op jit(solution)/shard_map/ppermute | solution.py:191
  10.3 11.2 %all-to-all-start = ((f32[8,8,128]{2,1,0:T(8,128)}), f32[8,8,128]{2,1,0:T(8,128)S(1)}, u32[]{:S(2)}, u32[]{:S(2)}) async-start(f32[8,8,128]{2,1,0:T(8,128)} %shard_map.67), calls=%async_computation | async-start | bytes 65536 | tf_op jit(solution)/shard_map/all_to_all | solution.py:182
  21.7 14.5 %collective-permute-start.3 = (bf16[128,2048]{1,0:T(8,128)(2,1)S(1)}, bf16[128,2048]{1,0:T(8,128)(2,1)S(1)}, u32[]{:S(2)}, u32[]{:S(2)}) collective-permute-start(bf16[128,2048]{1,0:T(8,128)(2,1)S(1)} %collective-permute-done.1.refs_2_), channel_id=1, source_target_pairs={{0,7},{1,0},{2,1},{3,2},{4,3},{5,4},{6,5},{7,6},{8,15},{9,8},{10,9... | collective-permute-start | bytes 1572872 | tf_op jit(solution)/shard_map/ppermute | solution.py:191
  21.9 15.0 %collective-permute-start.2 = (bf16[128,2048]{1,0:T(8,128)(2,1)S(1)}, bf16[128,2048]{1,0:T(8,128)(2,1)S(1)}, u32[]{:S(2)}, u32[]{:S(2)}) collective-permute-start(bf16[128,2048]{1,0:T(8,128)(2,1)S(1)} %collective-permute-done.refs_1_), channel_id=1, source_target_pairs={{0,1},{1,2},{2,3},{3,4},{4,5},{5,6},{6,7},{7,0},{8,9},{9,10},{10,1... | collective-permute-start | bytes 1572872 | tf_op jit(solution)/shard_map/ppermute | solution.py:191
  36.1 21.6 %collective-permute-start.5 = (bf16[128,2048]{1,0:T(8,128)(2,1)S(1)}, bf16[128,2048]{1,0:T(8,128)(2,1)S(1)}, u32[]{:S(2)}, u32[]{:S(2)}) collective-permute-start(bf16[128,2048]{1,0:T(8,128)(2,1)S(1)} %collective-permute-done.3.refs_4_), channel_id=1, source_target_pairs={{0,7},{1,0},{2,1},{3,2},{4,3},{5,4},{6,5},{7,6},{8,15},{9,8},{10,9... | collective-permute-start | bytes 1572872 | tf_op jit(solution)/shard_map/ppermute | solution.py:191
  37.0 23.2 %collective-permute-start.4 = (bf16[128,2048]{1,0:T(8,128)(2,1)S(1)}, bf16[128,2048]{1,0:T(8,128)(2,1)S(1)}, u32[]{:S(2)}, u32[]{:S(2)}) collective-permute-start(bf16[128,2048]{1,0:T(8,128)(2,1)S(1)} %collective-permute-done.2.refs_3_), channel_id=1, source_target_pairs={{0,1},{1,2},{2,3},{3,4},{4,5},{5,6},{6,7},{7,0},{8,9},{9,10},{10,1... | collective-permute-start | bytes 1572872 | tf_op jit(solution)/shard_map/ppermute | solution.py:191
  57.8 14.3 %collective-permute-start.7 = (bf16[64,2048]{1,0:T(8,128)(2,1)S(1)}, bf16[64,2048]{1,0:T(8,128)(2,1)S(1)}, u32[]{:S(2)}, u32[]{:S(2)}) collective-permute-start(bf16[64,2048]{1,0:T(8,128)(2,1)S(1)} %slice.7), channel_id=1, source_target_pairs={{0,7},{1,0},{2,1},{3,2},{4,3},{5,4},{6,5},{7,6},{8,15},{9,8},{10,9... | collective-permute-start | bytes 786440 | tf_op jit(solution)/shard_map/ppermute | solution.py:191
  60.2 11.9 %collective-permute-start.6 = (bf16[64,2048]{1,0:T(8,128)(2,1)S(1)}, bf16[64,2048]{1,0:T(8,128)(2,1)S(1)}, u32[]{:S(2)}, u32[]{:S(2)}) collective-permute-start(bf16[64,2048]{1,0:T(8,128)(2,1)S(1)} %slice.6), channel_id=1, source_target_pairs={{0,1},{1,2},{2,3},{3,4},{4,5},{5,6},{6,7},{7,0},{8,9},{9,10},{10,1... | collective-permute-start | bytes 786440 | tf_op jit(solution)/shard_map/ppermute | solution.py:191
  72.1 22.1 %copy-start.1 = (bf16[1,2048,896]{2,1,0:T(8,128)(2,1)S(1)}, bf16[1,2048,896]{2,1,0:T(8,128)(2,1)}, u32[]{:S(2)}) copy-start(bf16[1,2048,896]{2,1,0:T(8,128)(2,1)} %param.6) | copy-start | bytes 11010052
  76.5 3.1 %collective-permute-start.8 = (f32[8,512]{1,0:T(8,128)S(1)}, f32[8,512]{1,0:T(8,128)S(1)}, u32[]{:S(2)}, u32[]{:S(2)}) collective-permute-start(f32[8,512]{1,0:T(8,128)S(1)} %get-tuple-element.28), channel_id=1, source_target_pairs={{0,8},{8,0},{16,24},{24,16},{32,40},{40,32},{48,56},{56,48},{64,72... | collective-permute-start | bytes 49160 | tf_op jit(solution)/shard_map/ppermute | solution.py:231
  90.9 2.6 %collective-permute-start.9 = (f32[8,512]{1,0:T(8,128)S(1)}, f32[8,512]{1,0:T(8,128)S(1)}, u32[]{:S(2)}, u32[]{:S(2)}) collective-permute-start(f32[8,512]{1,0:T(8,128)S(1)} %shard_map.75.mine_ref), channel_id=1, source_target_pairs={{0,8},{8,0},{16,24},{24,16},{32,40},{40,32},{48,56},{56,48},{64,72... | collective-permute-start | bytes 49160 | tf_op jit(solution)/shard_map/ppermute | solution.py:233

commit v3 on v2

--- a/solution.py
+++ b/solution.py
@@ -1,3 +1,5 @@
+import functools
+
 import jax
 import jax.numpy as jnp
 from jax import lax
@@ -10,6 +12,7 @@
 R = 8
 HALF = 512
 TOKENS = 1024
+CHUNK = 512
 F32 = jnp.float32
 BF16 = jnp.bfloat16
 VMEM = pltpu.MemorySpace.VMEM
@@ -20,7 +23,13 @@
 
 
 CORES = [(i, i ^ 1) for i in range(DP)]
-CHIPS = [[2 * i for i in range(DP // 2)], [2 * i + 1 for i in range(DP // 2)]]
+ROWS = [[8 * y + o for o in range(8)] for y in range(4)]
+PLANES = [[(8 * y + o) * MP + z for y in range(4) for z in range(MP)] for o in range(8)]
+
+
+def along(base, size, step):
+    span = base * size
+    return [(i, i // span * span + (i + base * step) % span) for i in range(DP)]
 
 
 def after(x, *others):
@@ -69,6 +78,10 @@
     return [slice(i * step, (i + 1) * step) for i in range(count)]
 
 
+def kept(x):
+    return pltpu.with_memory_space_constraint(x, VMEM)
+
+
 def far(x):
     return pltpu.with_memory_space_constraint(x, pltpu.MemorySpace.HBM)
 
@@ -127,31 +140,29 @@
 
 
 def right_kernel(p_ref, err_ref, g_ref, *refs):
-    blocks, (keep_ref, send_ref, rows_ref, grads_ref, held, sems) = refs[:9], refs[9:]
+    blocks, (keep_ref, send_ref, rows_ref, grads_ref, held_ref, sems) = refs[:9], refs[9:]
     me = lax.axis_index("mp")
     starts = [me * 128]
     for step in range(1, 4):
         starts += [lax.rem(me + MP - step, MP) * 128, lax.rem(me + step, MP) * 128]
     last = lax.rem(me + 4, MP) * 128
     starts += [last, last + 64]
-    copies = [pltpu.make_async_copy(g_ref, grads_ref.at[pl.ds(0, TOKENS)], sems.at[9])]
+    copies = []
     for i, (block, start) in enumerate(zip(blocks, starts)):
         size = block.shape[0]
         copies.append(pltpu.make_async_copy(block, rows_ref.at[pl.ds(pl.multiple_of(start, size), size)], sems.at[i]))
-    copies.append(pltpu.make_async_copy(err_ref, held, sems.at[10]))
-    for copy in copies[1:] + copies[:1]:
+    copies.append(pltpu.make_async_copy(g_ref, grads_ref, sems.at[9]))
+    copies.append(pltpu.make_async_copy(err_ref, held_ref, sems.at[10]))
+    for copy in copies:
         copy.start()
-    a, b, c = terms(p_ref[...])
-    left = jnp.concatenate([a, b, c], axis=0).astype(BF16)
-    rows_ref[TOKENS:] = jnp.concatenate([a, a, a, b, b, c, jnp.zeros((2 * R, a.shape[1]), F32)], axis=0).astype(BF16)
-    grads_ref[TOKENS:] = jnp.zeros((8 * R, grads_ref.shape[1]), BF16)
-    for copy in copies[1:10]:
-        copy.wait()
-    projected = fold3(dot(left, rows_ref[:TOKENS], 1, 1))
-    copies[0].wait()
-    value = fold3(dot(split3(projected), grads_ref[:TOKENS], 1, 0))
+    left = split3(p_ref[...])
+    for copy in copies[:9]:
+        copy.wait()
+    projected = fold3(dot(left, rows_ref[...], 1, 1))
+    copies[9].wait()
+    value = fold3(dot(split3(projected), grads_ref[...], 1, 0))
     copies[10].wait()
-    value = value + fold3(dot(left, held[...], 1, 0))
+    value = value + fold3(dot(left, held_ref[...], 1, 0))
     first = value[:, :HALF]
     second = jnp.concatenate([value[:, HALF:], jnp.zeros((R, 2 * HALF - value.shape[1]), F32)], axis=1)
     core = lax.rem(lax.axis_index("dp"), 2)
@@ -159,23 +170,39 @@
     send_ref[...] = jnp.where(core == 0, second, first)
 
 
-def add_spread_kernel(a_ref, b_ref, out_ref):
-    out_ref[...] = jnp.broadcast_to((a_ref[...] + b_ref[...])[None], out_ref.shape)
-
-
-def mean_kernel(parts_ref, out_ref):
-    out_ref[...] = jnp.sum(parts_ref[...], axis=0) / DP
-
-
-def right_factor_kernel(mine_ref, other_ref, grads_ref, q_ref, out_ref):
+def merged_kernel(part, rows_ref, grads_ref, err_ref, out_ref):
+    at = pl.ds(part * CHUNK, CHUNK)
+    out_ref[...] = dot(rows_ref[:, at], grads_ref[...], 0, 0) + err_ref[at].astype(F32)
+
+
+def add_kernel(a_ref, b_ref, out_ref):
+    out_ref[...] = a_ref[...] + b_ref[...]
+
+
+def add4_kernel(scale, own_ref, across_ref, one_ref, other_ref, out_ref):
+    out_ref[...] = ((own_ref[...] + across_ref[...]) + (one_ref[...] + other_ref[...])) * scale
+
+
+def residue_kernel(p_ref, mine_ref, other_ref, *refs):
+    merged, (out_ref, q_ref, held, sems) = refs[:-4], refs[-4:]
     core = lax.rem(lax.axis_index("dp"), 2)
     mine, other = mine_ref[...], other_ref[...]
     first = jnp.where(core == 0, mine, other)
     second = jnp.where(core == 0, other, mine)
     q = jnp.concatenate([first, second[:, : q_ref.shape[1] - HALF]], axis=1)
     q_ref[...] = q
-    a, b, c = terms(-q)
-    out_ref[TOKENS:] = jnp.concatenate([a, b, c, a, b, a, jnp.zeros((2 * R, a.shape[1]), F32)], axis=0).astype(BF16)
+    a, b, c = terms(q)
+    right = jnp.concatenate([a, b, c, a, b, a], axis=0).astype(BF16)
+    copies = []
+    for i, part in enumerate(merged):
+        at = pl.ds(i * CHUNK, CHUNK)
+        a, b, c = terms(p_ref[:, at])
+        left = jnp.concatenate([a, a, a, b, b, c], axis=0).astype(BF16)
+        held[i] = (part[...] - dot(left, right, 0, 0)).astype(BF16)
+        copies.append(pltpu.make_async_copy(held.at[i], out_ref.at[at], sems.at[i]))
+        copies[-1].start()
+    for copy in copies:
+        copy.wait()
 
 
 def exchange(x, axis, groups=None):
@@ -203,43 +230,50 @@
     reduced = exchange(reduced, "mp")
     part = local(left_kernel, shape(MP, R, 256), reduced, tokens, more)
     right2, left2 = pass_on(after(right1, part), after(left1, part))
-    part = exchange(after(part, right1, left1), "mp")
+    part = exchange(after(part, right1, left1), "dp", ROWS)
     part = local(sum_spread_kernel, shape(DP, R, 256), part)
     right3, left3 = pass_on(after(right2, part), after(left2, part))
-    part = exchange(after(part, right2, left2), "dp")
+    part = exchange(after(part, right2, left2), ("dp", "mp"), PLANES)
     part = local(sum_spread_kernel, shape(MP, R, 256), part)
     right4, left4 = pass_on(after(right3, part)[:half], after(left3, part)[half:])
-    part = exchange(after(part, right3, left3), "mp")
+    part = exchange(after(part, right3, left3), "dp", ROWS)
     p_factor = local(gram_schmidt_kernel, pltpu.VMEM((R, depth), F32), part)
     blocks = (tokens, right1, left1, right2, left2, right3, left3, right4, left4)
 
-    keep, send, rows, grads = local(
+    keep, send, rows, grads, near = local(
         right_kernel,
         (
             shape(R, HALF),
             shape(R, HALF),
-            pltpu.VMEM((TOKENS + 8 * R, depth), BF16),
-            pltpu.VMEM((TOKENS + 8 * R, columns), BF16),
+            pltpu.VMEM((TOKENS, depth), BF16),
+            pltpu.VMEM((TOKENS, columns), BF16),
+            pltpu.VMEM((depth, columns), BF16),
         ),
-        pltpu.with_memory_space_constraint(p_factor, VMEM),
+        kept(p_factor),
         far(err),
         far(out_grad),
         *blocks,
         spaces=[VMEM, hbm, hbm] + [pl.ANY] * 9,
-        scratch=[pltpu.VMEM(err.shape, BF16), dma((11,))],
-    )
-    wide = local(add_spread_kernel, shape(DP // 2, R, HALF), keep, lax.ppermute(send, "dp", CORES))
-    mine = local(mean_kernel, shape(R, HALF), exchange(wide, "dp", CHIPS))
+        scratch=[dma((11,))],
+    )
+    rows, grads, near = kept(rows), kept(grads), kept(near)
+    merged = [
+        local(functools.partial(merged_kernel, i), pltpu.VMEM((CHUNK, columns), F32), rows, grads, near) for i in range(depth // CHUNK)
+    ]
+    mine = local(add_kernel, shape(R, HALF), after(keep, merged[0]), lax.ppermute(send, "dp", CORES))
+    for base, scale, beside in ((2, 1.0, merged[1:]), (8, 1.0 / DP, [])):
+        one, other, across = (lax.ppermute(mine, "dp", along(base, 4, step)) for step in (1, 3, 2))
+        mine = after(mine, *beside)
+        mine = local(functools.partial(add4_kernel, scale), shape(R, HALF), mine, across, one, other)
     other = lax.ppermute(mine, "dp", CORES)
-    q_factor, grads = local(
-        right_factor_kernel,
-        (shape(R, columns), pltpu.VMEM(grads.shape, BF16)),
-        mine,
-        other,
-        pltpu.with_memory_space_constraint(grads, VMEM),
-        input_output_aliases={2: 1},
-    )
-    new_error = (dot(rows, grads, 0, 0) + err.astype(F32)).astype(BF16)
+    new_error, q_factor = pl.pallas_call(
+        residue_kernel,
+        out_shape=(shape(depth, columns, dtype=BF16), shape(R, columns)),
+        in_specs=[pl.BlockSpec(memory_space=VMEM)] * (3 + len(merged)),
+        out_specs=(pl.BlockSpec(memory_space=hbm), pl.BlockSpec(memory_space=VMEM)),
+        scratch_shapes=[pltpu.VMEM((len(merged), CHUNK, columns), BF16), dma((len(merged),))],
+        compiler_params=pltpu.CompilerParams(vmem_limit_bytes=12 << 20),
+    )(kept(p_factor), mine, other, *[kept(part) for part in merged])
     return (p_factor, q_factor, new_error[None])
 
 

time: 101 us -> 95.7 us (0.948)
  blocking collectives: 55 us -> 41.9 us
  matrix products: 7 us -> 0 us
  Pallas kernels: 12.1 us -> 19 us
  starting transfers between devices: 20.1 us -> 27 us
    all_to_all x4 -> x3, blocking collectives: 55 us -> 41.9 us  [exchange(): return lax.all_to_all(x, axis, 0, 0, axis_index_groups=groups)]
    dot_general x1 -> x0, matrix products: 7 us -> none  [dot(): lax.dot_general(a, b, (((left,), (right,)), ((), ())), preferred_element_...]
    ppermute x0 -> x6, starting transfers between devices: none -> 6.83 us  [on_device(): lax.ppermute(mine, 'dp', along(base, 4, step))]
    pallas_call x10 -> x14, Pallas kernels: 12.1 us -> 16 us  [local(): pl.pallas_call(kernel, out_shape=out, in_specs=[pl.BlockSpec(memory_space...]
    pallas_call x0 -> x1, Pallas kernels: none -> 2.93 us  [on_device(): pl.pallas_call(residue_kernel, out_shape=(shape(depth, columns, dtype=BF1...]
    ppermute x1, starting transfers between devices: 1.76 us -> 3.24 us  [on_device(): other = lax.ppermute(mine, 'dp', CORES)]
    ppermute x1, starting transfers between devices: 2.3 us -> 0.86 us  [on_device(): lax.ppermute(send, 'dp', CORES)]
    ppermute x0 -> x6, waiting for transfers between devices: none -> 1.34 us  [on_device(): lax.ppermute(mine, 'dp', along(base, 4, step))]
  transfers between devices with their start and end apart: 11 -> 17, of which waited for: 3 -> 5; matrix products, arithmetic and copies ran while one was open for 1% -> 1% of each run, Pallas kernels for 7% -> 13%
where the time goes in v3:
time: 95.7 us; the launch traced here: 95.4 us
  blocking collectives  41.9 us (44%)
  starting transfers between devices  27 us (28%)
  Pallas kernels  19 us (20%)
  waiting for transfers between devices  5.83 us (6%)
  between operations  0.97 us (1%)
    all_to_all x3, blocking collectives, exchange(): return lax.all_to_all(x, axis, 0, 0, axis_index_groups=groups)  41.9 us
    pallas_call x14, Pallas kernels, local(): pl.pallas_call(kernel, out_shape=out, in_specs=[pl.BlockSpec(memory_space...  16 us
    ppermute x4, starting transfers between devices, pass_on(): lax.ppermute(left, 'mp', shift(MP, -1))  9.07 us
    ppermute x6, starting transfers between devices, on_device(): lax.ppermute(mine, 'dp', along(base, 4, step))  6.83 us
    all_to_all x1, waiting for transfers between devices, exchange(): return lax.all_to_all(x, axis, 0, 0, axis_index_groups=groups)  4.26 us
    all_to_all x1, starting transfers between devices, exchange(): return lax.all_to_all(x, axis, 0, 0, axis_index_groups=groups)  4.09 us
    ppermute x1, starting transfers between devices, on_device(): other = lax.ppermute(mine, 'dp', CORES)  3.24 us
    ppermute x4, starting transfers between devices, pass_on(): lax.ppermute(right, 'mp', shift(MP, 1))  2.95 us
  transfers between devices with their start and end apart: 17, of which 5 were waited for; matrix products, arithmetic and copies ran while one was open for 1% of the time, Pallas kernels for 13%

profile of v3, /device:TPU:1, one launch (start us, length us, event | category | flops | bytes accessed | tf_op | source)
XLA Modules:
  0.0 95.4 jit_solution(14734247649612062721)
XLA Ops:
  0.6 6.5 %collective-permute-start.1 = (bf16[128,2048]{1,0:T(8,128)(2,1)}, bf16[128,2048]{1,0:T(8,128)(2,1)S(1)}, u32[]{:S(2)}, u32[]{:S(2)}) collective-permute-start(bf16[128,2048]{1,0:T(8,128)(2,1)} %refs_0_.1), channel_id=1, source_target_pairs={{0,7},{1,0},{2,1},{3,2},{4,3},{5,4},{6,5},{7,6},{8,15},{9,8},{10,9... | collective-permute-start | bytes 1572872 | tf_op jit(solution)/shard_map/ppermute | solution.py:218
  7.1 0.0 collective-permute-start
  7.1 3.1 %shard_map.67 = f32[8,8,128]{2,1,0:T(8,128)} custom-call(f32[8,896]{1,0:T(8,128)} %q_ref.3, bf16[1024,896]{1,0:T(8,128)(2,1)} %g_ref.3), custom_call_target="tpu_custom_call" | custom-call | tf_op jit(solution)/shard_map/pallas_call | solution.py:61
  10.2 4.1 %all-to-all-start = ((f32[8,8,128]{2,1,0:T(8,128)}), f32[8,8,128]{2,1,0:T(8,128)S(1)}, u32[]{:S(2)}, u32[]{:S(2)}) async-start(f32[8,8,128]{2,1,0:T(8,128)} %shard_map.67), calls=%async_computation | async-start | bytes 65536 | tf_op jit(solution)/shard_map/all_to_all | solution.py:209
  14.3 0.0 copy-start
  14.3 2.8 %shard_map.68.more_ref = f32[8,2048]{1,0:T(8,128)S(1)} custom-call(f32[8,896]{1,0:T(8,128)} %q_ref.3, bf16[2048,896]{1,0:T(8,128)(2,1)} %bitcast.2), custom_call_target="tpu_custom_call" | custom-call | tf_op jit(solution)/shard_map/pallas_call | solution.py:61
  17.2 4.3 %all-to-all-done.parts_ref = f32[8,8,128]{2,1,0:T(8,128)S(1)} async-done(((f32[8,8,128]{2,1,0:T(8,128)}), f32[8,8,128]{2,1,0:T(8,128)S(1)}, u32[]{:S(2)}, u32[]{:S(2)}) %all-to-all-start) | async-done | bytes 32800 | tf_op jit(solution)/shard_map/all_to_all | solution.py:209
  21.4 0.0 copy-done
  21.4 0.2 shard_map.69
  21.7 0.0 collective-permute-done.1.refs_2_
  21.7 0.3 collective-permute-start.3
  21.9 0.0 collective-permute-done.refs_1_
  21.9 1.3 %collective-permute-start.2 = (bf16[128,2048]{1,0:T(8,128)(2,1)S(1)}, bf16[128,2048]{1,0:T(8,128)(2,1)S(1)}, u32[]{:S(2)}, u32[]{:S(2)}) collective-permute-start(bf16[128,2048]{1,0:T(8,128)(2,1)S(1)} %collective-permute-done.refs_1_), channel_id=1, source_target_pairs={{0,1},{1,2},{2,3},{3,4},{4,5},{5,6},{6,7},{7,0},{8,9},{9,10},{10,1... | collective-permute-start | bytes 1572872 | tf_op jit(solution)/shard_map/ppermute | solution.py:218
  23.2 11.8 %all_to_all.20.parts_ref = f32[8,8,256]{2,1,0:T(8,128)S(1)} all-to-all(f32[8,8,256]{2,1,0:T(8,128)S(1)} %shard_map.69), channel_id=1, replica_groups={{0,8,16,24,32,40,48,56},{64,72,80,88,96,104,112,120},{128,136,144,152,1..., dimensions={0} | all-to-all | bytes 131072 | tf_op jit(solution)/shard_map/all_to_all | solution.py:209
  35.0 0.0 collective-permute-done.3.refs_4_
  35.0 1.6 %collective-permute-start.5 = (bf16[128,2048]{1,0:T(8,128)(2,1)S(1)}, bf16[128,2048]{1,0:T(8,128)(2,1)S(1)}, u32[]{:S(2)}, u32[]{:S(2)}) collective-permute-start(bf16[128,2048]{1,0:T(8,128)(2,1)S(1)} %collective-permute-done.3.refs_4_), channel_id=1, source_target_pairs={{0,7},{1,0},{2,1},{3,2},{4,3},{5,4},{6,5},{7,6},{8,15},{9,8},{10,9... | collective-permute-start | bytes 1572872 | tf_op jit(solution)/shard_map/ppermute | solution.py:218
  36.6 0.0 collective-permute-done.2.refs_3_
  36.6 0.0 collective-permute-start.4
  36.6 18.8 %all_to_all.21.parts_ref = f32[32,8,256]{2,1,0:T(8,128)S(1)} all-to-all(f32[32,8,256]{2,1,0:T(8,128)S(1)} %shard_map.70), channel_id=1, replica_groups={{0,1,2,3,4,5,6,7,64,65,66,67,68,69,70,71,128,129,130,131,132,133,134,13..., dimensions={0} | all-to-all | bytes 524288 | tf_op jit(solution)/shard_map/all_to_all | solution.py:209
  55.4 0.0 collective-permute-done.5.refs_6_
  55.4 0.8 collective-permute-start.7
  56.2 0.0 collective-permute-done.4.refs_5_
  56.2 1.7 %collective-permute-start.6 = (bf16[64,2048]{1,0:T(8,128)(2,1)S(1)}, bf16[64,2048]{1,0:T(8,128)(2,1)S(1)}, u32[]{:S(2)}, u32[]{:S(2)}) collective-permute-start(bf16[64,2048]{1,0:T(8,128)(2,1)S(1)} %slice.6), channel_id=1, source_target_pairs={{0,1},{1,2},{2,3},{3,4},{4,5},{5,6},{6,7},{7,0},{8,9},{9,10},{10,1... | collective-permute-start | bytes 786440 | tf_op jit(solution)/shard_map/ppermute | solution.py:218
  57.9 11.4 %all_to_all.22.parts_ref = f32[8,8,256]{2,1,0:T(8,128)S(1)} all-to-all(f32[8,8,256]{2,1,0:T(8,128)S(1)} %shard_map.71), channel_id=1, replica_groups={{0,8,16,24,32,40,48,56},{64,72,80,88,96,104,112,120},{128,136,144,152,1..., dimensions={0} | all-to-all | bytes 131072 | tf_op jit(solution)/shard_map/all_to_all | solution.py:209
  69.2 0.9 shard_map.72.p_ref
  70.2 0.0 collective-permute-done.7.refs_8_
  70.2 0.0 collective-permute-done.6.refs_7_
  70.2 3.8 %shard_map.73 = (f32[8,512]{1,0:T(8,128)S(1)}, f32[8,512]{1,0:T(8,128)S(1)}, bf16[1024,2048]{1,0:T(8,128)(2,1)S(1)}, bf16[1024,896]{1,0:T(8,128)(2,1)S(1)}, bf16[2048,896]{1,0:T(8,128)(2,1)S(1)}) custom-call(f32[8,2048]{1,0:T(8,128)S(1)} %shard_map.72.p_ref, bf16[2048,896]{1,0:T(8,128)(2,1)} %bitcast.3, bf16[1024,896]{1,0:T(8,128)(2,1)} %g_ref.3, ...), custom_call_target="tpu_custom_call" | custom-call | tf_op jit(solution)/shard_map/pallas_call | solution.py:61
  74.0 0.9 collective-permute-start.8
  74.8 1.3 %shard_map.74.refs_0_ = f32[512,896]{1,0:T(8,128)S(1)} custom-call(bf16[1024,2048]{1,0:T(8,128)(2,1)S(1)} %get-tuple-element.31.rows_ref, bf16[1024,896]{1,0:T(8,128)(2,1)S(1)} %get-tuple-element.32.grads_ref, bf16[2048,896]{1,0:T(8,128)(2,1)S(1)} %get-tuple-element.33.err_ref), custom_call_target="tpu_custom_call" | custom-call | tf_op jit(solution)/shard_map/pallas_call | solution.py:61
  76.1 0.0 collective-permute-done.8.b_ref
  76.1 0.5 collective-permute-start.10
  76.7 2.4 %collective-permute-start.11 = (f32[8,512]{1,0:T(8,128)S(1)}, f32[8,512]{1,0:T(8,128)S(1)}, u32[]{:S(2)}, u32[]{:S(2)}) collective-permute-start(f32[8,512]{1,0:T(8,128)S(1)} %shard_map.75.own_ref), channel_id=1, source_target_pairs={{0,48},{8,56},{16,0},{24,8},{32,16},{40,24},{48,32},{56,40},{64,11... | collective-permute-start | bytes 49160 | tf_op jit(solution)/shard_map/ppermute | solution.py:265
  79.1 0.0 collective-permute-start.9
  79.1 1.3 %shard_map.78.refs_3_ = f32[512,896]{1,0:T(8,128)S(1)} custom-call(bf16[1024,2048]{1,0:T(8,128)(2,1)S(1)} %get-tuple-element.31.rows_ref, bf16[1024,896]{1,0:T(8,128)(2,1)S(1)} %get-tuple-element.32.grads_ref, bf16[2048,896]{1,0:T(8,128)(2,1)S(1)} %get-tuple-element.33.err_ref), custom_call_target="tpu_custom_call" | custom-call | tf_op jit(solution)/shard_map/pallas_call | solution.py:61
  80.4 1.3 %shard_map.77.refs_2_ = f32[512,896]{1,0:T(8,128)S(1)} custom-call(bf16[1024,2048]{1,0:T(8,128)(2,1)S(1)} %get-tuple-element.31.rows_ref, bf16[1024,896]{1,0:T(8,128)(2,1)S(1)} %get-tuple-element.32.grads_ref, bf16[2048,896]{1,0:T(8,128)(2,1)S(1)} %get-tuple-element.33.err_ref), custom_call_target="tpu_custom_call" | custom-call | tf_op jit(solution)/shard_map/pallas_call | solution.py:61
  81.6 1.3 %shard_map.76.refs_1_ = f32[512,896]{1,0:T(8,128)S(1)} custom-call(bf16[1024,2048]{1,0:T(8,128)(2,1)S(1)} %get-tuple-element.31.rows_ref, bf16[1024,896]{1,0:T(8,128)(2,1)S(1)} %get-tuple-element.32.grads_ref, bf16[2048,896]{1,0:T(8,128)(2,1)S(1)} %get-tuple-element.33.err_ref), custom_call_target="tpu_custom_call" | custom-call | tf_op jit(solution)/shard_map/pallas_call | solution.py:61
  82.9 0.0 collective-permute-done.10.one_ref
  82.9 0.0 collective-permute-done.11.other_ref
  83.0 0.2 collective-permute-done.9.across_ref
  83.2 1.2 %collective-permute-start.12 = (f32[8,512]{1,0:T(8,128)S(1)}, f32[8,512]{1,0:T(8,128)S(1)}, u32[]{:S(2)}, u32[]{:S(2)}) collective-permute-start(f32[8,512]{1,0:T(8,128)S(1)} %shard_map.79.own_ref), channel_id=1, source_target_pairs={{0,128},{8,136},{16,144},{24,152},{32,160},{40,168},{48,176},{56,1... | collective-permute-start | bytes 49160 | tf_op jit(solution)/shard_map/ppermute | solution.py:265
  84.4 0.2 collective-permute-start.13
  84.6 2.5 %collective-permute-start.14 = (f32[8,512]{1,0:T(8,128)S(1)}, f32[8,512]{1,0:T(8,128)S(1)}, u32[]{:S(2)}, u32[]{:S(2)}) collective-permute-start(f32[8,512]{1,0:T(8,128)S(1)} %shard_map.79.own_ref), channel_id=1, source_target_pairs={{0,192},{8,200},{16,208},{24,216},{32,224},{40,232},{48,240},{56,2... | collective-permute-start | bytes 49160 | tf_op jit(solution)/shard_map/ppermute | solution.py:265
  87.1 0.3 collective-permute-done.12.across_ref
  87.3 0.8 collective-permute-done.13.one_ref
  88.2 0.0 collective-permute-done.14.other_ref
  88.2 3.2 %collective-permute-start.15 = (f32[8,512]{1,0:T(8,128)S(1)}, f32[8,512]{1,0:T(8,128)S(1)}, u32[]{:S(2)}, u32[]{:S(2)}) collective-permute-start(f32[8,512]{1,0:T(8,128)S(1)} %shard_map.80.mine_ref), channel_id=1, source_target_pairs={{0,8},{8,0},{16,24},{24,16},{32,40},{40,32},{48,56},{56,48},{64,72... | collective-permute-start | bytes 49160 | tf_op jit(solution)/shard_map/ppermute | solution.py:268
  91.4 0.6 copy.7
  92.1 0.2 collective-permute-done.15.other_ref
  92.3 2.9 %shard_map.81 = (bf16[2048,896]{1,0:T(8,128)(2,1)}, f32[8,896]{1,0:T(8,128)}) custom-call(f32[8,2048]{1,0:T(8,128)S(1)} %shard_map.72.p_ref, f32[8,512]{1,0:T(8,128)S(1)} %shard_map.80.mine_ref, f32[8,512]{1,0:T(8,128)S(1)} %collective-permute-done.15.other_ref, f32[512,896]{1,0:T(8,128)S(1)} %shard_map.74.refs_0_, f32[512,896]{1,0:T(8,128)S(1)} %shard_map.76.refs_1_, ...), custom_call_target="tpu_custom_call" | custom-call | tf_op jit(solution)/shard_map/pallas_call | solution.py:269
  (7 shorter events, 0.1 us)
Async XLA Ops:
  0.6 21.0 %collective-permute-start.1 = (bf16[128,2048]{1,0:T(8,128)(2,1)}, bf16[128,2048]{1,0:T(8,128)(2,1)S(1)}, u32[]{:S(2)}, u32[]{:S(2)}) collective-permute-start(bf16[128,2048]{1,0:T(8,128)(2,1)} %refs_0_.1), channel_id=1, source_target_pairs={{0,7},{1,0},{2,1},{3,2},{4,3},{5,4},{6,5},{7,6},{8,15},{9,8},{10,9... | collective-permute-start | bytes 1572872 | tf_op jit(solution)/shard_map/ppermute | solution.py:218
  7.1 14.8 %collective-permute-start = (bf16[128,2048]{1,0:T(8,128)(2,1)}, bf16[128,2048]{1,0:T(8,128)(2,1)S(1)}, u32[]{:S(2)}, u32[]{:S(2)}) collective-permute-start(bf16[128,2048]{1,0:T(8,128)(2,1)} %refs_0_.1), channel_id=1, source_target_pairs={{0,1},{1,2},{2,3},{3,4},{4,5},{5,6},{6,7},{7,0},{8,9},{9,10},{10,1... | collective-permute-start | bytes 1572872 | tf_op jit(solution)/shard_map/ppermute | solution.py:218
  10.2 11.2 %all-to-all-start = ((f32[8,8,128]{2,1,0:T(8,128)}), f32[8,8,128]{2,1,0:T(8,128)S(1)}, u32[]{:S(2)}, u32[]{:S(2)}) async-start(f32[8,8,128]{2,1,0:T(8,128)} %shard_map.67), calls=%async_computation | async-start | bytes 65536 | tf_op jit(solution)/shard_map/all_to_all | solution.py:209
  14.3 7.1 %copy-start = (bf16[128,2048]{1,0:T(8,128)(2,1)S(1)}, bf16[128,2048]{1,0:T(8,128)(2,1)}, u32[]{:S(2)}) copy-start(bf16[128,2048]{1,0:T(8,128)(2,1)} %refs_0_.1) | copy-start | bytes 1572868
  21.7 13.3 %collective-permute-start.3 = (bf16[128,2048]{1,0:T(8,128)(2,1)S(1)}, bf16[128,2048]{1,0:T(8,128)(2,1)S(1)}, u32[]{:S(2)}, u32[]{:S(2)}) collective-permute-start(bf16[128,2048]{1,0:T(8,128)(2,1)S(1)} %collective-permute-done.1.refs_2_), channel_id=1, source_target_pairs={{0,7},{1,0},{2,1},{3,2},{4,3},{5,4},{6,5},{7,6},{8,15},{9,8},{10,9... | collective-permute-start | bytes 1572872 | tf_op jit(solution)/shard_map/ppermute | solution.py:218
  21.9 14.6 %collective-permute-start.2 = (bf16[128,2048]{1,0:T(8,128)(2,1)S(1)}, bf16[128,2048]{1,0:T(8,128)(2,1)S(1)}, u32[]{:S(2)}, u32[]{:S(2)}) collective-permute-start(bf16[128,2048]{1,0:T(8,128)(2,1)S(1)} %collective-permute-done.refs_1_), channel_id=1, source_target_pairs={{0,1},{1,2},{2,3},{3,4},{4,5},{5,6},{6,7},{7,0},{8,9},{9,10},{10,1... | collective-permute-start | bytes 1572872 | tf_op jit(solution)/shard_map/ppermute | solution.py:218
  35.0 20.4 %collective-permute-start.5 = (bf16[128,2048]{1,0:T(8,128)(2,1)S(1)}, bf16[128,2048]{1,0:T(8,128)(2,1)S(1)}, u32[]{:S(2)}, u32[]{:S(2)}) collective-permute-start(bf16[128,2048]{1,0:T(8,128)(2,1)S(1)} %collective-permute-done.3.refs_4_), channel_id=1, source_target_pairs={{0,7},{1,0},{2,1},{3,2},{4,3},{5,4},{6,5},{7,6},{8,15},{9,8},{10,9... | collective-permute-start | bytes 1572872 | tf_op jit(solution)/shard_map/ppermute | solution.py:218
  36.6 19.6 %collective-permute-start.4 = (bf16[128,2048]{1,0:T(8,128)(2,1)S(1)}, bf16[128,2048]{1,0:T(8,128)(2,1)S(1)}, u32[]{:S(2)}, u32[]{:S(2)}) collective-permute-start(bf16[128,2048]{1,0:T(8,128)(2,1)S(1)} %collective-permute-done.2.refs_3_), channel_id=1, source_target_pairs={{0,1},{1,2},{2,3},{3,4},{4,5},{5,6},{6,7},{7,0},{8,9},{9,10},{10,1... | collective-permute-start | bytes 1572872 | tf_op jit(solution)/shard_map/ppermute | solution.py:218
  55.4 14.7 %collective-permute-start.7 = (bf16[64,2048]{1,0:T(8,128)(2,1)S(1)}, bf16[64,2048]{1,0:T(8,128)(2,1)S(1)}, u32[]{:S(2)}, u32[]{:S(2)}) collective-permute-start(bf16[64,2048]{1,0:T(8,128)(2,1)S(1)} %slice.7), channel_id=1, source_target_pairs={{0,7},{1,0},{2,1},{3,2},{4,3},{5,4},{6,5},{7,6},{8,15},{9,8},{10,9... | collective-permute-start | bytes 786440 | tf_op jit(solution)/shard_map/ppermute | solution.py:218
  56.2 14.0 %collective-permute-start.6 = (bf16[64,2048]{1,0:T(8,128)(2,1)S(1)}, bf16[64,2048]{1,0:T(8,128)(2,1)S(1)}, u32[]{:S(2)}, u32[]{:S(2)}) collective-permute-start(bf16[64,2048]{1,0:T(8,128)(2,1)S(1)} %slice.6), channel_id=1, source_target_pairs={{0,1},{1,2},{2,3},{3,4},{4,5},{5,6},{6,7},{7,0},{8,9},{9,10},{10,1... | collective-permute-start | bytes 786440 | tf_op jit(solution)/shard_map/ppermute | solution.py:218
  74.0 2.2 %collective-permute-start.8 = (f32[8,512]{1,0:T(8,128)S(1)}, f32[8,512]{1,0:T(8,128)S(1)}, u32[]{:S(2)}, u32[]{:S(2)}) collective-permute-start(f32[8,512]{1,0:T(8,128)S(1)} %get-tuple-element.35), channel_id=1, source_target_pairs={{0,8},{8,0},{16,24},{24,16},{32,40},{40,32},{48,56},{56,48},{64,72... | collective-permute-start | bytes 49160 | tf_op jit(solution)/shard_map/ppermute | solution.py:263
  76.1 6.8 %collective-permute-start.10 = (f32[8,512]{1,0:T(8,128)S(1)}, f32[8,512]{1,0:T(8,128)S(1)}, u32[]{:S(2)}, u32[]{:S(2)}) collective-permute-start(f32[8,512]{1,0:T(8,128)S(1)} %shard_map.75.own_ref), channel_id=1, source_target_pairs={{0,16},{8,24},{16,32},{24,40},{32,48},{40,56},{48,0},{56,8},{64,80... | collective-permute-start | bytes 49160 | tf_op jit(solution)/shard_map/ppermute | solution.py:265
  76.7 6.3 %collective-permute-start.11 = (f32[8,512]{1,0:T(8,128)S(1)}, f32[8,512]{1,0:T(8,128)S(1)}, u32[]{:S(2)}, u32[]{:S(2)}) collective-permute-start(f32[8,512]{1,0:T(8,128)S(1)} %shard_map.75.own_ref), channel_id=1, source_target_pairs={{0,48},{8,56},{16,0},{24,8},{32,16},{40,24},{48,32},{56,40},{64,11... | collective-permute-start | bytes 49160 | tf_op jit(solution)/shard_map/ppermute | solution.py:265
  79.1 4.1 %collective-permute-start.9 = (f32[8,512]{1,0:T(8,128)S(1)}, f32[8,512]{1,0:T(8,128)S(1)}, u32[]{:S(2)}, u32[]{:S(2)}) collective-permute-start(f32[8,512]{1,0:T(8,128)S(1)} %shard_map.75.own_ref), channel_id=1, source_target_pairs={{0,32},{8,40},{16,48},{24,56},{32,0},{40,8},{48,16},{56,24},{64,96... | collective-permute-start | bytes 49160 | tf_op jit(solution)/shard_map/ppermute | solution.py:265
  83.2 4.2 %collective-permute-start.12 = (f32[8,512]{1,0:T(8,128)S(1)}, f32[8,512]{1,0:T(8,128)S(1)}, u32[]{:S(2)}, u32[]{:S(2)}) collective-permute-start(f32[8,512]{1,0:T(8,128)S(1)} %shard_map.79.own_ref), channel_id=1, source_target_pairs={{0,128},{8,136},{16,144},{24,152},{32,160},{40,168},{48,176},{56,1... | collective-permute-start | bytes 49160 | tf_op jit(solution)/shard_map/ppermute | solution.py:265
  84.4 3.8 %collective-permute-start.13 = (f32[8,512]{1,0:T(8,128)S(1)}, f32[8,512]{1,0:T(8,128)S(1)}, u32[]{:S(2)}, u32[]{:S(2)}) collective-permute-start(f32[8,512]{1,0:T(8,128)S(1)} %shard_map.79.own_ref), channel_id=1, source_target_pairs={{0,64},{8,72},{16,80},{24,88},{32,96},{40,104},{48,112},{56,120},{... | collective-permute-start | bytes 49160 | tf_op jit(solution)/shard_map/ppermute | solution.py:265
  84.6 3.6 %collective-permute-start.14 = (f32[8,512]{1,0:T(8,128)S(1)}, f32[8,512]{1,0:T(8,128)S(1)}, u32[]{:S(2)}, u32[]{:S(2)}) collective-permute-start(f32[8,512]{1,0:T(8,128)S(1)} %shard_map.79.own_ref), channel_id=1, source_target_pairs={{0,192},{8,200},{16,208},{24,216},{32,224},{40,232},{48,240},{56,2... | collective-permute-start | bytes 49160 | tf_op jit(solution)/shard_map/ppermute | solution.py:265
  88.2 4.1 %collective-permute-start.15 = (f32[8,512]{1,0:T(8,128)S(1)}, f32[8,512]{1,0:T(8,128)S(1)}, u32[]{:S(2)}, u32[]{:S(2)}) collective-permute-start(f32[8,512]{1,0:T(8,128)S(1)} %shard_map.80.mine_ref), channel_id=1, source_target_pairs={{0,8},{8,0},{16,24},{24,16},{32,40},{40,32},{48,56},{56,48},{64,72... | collective-permute-start | bytes 49160 | tf_op jit(solution)/shard_map/ppermute | solution.py:268

commit v4 on v3

--- a/solution.py
+++ b/solution.py
@@ -23,8 +23,7 @@
 
 
 CORES = [(i, i ^ 1) for i in range(DP)]
-ROWS = [[8 * y + o for o in range(8)] for y in range(4)]
-PLANES = [[(8 * y + o) * MP + z for y in range(4) for z in range(MP)] for o in range(8)]
+CHIPS = [[2 * i for i in range(DP // 2)], [2 * i + 1 for i in range(DP // 2)]]
 
 
 def along(base, size, step):
@@ -89,16 +88,17 @@
 def reduce_kernel(q_ref, g_ref, out_ref, q_held, held, sems):
     first = pltpu.make_async_copy(q_ref, q_held, sems.at[0])
     first.start()
-    copies = [pltpu.make_async_copy(g_ref.at[at], held.at[at], sems.at[1 + i]) for i, at in enumerate(pieces(TOKENS, 4))]
+    parts = pieces(TOKENS, 2)
+    copies = [pltpu.make_async_copy(g_ref.at[at], held.at[at], sems.at[1 + i]) for i, at in enumerate(parts)]
     for copy in copies:
         copy.start()
     first.wait()
     q = split3(q_held[...])
-    for i, (copy, at) in enumerate(zip(copies, pieces(TOKENS, 4))):
+    for i, (copy, at) in enumerate(zip(copies, parts)):
         copy.wait()
         value = fold3(dot(q, held[at], 1, 1))
-        out_ref[2 * i] = value[:, :128]
-        out_ref[2 * i + 1] = value[:, 128:]
+        for j in range(4):
+            out_ref[4 * i + j] = value[:, j * 128 : (j + 1) * 128]
 
 
 def error_left_kernel(q_ref, err_ref, out_ref, q_held, held, sems):
@@ -118,8 +118,16 @@
 def left_kernel(parts_ref, x_ref, more_ref, out_ref):
     reduced = jnp.sum(parts_ref[...], axis=0)
     value = fold3(dot(split3(reduced), x_ref[...], 1, 0)) + more_ref[...]
-    for z in range(MP):
-        out_ref[z] = value[:, z * 256 : (z + 1) * 256]
+    for i in range(out_ref.shape[0]):
+        out_ref[i] = value[:, i * 128 : (i + 1) * 128]
+
+
+def sum_kernel(parts_ref, out_ref):
+    out_ref[...] = jnp.sum(parts_ref[...], axis=0)
+
+
+def add_spread_kernel(a_ref, b_ref, out_ref):
+    out_ref[...] = jnp.broadcast_to((a_ref[...] + b_ref[...])[None], out_ref.shape)
 
 
 def sum_spread_kernel(parts_ref, out_ref):
@@ -127,8 +135,7 @@
     out_ref[...] = jnp.broadcast_to(value[None], out_ref.shape)
 
 
-def gram_schmidt_kernel(parts_ref, out_ref):
-    rows = jnp.concatenate([parts_ref[z] for z in range(MP)], axis=1)
+def gram_schmidt(rows):
     index = lax.broadcasted_iota(jnp.int32, (R, 1), 0)
     for i in range(R):
         vector = rows[i : i + 1]
@@ -136,11 +143,11 @@
         scale = 1.0 / jnp.sqrt(products[i : i + 1] + 1e-06)
         vector = vector * scale
         rows = jnp.where(index > i, rows - (products * scale) * vector, jnp.where(index == i, vector, rows))
-    out_ref[...] = rows
-
-
-def right_kernel(p_ref, err_ref, g_ref, *refs):
-    blocks, (keep_ref, send_ref, rows_ref, grads_ref, held_ref, sems) = refs[:9], refs[9:]
+    return rows
+
+
+def right_kernel(parts_ref, err_ref, g_ref, *refs):
+    blocks, (p_ref, keep_ref, send_ref, rows_ref, grads_ref, held_ref, sems) = refs[:9], refs[9:]
     me = lax.axis_index("mp")
     starts = [me * 128]
     for step in range(1, 4):
@@ -155,7 +162,9 @@
     copies.append(pltpu.make_async_copy(err_ref, held_ref, sems.at[10]))
     for copy in copies:
         copy.start()
-    left = split3(p_ref[...])
+    p = gram_schmidt(jnp.concatenate([parts_ref[i] for i in range(parts_ref.shape[0])], axis=1))
+    p_ref[...] = p
+    left = split3(p)
     for copy in copies[:9]:
         copy.wait()
     projected = fold3(dot(left, rows_ref[...], 1, 1))
@@ -228,28 +237,28 @@
         error_left_kernel, shape(R, depth), far(q_prev), far(err), spaces=[hbm, hbm], scratch=[held, pltpu.VMEM(err.shape, BF16), dma((5,))]
     )
     reduced = exchange(reduced, "mp")
-    part = local(left_kernel, shape(MP, R, 256), reduced, tokens, more)
+    part = local(left_kernel, shape(DP // 2, R, 128), reduced, tokens, more)
     right2, left2 = pass_on(after(right1, part), after(left1, part))
-    part = exchange(after(part, right1, left1), "dp", ROWS)
-    part = local(sum_spread_kernel, shape(DP, R, 256), part)
+    part = local(sum_kernel, shape(R, 128), exchange(after(part, right1, left1), "dp", CHIPS))
     right3, left3 = pass_on(after(right2, part), after(left2, part))
-    part = exchange(after(part, right2, left2), ("dp", "mp"), PLANES)
-    part = local(sum_spread_kernel, shape(MP, R, 256), part)
+    part = local(add_spread_kernel, shape(MP, R, 128), part, lax.ppermute(part, "dp", CORES))
+    part = exchange(after(part, right2, left2), "mp")
+    part = local(sum_spread_kernel, shape(DP // 2, R, 128), part)
     right4, left4 = pass_on(after(right3, part)[:half], after(left3, part)[half:])
-    part = exchange(after(part, right3, left3), "dp", ROWS)
-    p_factor = local(gram_schmidt_kernel, pltpu.VMEM((R, depth), F32), part)
+    part = exchange(after(part, right3, left3), "dp", CHIPS)
     blocks = (tokens, right1, left1, right2, left2, right3, left3, right4, left4)
 
-    keep, send, rows, grads, near = local(
+    p_factor, keep, send, rows, grads, near = local(
         right_kernel,
         (
+            pltpu.VMEM((R, depth), F32),
             shape(R, HALF),
             shape(R, HALF),
             pltpu.VMEM((TOKENS, depth), BF16),
             pltpu.VMEM((TOKENS, columns), BF16),
             pltpu.VMEM((depth, columns), BF16),
         ),
-        kept(p_factor),
+        part,
         far(err),
         far(out_grad),
         *blocks,
@@ -261,7 +270,7 @@
         local(functools.partial(merged_kernel, i), pltpu.VMEM((CHUNK, columns), F32), rows, grads, near) for i in range(depth // CHUNK)
     ]
     mine = local(add_kernel, shape(R, HALF), after(keep, merged[0]), lax.ppermute(send, "dp", CORES))
-    for base, scale, beside in ((2, 1.0, merged[1:]), (8, 1.0 / DP, [])):
+    for base, scale, beside in ((2, 1.0, merged[1:3]), (8, 1.0 / DP, merged[3:])):
         one, other, across = (lax.ppermute(mine, "dp", along(base, 4, step)) for step in (1, 3, 2))
         mine = after(mine, *beside)
         mine = local(functools.partial(add4_kernel, scale), shape(R, HALF), mine, across, one, other)

time: 95.7 us -> 92.4 us (0.966)
  blocking collectives: 41.9 us -> 33.5 us
  starting transfers between devices: 27 us -> 33.6 us
  Pallas kernels: 19 us -> 17.6 us
    all_to_all x3, blocking collectives: 41.9 us -> 33.5 us  [exchange(): return lax.all_to_all(x, axis, 0, 0, axis_index_groups=groups)]
    ppermute x0 -> x1, starting transfers between devices: none -> 4.65 us  [on_device(): lax.ppermute(part, 'dp', CORES)]
    ppermute x1, starting transfers between devices: 0.86 us -> 3.72 us  [on_device(): lax.ppermute(send, 'dp', CORES)]
    pallas_call x14, Pallas kernels: 16 us -> 14.7 us  [local(): pl.pallas_call(kernel, out_shape=out, in_specs=[pl.BlockSpec(memory_space...]
    ppermute x6, waiting for transfers between devices: 1.34 us -> 0.02 us  [on_device(): lax.ppermute(mine, 'dp', along(base, 4, step))]
    ppermute x1, starting transfers between devices: 3.24 us -> 2.17 us  [on_device(): other = lax.ppermute(mine, 'dp', CORES)]
  transfers between devices with their start and end apart: 17 -> 18, of which waited for: 5 -> 3; matrix products, arithmetic and copies ran while one was open for 1% -> 1% of each run, Pallas kernels for 13% -> 12%
where the time goes in v4:
time: 92.4 us; the launch traced here: 92.2 us
  starting transfers between devices  33.6 us (36%)
  blocking collectives  33.5 us (36%)
  Pallas kernels  17.6 us (19%)
  waiting for transfers between devices  5.83 us (6%)
  between operations  0.98 us (1%)
    all_to_all x3, blocking collectives, exchange(): return lax.all_to_all(x, axis, 0, 0, axis_index_groups=groups)  33.5 us
    pallas_call x14, Pallas kernels, local(): pl.pallas_call(kernel, out_shape=out, in_specs=[pl.BlockSpec(memory_space...  14.7 us
    ppermute x4, starting transfers between devices, pass_on(): lax.ppermute(left, 'mp', shift(MP, -1))  8.84 us
    ppermute x6, starting transfers between devices, on_device(): lax.ppermute(mine, 'dp', along(base, 4, step))  7.67 us
    all_to_all x1, waiting for transfers between devices, exchange(): return lax.all_to_all(x, axis, 0, 0, axis_index_groups=groups)  4.76 us
    ppermute x1, starting transfers between devices, on_device(): lax.ppermute(part, 'dp', CORES)  4.65 us
    all_to_all x1, starting transfers between devices, exchange(): return lax.all_to_all(x, axis, 0, 0, axis_index_groups=groups)  4.08 us
    ppermute x1, starting transfers between devices, on_device(): lax.ppermute(send, 'dp', CORES)  3.72 us
  transfers between devices with their start and end apart: 18, of which 3 were waited for; matrix products, arithmetic and copies ran while one was open for 1% of the time, Pallas kernels for 12%

profile of v4, /device:TPU:1, one launch (start us, length us, event | category | flops | bytes accessed | tf_op | source)
XLA Modules:
  0.0 92.2 jit_solution(7841922816052840696)
XLA Ops:
  0.6 6.5 %collective-permute-start.1 = (bf16[128,2048]{1,0:T(8,128)(2,1)}, bf16[128,2048]{1,0:T(8,128)(2,1)S(1)}, u32[]{:S(2)}, u32[]{:S(2)}) collective-permute-start(bf16[128,2048]{1,0:T(8,128)(2,1)} %refs_0_.1), channel_id=1, source_target_pairs={{0,7},{1,0},{2,1},{3,2},{4,3},{5,4},{6,5},{7,6},{8,15},{9,8},{10,9... | collective-permute-start | bytes 1572872 | tf_op jit(solution)/shard_map/ppermute | solution.py:227
  7.1 0.0 collective-permute-start
  7.1 2.6 %shard_map.67 = f32[8,8,128]{2,1,0:T(8,128)} custom-call(f32[8,896]{1,0:T(8,128)} %q_ref.3, bf16[1024,896]{1,0:T(8,128)(2,1)} %g_ref.3), custom_call_target="tpu_custom_call" | custom-call | tf_op jit(solution)/shard_map/pallas_call | solution.py:60
  9.7 4.1 %all-to-all-start = ((f32[8,8,128]{2,1,0:T(8,128)}), f32[8,8,128]{2,1,0:T(8,128)S(1)}, u32[]{:S(2)}, u32[]{:S(2)}) async-start(f32[8,8,128]{2,1,0:T(8,128)} %shard_map.67), calls=%async_computation | async-start | bytes 65536 | tf_op jit(solution)/shard_map/all_to_all | solution.py:218
  13.8 0.0 copy-start
  13.8 2.8 %shard_map.68.more_ref = f32[8,2048]{1,0:T(8,128)S(1)} custom-call(f32[8,896]{1,0:T(8,128)} %q_ref.3, bf16[2048,896]{1,0:T(8,128)(2,1)} %bitcast.2), custom_call_target="tpu_custom_call" | custom-call | tf_op jit(solution)/shard_map/pallas_call | solution.py:60
  16.7 4.8 %all-to-all-done.parts_ref = f32[8,8,128]{2,1,0:T(8,128)S(1)} async-done(((f32[8,8,128]{2,1,0:T(8,128)}), f32[8,8,128]{2,1,0:T(8,128)S(1)}, u32[]{:S(2)}, u32[]{:S(2)}) %all-to-all-start) | async-done | bytes 32800 | tf_op jit(solution)/shard_map/all_to_all | solution.py:218
  21.4 0.0 copy-done
  21.4 0.2 shard_map.69
  21.7 0.0 collective-permute-done.1.refs_2_
  21.7 0.4 collective-permute-start.4
  22.1 0.0 collective-permute-done.refs_1_
  22.1 1.2 %collective-permute-start.3 = (bf16[128,2048]{1,0:T(8,128)(2,1)S(1)}, bf16[128,2048]{1,0:T(8,128)(2,1)S(1)}, u32[]{:S(2)}, u32[]{:S(2)}) collective-permute-start(bf16[128,2048]{1,0:T(8,128)(2,1)S(1)} %collective-permute-done.refs_1_), channel_id=1, source_target_pairs={{0,1},{1,2},{2,3},{3,4},{4,5},{5,6},{6,7},{7,0},{8,9},{9,10},{10,1... | collective-permute-start | bytes 1572872 | tf_op jit(solution)/shard_map/ppermute | solution.py:227
  23.2 13.1 %all_to_all.20.parts_ref = f32[16,8,128]{2,1,0:T(8,128)S(1)} all-to-all(f32[16,8,128]{2,1,0:T(8,128)S(1)} %shard_map.69), channel_id=1, replica_groups={{0,16,32,48,64,80,96,112,128,144,160,176,192,208,224,240},{8,24,40,56,7..., dimensions={0} | all-to-all | bytes 131072 | tf_op jit(solution)/shard_map/all_to_all | solution.py:218
  36.3 0.0 collective-permute-done.4.refs_4_
  36.3 1.6 %collective-permute-start.6 = (bf16[128,2048]{1,0:T(8,128)(2,1)S(1)}, bf16[128,2048]{1,0:T(8,128)(2,1)S(1)}, u32[]{:S(2)}, u32[]{:S(2)}) collective-permute-start(bf16[128,2048]{1,0:T(8,128)(2,1)S(1)} %collective-permute-done.4.refs_4_), channel_id=1, source_target_pairs={{0,7},{1,0},{2,1},{3,2},{4,3},{5,4},{6,5},{7,6},{8,15},{9,8},{10,9... | collective-permute-start | bytes 1572872 | tf_op jit(solution)/shard_map/ppermute | solution.py:227
  37.9 0.0 collective-permute-done.3.refs_3_
  37.9 0.0 collective-permute-start.5
  37.9 4.7 %collective-permute-start.2 = (f32[8,128]{1,0:T(8,128)S(1)}, f32[8,128]{1,0:T(8,128)S(1)}, u32[]{:S(2)}, u32[]{:S(2)}) collective-permute-start(f32[8,128]{1,0:T(8,128)S(1)} %shard_map.70.a_ref), channel_id=1, source_target_pairs={{0,8},{8,0},{16,24},{24,16},{32,40},{40,32},{48,56},{56,48},{64,72... | collective-permute-start | bytes 12296 | tf_op jit(solution)/shard_map/ppermute | solution.py:244
  42.6 0.8 collective-permute-done.2.b_ref
  43.4 11.1 %all_to_all.21.parts_ref = f32[8,8,128]{2,1,0:T(8,128)S(1)} all-to-all(f32[8,8,128]{2,1,0:T(8,128)S(1)} %shard_map.71), channel_id=1, replica_groups=mesh['dp'=32,'mp'=8] {'mp'}, dimensions={0} | all-to-all | bytes 65536 | tf_op jit(solution)/shard_map/all_to_all | solution.py:218
  54.5 0.0 collective-permute-done.6.refs_6_
  54.5 0.4 collective-permute-start.8
  54.9 0.0 collective-permute-done.5.refs_5_
  54.9 1.3 %collective-permute-start.7 = (bf16[64,2048]{1,0:T(8,128)(2,1)S(1)}, bf16[64,2048]{1,0:T(8,128)(2,1)S(1)}, u32[]{:S(2)}, u32[]{:S(2)}) collective-permute-start(bf16[64,2048]{1,0:T(8,128)(2,1)S(1)} %slice.6), channel_id=1, source_target_pairs={{0,1},{1,2},{2,3},{3,4},{4,5},{5,6},{6,7},{7,0},{8,9},{9,10},{10,1... | collective-permute-start | bytes 786440 | tf_op jit(solution)/shard_map/ppermute | solution.py:227
  56.2 9.4 %all_to_all.22.parts_ref = f32[16,8,128]{2,1,0:T(8,128)S(1)} all-to-all(f32[16,8,128]{2,1,0:T(8,128)S(1)} %shard_map.72), channel_id=1, replica_groups={{0,16,32,48,64,80,96,112,128,144,160,176,192,208,224,240},{8,24,40,56,7..., dimensions={0} | all-to-all | bytes 131072 | tf_op jit(solution)/shard_map/all_to_all | solution.py:218
  65.5 0.0 collective-permute-done.8.refs_8_
  65.5 0.0 collective-permute-done.7.refs_7_
  65.5 3.8 %shard_map.73 = (f32[8,2048]{1,0:T(8,128)S(1)}, f32[8,512]{1,0:T(8,128)S(1)}, f32[8,512]{1,0:T(8,128)S(1)}, bf16[1024,2048]{1,0:T(8,128)(2,1)S(1)}, bf16[1024,89...) custom-call(f32[16,8,128]{2,1,0:T(8,128)S(1)} %all_to_all.22.parts_ref, bf16[2048,896]{1,0:T(8,128)(2,1)} %bitcast.3, ...), custom_call_target="tpu_custom_call" | custom-call | tf_op jit(solution)/shard_map/pallas_call | solution.py:60
  69.4 3.7 %collective-permute-start.9 = (f32[8,512]{1,0:T(8,128)S(1)}, f32[8,512]{1,0:T(8,128)S(1)}, u32[]{:S(2)}, u32[]{:S(2)}) collective-permute-start(f32[8,512]{1,0:T(8,128)S(1)} %get-tuple-element.38), channel_id=1, source_target_pairs={{0,8},{8,0},{16,24},{24,16},{32,40},{40,32},{48,56},{56,48},{64,72... | collective-permute-start | bytes 49160 | tf_op jit(solution)/shard_map/ppermute | solution.py:272
  73.1 1.3 %shard_map.74.refs_0_ = f32[512,896]{1,0:T(8,128)S(1)} custom-call(bf16[1024,2048]{1,0:T(8,128)(2,1)S(1)} %get-tuple-element.34.rows_ref, bf16[1024,896]{1,0:T(8,128)(2,1)S(1)} %get-tuple-element.35.grads_ref, bf16[2048,896]{1,0:T(8,128)(2,1)S(1)} %get-tuple-element.36.err_ref), custom_call_target="tpu_custom_call" | custom-call | tf_op jit(solution)/shard_map/pallas_call | solution.py:60
  74.4 0.0 collective-permute-done.9.b_ref
  74.4 1.3 %collective-permute-start.10 = (f32[8,512]{1,0:T(8,128)S(1)}, f32[8,512]{1,0:T(8,128)S(1)}, u32[]{:S(2)}, u32[]{:S(2)}) collective-permute-start(f32[8,512]{1,0:T(8,128)S(1)} %shard_map.75.own_ref), channel_id=1, source_target_pairs={{0,32},{8,40},{16,48},{24,56},{32,0},{40,8},{48,16},{56,24},{64,96... | collective-permute-start | bytes 49160 | tf_op jit(solution)/shard_map/ppermute | solution.py:274
  75.7 0.4 collective-permute-start.11
  76.2 2.2 %collective-permute-start.12 = (f32[8,512]{1,0:T(8,128)S(1)}, f32[8,512]{1,0:T(8,128)S(1)}, u32[]{:S(2)}, u32[]{:S(2)}) collective-permute-start(f32[8,512]{1,0:T(8,128)S(1)} %shard_map.75.own_ref), channel_id=1, source_target_pairs={{0,48},{8,56},{16,0},{24,8},{32,16},{40,24},{48,32},{56,40},{64,11... | collective-permute-start | bytes 49160 | tf_op jit(solution)/shard_map/ppermute | solution.py:274
  78.4 1.3 %shard_map.77.refs_2_ = f32[512,896]{1,0:T(8,128)S(1)} custom-call(bf16[1024,2048]{1,0:T(8,128)(2,1)S(1)} %get-tuple-element.34.rows_ref, bf16[1024,896]{1,0:T(8,128)(2,1)S(1)} %get-tuple-element.35.grads_ref, bf16[2048,896]{1,0:T(8,128)(2,1)S(1)} %get-tuple-element.36.err_ref), custom_call_target="tpu_custom_call" | custom-call | tf_op jit(solution)/shard_map/pallas_call | solution.py:60
  79.7 1.3 %shard_map.76.refs_1_ = f32[512,896]{1,0:T(8,128)S(1)} custom-call(bf16[1024,2048]{1,0:T(8,128)(2,1)S(1)} %get-tuple-element.34.rows_ref, bf16[1024,896]{1,0:T(8,128)(2,1)S(1)} %get-tuple-element.35.grads_ref, bf16[2048,896]{1,0:T(8,128)(2,1)S(1)} %get-tuple-element.36.err_ref), custom_call_target="tpu_custom_call" | custom-call | tf_op jit(solution)/shard_map/pallas_call | solution.py:60
  81.0 0.0 collective-permute-done.10.across_ref
  81.0 0.0 collective-permute-done.11.one_ref
  81.0 0.0 collective-permute-done.12.other_ref
  81.0 1.0 %collective-permute-start.13 = (f32[8,512]{1,0:T(8,128)S(1)}, f32[8,512]{1,0:T(8,128)S(1)}, u32[]{:S(2)}, u32[]{:S(2)}) collective-permute-start(f32[8,512]{1,0:T(8,128)S(1)} %shard_map.78.own_ref), channel_id=1, source_target_pairs={{0,128},{8,136},{16,144},{24,152},{32,160},{40,168},{48,176},{56,1... | collective-permute-start | bytes 49160 | tf_op jit(solution)/shard_map/ppermute | solution.py:274
  82.0 0.5 collective-permute-start.14
  82.6 2.2 %collective-permute-start.15 = (f32[8,512]{1,0:T(8,128)S(1)}, f32[8,512]{1,0:T(8,128)S(1)}, u32[]{:S(2)}, u32[]{:S(2)}) collective-permute-start(f32[8,512]{1,0:T(8,128)S(1)} %shard_map.78.own_ref), channel_id=1, source_target_pairs={{0,192},{8,200},{16,208},{24,216},{32,224},{40,232},{48,240},{56,2... | collective-permute-start | bytes 49160 | tf_op jit(solution)/shard_map/ppermute | solution.py:274
  84.7 1.3 %shard_map.79.refs_3_ = f32[512,896]{1,0:T(8,128)S(1)} custom-call(bf16[1024,2048]{1,0:T(8,128)(2,1)S(1)} %get-tuple-element.34.rows_ref, bf16[1024,896]{1,0:T(8,128)(2,1)S(1)} %get-tuple-element.35.grads_ref, bf16[2048,896]{1,0:T(8,128)(2,1)S(1)} %get-tuple-element.36.err_ref), custom_call_target="tpu_custom_call" | custom-call | tf_op jit(solution)/shard_map/pallas_call | solution.py:60
  86.0 0.0 collective-permute-done.13.across_ref
  86.0 0.0 collective-permute-done.14.one_ref
  86.0 0.0 collective-permute-done.15.other_ref
  86.1 2.2 %collective-permute-start.16 = (f32[8,512]{1,0:T(8,128)S(1)}, f32[8,512]{1,0:T(8,128)S(1)}, u32[]{:S(2)}, u32[]{:S(2)}) collective-permute-start(f32[8,512]{1,0:T(8,128)S(1)} %shard_map.80.mine_ref), channel_id=1, source_target_pairs={{0,8},{8,0},{16,24},{24,16},{32,40},{40,32},{48,56},{56,48},{64,72... | collective-permute-start | bytes 49160 | tf_op jit(solution)/shard_map/ppermute | solution.py:277
  88.2 0.6 copy.7
  88.9 0.2 collective-permute-done.16.other_ref
  89.1 2.9 %shard_map.81 = (bf16[2048,896]{1,0:T(8,128)(2,1)}, f32[8,896]{1,0:T(8,128)}) custom-call(f32[8,2048]{1,0:T(8,128)S(1)} %get-tuple-element.43.p_ref, f32[8,512]{1,0:T(8,128)S(1)} %shard_map.80.mine_ref, f32[8,512]{1,0:T(8,128)S(1)} %collective-permute-done.16.other_ref, f32[512,896]{1,0:T(8,128)S(1)} %shard_map.74.refs_0_, ...), custom_call_target="tpu_custom_call" | custom-call | tf_op jit(solution)/shard_map/pallas_call | solution.py:278
  (8 shorter events, 0.1 us)
Async XLA Ops:
  0.6 21.0 %collective-permute-start.1 = (bf16[128,2048]{1,0:T(8,128)(2,1)}, bf16[128,2048]{1,0:T(8,128)(2,1)S(1)}, u32[]{:S(2)}, u32[]{:S(2)}) collective-permute-start(bf16[128,2048]{1,0:T(8,128)(2,1)} %refs_0_.1), channel_id=1, source_target_pairs={{0,7},{1,0},{2,1},{3,2},{4,3},{5,4},{6,5},{7,6},{8,15},{9,8},{10,9... | collective-permute-start | bytes 1572872 | tf_op jit(solution)/shard_map/ppermute | solution.py:227
  7.1 14.9 %collective-permute-start = (bf16[128,2048]{1,0:T(8,128)(2,1)}, bf16[128,2048]{1,0:T(8,128)(2,1)S(1)}, u32[]{:S(2)}, u32[]{:S(2)}) collective-permute-start(bf16[128,2048]{1,0:T(8,128)(2,1)} %refs_0_.1), channel_id=1, source_target_pairs={{0,1},{1,2},{2,3},{3,4},{4,5},{5,6},{6,7},{7,0},{8,9},{9,10},{10,1... | collective-permute-start | bytes 1572872 | tf_op jit(solution)/shard_map/ppermute | solution.py:227
  9.7 11.7 %all-to-all-start = ((f32[8,8,128]{2,1,0:T(8,128)}), f32[8,8,128]{2,1,0:T(8,128)S(1)}, u32[]{:S(2)}, u32[]{:S(2)}) async-start(f32[8,8,128]{2,1,0:T(8,128)} %shard_map.67), calls=%async_computation | async-start | bytes 65536 | tf_op jit(solution)/shard_map/all_to_all | solution.py:218
  13.8 7.6 %copy-start = (bf16[128,2048]{1,0:T(8,128)(2,1)S(1)}, bf16[128,2048]{1,0:T(8,128)(2,1)}, u32[]{:S(2)}) copy-start(bf16[128,2048]{1,0:T(8,128)(2,1)} %refs_0_.1) | copy-start | bytes 1572868
  21.7 14.6 %collective-permute-start.4 = (bf16[128,2048]{1,0:T(8,128)(2,1)S(1)}, bf16[128,2048]{1,0:T(8,128)(2,1)S(1)}, u32[]{:S(2)}, u32[]{:S(2)}) collective-permute-start(bf16[128,2048]{1,0:T(8,128)(2,1)S(1)} %collective-permute-done.1.refs_2_), channel_id=1, source_target_pairs={{0,7},{1,0},{2,1},{3,2},{4,3},{5,4},{6,5},{7,6},{8,15},{9,8},{10,9... | collective-permute-start | bytes 1572872 | tf_op jit(solution)/shard_map/ppermute | solution.py:227
  22.1 15.8 %collective-permute-start.3 = (bf16[128,2048]{1,0:T(8,128)(2,1)S(1)}, bf16[128,2048]{1,0:T(8,128)(2,1)S(1)}, u32[]{:S(2)}, u32[]{:S(2)}) collective-permute-start(bf16[128,2048]{1,0:T(8,128)(2,1)S(1)} %collective-permute-done.refs_1_), channel_id=1, source_target_pairs={{0,1},{1,2},{2,3},{3,4},{4,5},{5,6},{6,7},{7,0},{8,9},{9,10},{10,1... | collective-permute-start | bytes 1572872 | tf_op jit(solution)/shard_map/ppermute | solution.py:227
  36.3 18.2 %collective-permute-start.6 = (bf16[128,2048]{1,0:T(8,128)(2,1)S(1)}, bf16[128,2048]{1,0:T(8,128)(2,1)S(1)}, u32[]{:S(2)}, u32[]{:S(2)}) collective-permute-start(bf16[128,2048]{1,0:T(8,128)(2,1)S(1)} %collective-permute-done.4.refs_4_), channel_id=1, source_target_pairs={{0,7},{1,0},{2,1},{3,2},{4,3},{5,4},{6,5},{7,6},{8,15},{9,8},{10,9... | collective-permute-start | bytes 1572872 | tf_op jit(solution)/shard_map/ppermute | solution.py:227
  37.9 17.0 %collective-permute-start.5 = (bf16[128,2048]{1,0:T(8,128)(2,1)S(1)}, bf16[128,2048]{1,0:T(8,128)(2,1)S(1)}, u32[]{:S(2)}, u32[]{:S(2)}) collective-permute-start(bf16[128,2048]{1,0:T(8,128)(2,1)S(1)} %collective-permute-done.3.refs_3_), channel_id=1, source_target_pairs={{0,1},{1,2},{2,3},{3,4},{4,5},{5,6},{6,7},{7,0},{8,9},{9,10},{10,1... | collective-permute-start | bytes 1572872 | tf_op jit(solution)/shard_map/ppermute | solution.py:227
  37.9 5.5 %collective-permute-start.2 = (f32[8,128]{1,0:T(8,128)S(1)}, f32[8,128]{1,0:T(8,128)S(1)}, u32[]{:S(2)}, u32[]{:S(2)}) collective-permute-start(f32[8,128]{1,0:T(8,128)S(1)} %shard_map.70.a_ref), channel_id=1, source_target_pairs={{0,8},{8,0},{16,24},{24,16},{32,40},{40,32},{48,56},{56,48},{64,72... | collective-permute-start | bytes 12296 | tf_op jit(solution)/shard_map/ppermute | solution.py:244
  54.5 11.0 %collective-permute-start.8 = (bf16[64,2048]{1,0:T(8,128)(2,1)S(1)}, bf16[64,2048]{1,0:T(8,128)(2,1)S(1)}, u32[]{:S(2)}, u32[]{:S(2)}) collective-permute-start(bf16[64,2048]{1,0:T(8,128)(2,1)S(1)} %slice.7), channel_id=1, source_target_pairs={{0,7},{1,0},{2,1},{3,2},{4,3},{5,4},{6,5},{7,6},{8,15},{9,8},{10,9... | collective-permute-start | bytes 786440 | tf_op jit(solution)/shard_map/ppermute | solution.py:227
  54.9 10.6 %collective-permute-start.7 = (bf16[64,2048]{1,0:T(8,128)(2,1)S(1)}, bf16[64,2048]{1,0:T(8,128)(2,1)S(1)}, u32[]{:S(2)}, u32[]{:S(2)}) collective-permute-start(bf16[64,2048]{1,0:T(8,128)(2,1)S(1)} %slice.6), channel_id=1, source_target_pairs={{0,1},{1,2},{2,3},{3,4},{4,5},{5,6},{6,7},{7,0},{8,9},{9,10},{10,1... | collective-permute-start | bytes 786440 | tf_op jit(solution)/shard_map/ppermute | solution.py:227
  69.4 5.0 %collective-permute-start.9 = (f32[8,512]{1,0:T(8,128)S(1)}, f32[8,512]{1,0:T(8,128)S(1)}, u32[]{:S(2)}, u32[]{:S(2)}) collective-permute-start(f32[8,512]{1,0:T(8,128)S(1)} %get-tuple-element.38), channel_id=1, source_target_pairs={{0,8},{8,0},{16,24},{24,16},{32,40},{40,32},{48,56},{56,48},{64,72... | collective-permute-start | bytes 49160 | tf_op jit(solution)/shard_map/ppermute | solution.py:272
  74.4 6.5 %collective-permute-start.10 = (f32[8,512]{1,0:T(8,128)S(1)}, f32[8,512]{1,0:T(8,128)S(1)}, u32[]{:S(2)}, u32[]{:S(2)}) collective-permute-start(f32[8,512]{1,0:T(8,128)S(1)} %shard_map.75.own_ref), channel_id=1, source_target_pairs={{0,32},{8,40},{16,48},{24,56},{32,0},{40,8},{48,16},{56,24},{64,96... | collective-permute-start | bytes 49160 | tf_op jit(solution)/shard_map/ppermute | solution.py:274
  75.7 5.3 %collective-permute-start.11 = (f32[8,512]{1,0:T(8,128)S(1)}, f32[8,512]{1,0:T(8,128)S(1)}, u32[]{:S(2)}, u32[]{:S(2)}) collective-permute-start(f32[8,512]{1,0:T(8,128)S(1)} %shard_map.75.own_ref), channel_id=1, source_target_pairs={{0,16},{8,24},{16,32},{24,40},{32,48},{40,56},{48,0},{56,8},{64,80... | collective-permute-start | bytes 49160 | tf_op jit(solution)/shard_map/ppermute | solution.py:274
  76.2 4.8 %collective-permute-start.12 = (f32[8,512]{1,0:T(8,128)S(1)}, f32[8,512]{1,0:T(8,128)S(1)}, u32[]{:S(2)}, u32[]{:S(2)}) collective-permute-start(f32[8,512]{1,0:T(8,128)S(1)} %shard_map.75.own_ref), channel_id=1, source_target_pairs={{0,48},{8,56},{16,0},{24,8},{32,16},{40,24},{48,32},{56,40},{64,11... | collective-permute-start | bytes 49160 | tf_op jit(solution)/shard_map/ppermute | solution.py:274
  81.0 5.0 %collective-permute-start.13 = (f32[8,512]{1,0:T(8,128)S(1)}, f32[8,512]{1,0:T(8,128)S(1)}, u32[]{:S(2)}, u32[]{:S(2)}) collective-permute-start(f32[8,512]{1,0:T(8,128)S(1)} %shard_map.78.own_ref), channel_id=1, source_target_pairs={{0,128},{8,136},{16,144},{24,152},{32,160},{40,168},{48,176},{56,1... | collective-permute-start | bytes 49160 | tf_op jit(solution)/shard_map/ppermute | solution.py:274
  82.0 4.0 %collective-permute-start.14 = (f32[8,512]{1,0:T(8,128)S(1)}, f32[8,512]{1,0:T(8,128)S(1)}, u32[]{:S(2)}, u32[]{:S(2)}) collective-permute-start(f32[8,512]{1,0:T(8,128)S(1)} %shard_map.78.own_ref), channel_id=1, source_target_pairs={{0,64},{8,72},{16,80},{24,88},{32,96},{40,104},{48,112},{56,120},{... | collective-permute-start | bytes 49160 | tf_op jit(solution)/shard_map/ppermute | solution.py:274
  82.6 3.5 %collective-permute-start.15 = (f32[8,512]{1,0:T(8,128)S(1)}, f32[8,512]{1,0:T(8,128)S(1)}, u32[]{:S(2)}, u32[]{:S(2)}) collective-permute-start(f32[8,512]{1,0:T(8,128)S(1)} %shard_map.78.own_ref), channel_id=1, source_target_pairs={{0,192},{8,200},{16,208},{24,216},{32,224},{40,232},{48,240},{56,2... | collective-permute-start | bytes 49160 | tf_op jit(solution)/shard_map/ppermute | solution.py:274
  86.1 3.0 %collective-permute-start.16 = (f32[8,512]{1,0:T(8,128)S(1)}, f32[8,512]{1,0:T(8,128)S(1)}, u32[]{:S(2)}, u32[]{:S(2)}) collective-permute-start(f32[8,512]{1,0:T(8,128)S(1)} %shard_map.80.mine_ref), channel_id=1, source_target_pairs={{0,8},{8,0},{16,24},{24,16},{32,40},{40,32},{48,56},{56,48},{64,72... | collective-permute-start | bytes 49160 | tf_op jit(solution)/shard_map/ppermute | solution.py:277

commit v5 on v4

--- a/solution.py
+++ b/solution.py
@@ -10,7 +10,6 @@
 MP = 8
 DP = 32
 R = 8
-HALF = 512
 TOKENS = 1024
 CHUNK = 512
 F32 = jnp.float32
@@ -146,68 +145,68 @@
     return rows
 
 
+def starts_of():
+    me = lax.axis_index("mp")
+    owners = [me]
+    for step in range(1, 4):
+        owners += [lax.rem(me + MP - step, MP), lax.rem(me + step, MP)]
+    owners.append(lax.rem(me + 4, MP))
+    return [pl.multiple_of(owner * 128, 128) for owner in owners]
+
+
 def right_kernel(parts_ref, err_ref, g_ref, *refs):
-    blocks, (p_ref, keep_ref, send_ref, rows_ref, grads_ref, held_ref, sems) = refs[:9], refs[9:]
-    me = lax.axis_index("mp")
-    starts = [me * 128]
-    for step in range(1, 4):
-        starts += [lax.rem(me + MP - step, MP) * 128, lax.rem(me + step, MP) * 128]
-    last = lax.rem(me + 4, MP) * 128
-    starts += [last, last + 64]
+    blocks, (p_ref, value_ref, projected_ref, rows_ref, grads_ref, held_ref, sems) = refs[:7], refs[7:]
     copies = []
-    for i, (block, start) in enumerate(zip(blocks, starts)):
-        size = block.shape[0]
-        copies.append(pltpu.make_async_copy(block, rows_ref.at[pl.ds(pl.multiple_of(start, size), size)], sems.at[i]))
-    copies.append(pltpu.make_async_copy(g_ref, grads_ref, sems.at[9]))
-    copies.append(pltpu.make_async_copy(err_ref, held_ref, sems.at[10]))
+    for i, (block, start) in enumerate(zip(blocks, starts_of())):
+        copies.append(pltpu.make_async_copy(block, rows_ref.at[pl.ds(start, 128)], sems.at[i]))
+    copies.append(pltpu.make_async_copy(err_ref, held_ref, sems.at[7]))
+    copies.append(pltpu.make_async_copy(g_ref, grads_ref, sems.at[8]))
     for copy in copies:
         copy.start()
+    rows_ref[pl.ds(starts_of()[7], 128)] = jnp.zeros((128, rows_ref.shape[1]), BF16)
     p = gram_schmidt(jnp.concatenate([parts_ref[i] for i in range(parts_ref.shape[0])], axis=1))
     p_ref[...] = p
     left = split3(p)
-    for copy in copies[:9]:
+    for copy in copies[:7]:
         copy.wait()
-    projected = fold3(dot(left, rows_ref[...], 1, 1))
-    copies[9].wait()
-    value = fold3(dot(split3(projected), grads_ref[...], 1, 0))
-    copies[10].wait()
-    value = value + fold3(dot(left, held_ref[...], 1, 0))
-    first = value[:, :HALF]
-    second = jnp.concatenate([value[:, HALF:], jnp.zeros((R, 2 * HALF - value.shape[1]), F32)], axis=1)
-    core = lax.rem(lax.axis_index("dp"), 2)
-    keep_ref[...] = jnp.where(core == 0, first, second)
-    send_ref[...] = jnp.where(core == 0, second, first)
-
-
-def merged_kernel(part, rows_ref, grads_ref, err_ref, out_ref):
+    projected_ref[...] = fold3(dot(left, rows_ref[...], 1, 1))
+    copies[7].wait()
+    value_ref[...] = fold3(dot(left, held_ref[...], 1, 0))
+    copies[8].wait()
+
+
+def right_last_kernel(p_ref, value_ref, projected_ref, grads_ref, block_ref, old_ref, out_ref, rows_ref, total, sem):
+    del old_ref
+    start = starts_of()[7]
+    copy = pltpu.make_async_copy(block_ref, rows_ref.at[pl.ds(start, 128)], sem)
+    copy.start()
+    total[...] = projected_ref[...]
+    total[:, pl.ds(start, 128)] = fold3(dot(split3(p_ref[...]), block_ref[...], 1, 1))
+    out_ref[...] = value_ref[...] + fold3(dot(split3(total[...]), grads_ref[...], 1, 0))
+    copy.wait()
+
+
+def merged_kernel(part, p_ref, rows_ref, grads_ref, err_ref, out_ref, left_ref):
     at = pl.ds(part * CHUNK, CHUNK)
+    a, b, c = terms(p_ref[:, at])
+    left_ref[...] = jnp.concatenate([a, a, a, b, b, c], axis=0).T.astype(BF16)
     out_ref[...] = dot(rows_ref[:, at], grads_ref[...], 0, 0) + err_ref[at].astype(F32)
 
 
-def add_kernel(a_ref, b_ref, out_ref):
-    out_ref[...] = a_ref[...] + b_ref[...]
-
-
-def add4_kernel(scale, own_ref, across_ref, one_ref, other_ref, out_ref):
-    out_ref[...] = ((own_ref[...] + across_ref[...]) + (one_ref[...] + other_ref[...])) * scale
-
-
-def residue_kernel(p_ref, mine_ref, other_ref, *refs):
-    merged, (out_ref, q_ref, held, sems) = refs[:-4], refs[-4:]
-    core = lax.rem(lax.axis_index("dp"), 2)
-    mine, other = mine_ref[...], other_ref[...]
-    first = jnp.where(core == 0, mine, other)
-    second = jnp.where(core == 0, other, mine)
-    q = jnp.concatenate([first, second[:, : q_ref.shape[1] - HALF]], axis=1)
+def add4_kernel(own_ref, across_ref, one_ref, other_ref, out_ref):
+    out_ref[...] = (own_ref[...] + across_ref[...]) + (one_ref[...] + other_ref[...])
+
+
+def residue_kernel(mine_ref, other_ref, *refs):
+    merged, lefts, (out_ref, q_ref, held, sems) = refs[:4], refs[4:8], refs[8:]
+    q = (mine_ref[...] + other_ref[...]) / DP
     q_ref[...] = q
     a, b, c = terms(q)
     right = jnp.concatenate([a, b, c, a, b, a], axis=0).astype(BF16)
     copies = []
-    for i, part in enumerate(merged):
+    for i, (part, left) in enumerate(zip(merged, lefts)):
         at = pl.ds(i * CHUNK, CHUNK)
-        a, b, c = terms(p_ref[:, at])
-        left = jnp.concatenate([a, a, a, b, b, c], axis=0).astype(BF16)
-        held[i] = (part[...] - dot(left, right, 0, 0)).astype(BF16)
+        held[i] = (part[...] - dot(left[...], right, 1, 0)).astype(BF16)
         copies.append(pltpu.make_async_copy(held.at[i], out_ref.at[at], sems.at[i]))
         copies[-1].start()
     for copy in copies:
@@ -221,39 +220,41 @@
 def on_device(tokens, out_grad, error, q_prev):
     err = error[0]
     depth, columns = err.shape
-    half = tokens.shape[0] // 2
-
-    def pass_on(right, left):
-        return lax.ppermute(right, "mp", shift(MP, 1)), lax.ppermute(left, "mp", shift(MP, -1))
-
-    right1, left1 = pass_on(tokens, tokens)
+
+    def rightward(x):
+        return lax.ppermute(x, "mp", shift(MP, 1))
+
+    def leftward(x):
+        return lax.ppermute(x, "mp", shift(MP, -1))
+
+    right1 = rightward(tokens)
     hbm = pltpu.MemorySpace.HBM
     dma = pltpu.SemaphoreType.DMA
     held = pltpu.VMEM((R, columns), F32)
     reduced = local(
         reduce_kernel, shape(MP, R, 128), far(q_prev), far(out_grad), spaces=[hbm, hbm], scratch=[held, pltpu.VMEM(out_grad.shape, BF16), dma((5,))]
     )
+    left1 = leftward(after(tokens, reduced))
     more = local(
         error_left_kernel, shape(R, depth), far(q_prev), far(err), spaces=[hbm, hbm], scratch=[held, pltpu.VMEM(err.shape, BF16), dma((5,))]
     )
     reduced = exchange(reduced, "mp")
     part = local(left_kernel, shape(DP // 2, R, 128), reduced, tokens, more)
-    right2, left2 = pass_on(after(right1, part), after(left1, part))
-    part = local(sum_kernel, shape(R, 128), exchange(after(part, right1, left1), "dp", CHIPS))
-    right3, left3 = pass_on(after(right2, part), after(left2, part))
+    right2 = rightward(after(right1, part))
+    part = local(sum_kernel, shape(R, 128), exchange(after(part, right1), "dp", CHIPS))
+    right3, left2 = rightward(after(right2, part)), leftward(after(left1, part))
     part = local(add_spread_kernel, shape(MP, R, 128), part, lax.ppermute(part, "dp", CORES))
-    part = exchange(after(part, right2, left2), "mp")
+    part = exchange(after(part, right2, left1), "mp")
     part = local(sum_spread_kernel, shape(DP // 2, R, 128), part)
-    right4, left4 = pass_on(after(right3, part)[:half], after(left3, part)[half:])
-    part = exchange(after(part, right3, left3), "dp", CHIPS)
-    blocks = (tokens, right1, left1, right2, left2, right3, left3, right4, left4)
-
-    p_factor, keep, send, rows, grads, near = local(
+    right4, left3 = rightward(after(right3, part)), leftward(after(left2, part))
+    part = exchange(after(part, right3, left2), "dp", CHIPS)
+    blocks = (tokens, right1, left1, right2, left2, right3, left3)
+    p_factor, value, projected, rows, grads, near = local(
         right_kernel,
         (
             pltpu.VMEM((R, depth), F32),
-            shape(R, HALF),
-            shape(R, HALF),
+            pltpu.VMEM((R, columns), F32),
+            pltpu.VMEM((R, TOKENS), F32),
             pltpu.VMEM((TOKENS, depth), BF16),
             pltpu.VMEM((TOKENS, columns), BF16),
             pltpu.VMEM((depth, columns), BF16),
@@ -262,27 +263,37 @@
         far(err),
         far(out_grad),
         *blocks,
-        spaces=[VMEM, hbm, hbm] + [pl.ANY] * 9,
-        scratch=[dma((11,))],
-    )
-    rows, grads, near = kept(rows), kept(grads), kept(near)
-    merged = [
-        local(functools.partial(merged_kernel, i), pltpu.VMEM((CHUNK, columns), F32), rows, grads, near) for i in range(depth // CHUNK)
-    ]
-    mine = local(add_kernel, shape(R, HALF), after(keep, merged[0]), lax.ppermute(send, "dp", CORES))
-    for base, scale, beside in ((2, 1.0, merged[1:3]), (8, 1.0 / DP, merged[3:])):
+        spaces=[VMEM, hbm, hbm] + [pl.ANY] * 7,
+        scratch=[dma((9,))],
+    )
+    p, grads, near = kept(p_factor), kept(grads), kept(near)
+    mine, rows = local(
+        right_last_kernel,
+        (shape(R, columns), pltpu.VMEM((TOKENS, depth), BF16)),
+        p,
+        kept(value),
+        kept(projected),
+        grads,
+        right4,
+        kept(rows),
+        scratch=[pltpu.VMEM((R, TOKENS), F32), dma],
+        input_output_aliases={5: 1},
+    )
+    rows = kept(rows)
+    out = (pltpu.VMEM((CHUNK, columns), F32), pltpu.VMEM((CHUNK, 6 * R), BF16))
+    merged, lefts = zip(*[local(functools.partial(merged_kernel, i), out, p, rows, grads, near) for i in range(depth // CHUNK)])
+    for base, beside in ((2, merged[:2]), (8, merged[2:])):
         one, other, across = (lax.ppermute(mine, "dp", along(base, 4, step)) for step in (1, 3, 2))
-        mine = after(mine, *beside)
-        mine = local(functools.partial(add4_kernel, scale), shape(R, HALF), mine, across, one, other)
+        mine = local(add4_kernel, shape(R, columns), after(mine, *beside), across, one, other)
     other = lax.ppermute(mine, "dp", CORES)
     new_error, q_factor = pl.pallas_call(
         residue_kernel,
         out_shape=(shape(depth, columns, dtype=BF16), shape(R, columns)),
-        in_specs=[pl.BlockSpec(memory_space=VMEM)] * (3 + len(merged)),
+        in_specs=[pl.BlockSpec(memory_space=VMEM)] * (2 + 2 * len(merged)),
         out_specs=(pl.BlockSpec(memory_space=hbm), pl.BlockSpec(memory_space=VMEM)),
         scratch_shapes=[pltpu.VMEM((len(merged), CHUNK, columns), BF16), dma((len(merged),))],
         compiler_params=pltpu.CompilerParams(vmem_limit_bytes=12 << 20),
-    )(kept(p_factor), mine, other, *[kept(part) for part in merged])
+    )(mine, other, *[kept(part) for part in merged + lefts])
     return (p_factor, q_factor, new_error[None])
 
 

time: 92.4 us -> 90.8 us (0.983)
  starting transfers between devices: 33.6 us -> 32.3 us
    ppermute x9 -> x7, starting transfers between devices: 15 us -> 9.57 us  [the longest x3 5.91 us: leftward(): return lax.ppermute(x, 'mp', shift(MP, -1))]
    ppermute x1, starting transfers between devices: 2.17 us -> 5.47 us  [on_device(): other = lax.ppermute(mine, 'dp', CORES)]
    all_to_all x1, starting transfers between devices: 4.08 us -> 7.3 us  [exchange(): return lax.all_to_all(x, axis, 0, 0, axis_index_groups=groups)]
    all_to_all x1, waiting for transfers between devices: 4.76 us -> 2.26 us  [exchange(): return lax.all_to_all(x, axis, 0, 0, axis_index_groups=groups)]
    ppermute x6, starting transfers between devices: 7.67 us -> 6.07 us  [on_device(): lax.ppermute(mine, 'dp', along(base, 4, step))]
    ppermute x6, waiting for transfers between devices: 0.02 us -> 1.31 us  [on_device(): lax.ppermute(mine, 'dp', along(base, 4, step))]
  transfers between devices with their start and end apart: 18 -> 16, of which waited for: 3 -> 6; matrix products, arithmetic and copies ran while one was open for 1% -> 1% of each run, Pallas kernels for 12% -> 16%
where the time goes in v5:
time: 90.8 us; the launch traced here: 90.5 us
  blocking collectives  33.6 us (37%)
  starting transfers between devices  32.3 us (36%)
  Pallas kernels  18.1 us (20%)
  waiting for transfers between devices  4.97 us (5%)
  between operations  0.96 us (1%)
    all_to_all x3, blocking collectives, exchange(): return lax.all_to_all(x, axis, 0, 0, axis_index_groups=groups)  33.6 us
    pallas_call x14, Pallas kernels, local(): pl.pallas_call(kernel, out_shape=out, in_specs=[pl.BlockSpec(memory_space...  15.2 us
    all_to_all x1, starting transfers between devices, exchange(): return lax.all_to_all(x, axis, 0, 0, axis_index_groups=groups)  7.3 us
    ppermute x6, starting transfers between devices, on_device(): lax.ppermute(mine, 'dp', along(base, 4, step))  6.07 us
    ppermute x3, starting transfers between devices, leftward(): return lax.ppermute(x, 'mp', shift(MP, -1))  5.91 us
    ppermute x1, starting transfers between devices, on_device(): other = lax.ppermute(mine, 'dp', CORES)  5.47 us
    ppermute x1, starting transfers between devices, on_device(): lax.ppermute(part, 'dp', CORES)  3.87 us
    ppermute x4, starting transfers between devices, rightward(): return lax.ppermute(x, 'mp', shift(MP, 1))  3.66 us
  transfers between devices with their start and end apart: 16, of which 6 were waited for; matrix products, arithmetic and copies ran while one was open for 1% of the time, Pallas kernels for 16%

profile of v5, /device:TPU:1, one launch (start us, length us, event | category | flops | bytes accessed | tf_op | source)
XLA Modules:
  0.0 90.5 jit_solution(11651680164461357333)
XLA Ops:
  0.6 0.0 copy-start
  0.6 2.5 %collective-permute-start = (bf16[128,2048]{1,0:T(8,128)(2,1)}, bf16[128,2048]{1,0:T(8,128)(2,1)S(1)}, u32[]{:S(2)}, u32[]{:S(2)}) collective-permute-start(bf16[128,2048]{1,0:T(8,128)(2,1)} %refs_0_.1), channel_id=1, source_target_pairs={{0,1},{1,2},{2,3},{3,4},{4,5},{5,6},{6,7},{7,0},{8,9},{9,10},{10,1... | collective-permute-start | bytes 1572872 | tf_op jit(solution)/shard_map/ppermute | solution.py:225
  3.2 2.6 %shard_map.67 = f32[8,8,128]{2,1,0:T(8,128)} custom-call(f32[8,896]{1,0:T(8,128)} %q_ref.3, bf16[1024,896]{1,0:T(8,128)(2,1)} %g_ref.3), custom_call_target="tpu_custom_call" | custom-call | tf_op jit(solution)/shard_map/pallas_call | solution.py:59
  5.8 7.3 %all-to-all-start = ((f32[8,8,128]{2,1,0:T(8,128)}), f32[8,8,128]{2,1,0:T(8,128)S(1)}, u32[]{:S(2)}, u32[]{:S(2)}) async-start(f32[8,8,128]{2,1,0:T(8,128)} %shard_map.67), calls=%async_computation | async-start | bytes 65536 | tf_op jit(solution)/shard_map/all_to_all | solution.py:217
  13.1 0.0 copy-done
  13.1 2.7 %collective-permute-start.3 = (bf16[128,2048]{1,0:T(8,128)(2,1)S(1)}, bf16[128,2048]{1,0:T(8,128)(2,1)S(1)}, u32[]{:S(2)}, u32[]{:S(2)}) collective-permute-start(bf16[128,2048]{1,0:T(8,128)(2,1)S(1)} %copy-done), channel_id=1, source_target_pairs={{0,7},{1,0},{2,1},{3,2},{4,3},{5,4},{6,5},{7,6},{8,15},{9,8},{10,9... | collective-permute-start | bytes 1572872 | tf_op jit(solution)/shard_map/ppermute | solution.py:228
  15.8 2.8 %shard_map.68.more_ref = f32[8,2048]{1,0:T(8,128)S(1)} custom-call(f32[8,896]{1,0:T(8,128)} %q_ref.3, bf16[2048,896]{1,0:T(8,128)(2,1)} %bitcast.2), custom_call_target="tpu_custom_call" | custom-call | tf_op jit(solution)/shard_map/pallas_call | solution.py:59
  18.6 2.3 %all-to-all-done.parts_ref = f32[8,8,128]{2,1,0:T(8,128)S(1)} async-done(((f32[8,8,128]{2,1,0:T(8,128)}), f32[8,8,128]{2,1,0:T(8,128)S(1)}, u32[]{:S(2)}, u32[]{:S(2)}) %all-to-all-start) | async-done | bytes 32800 | tf_op jit(solution)/shard_map/all_to_all | solution.py:217
  20.8 0.2 shard_map.69
  21.0 0.0 collective-permute-done.refs_1_
  21.0 0.1 collective-permute-start.2
  21.1 13.1 %all_to_all.20.parts_ref = f32[16,8,128]{2,1,0:T(8,128)S(1)} all-to-all(f32[16,8,128]{2,1,0:T(8,128)S(1)} %shard_map.69), channel_id=1, replica_groups={{0,16,32,48,64,80,96,112,128,144,160,176,192,208,224,240},{8,24,40,56,7..., dimensions={0} | all-to-all | bytes 131072 | tf_op jit(solution)/shard_map/all_to_all | solution.py:217
  34.2 0.0 collective-permute-done.3.refs_2_
  34.2 2.7 %collective-permute-start.5 = (bf16[128,2048]{1,0:T(8,128)(2,1)S(1)}, bf16[128,2048]{1,0:T(8,128)(2,1)S(1)}, u32[]{:S(2)}, u32[]{:S(2)}) collective-permute-start(bf16[128,2048]{1,0:T(8,128)(2,1)S(1)} %collective-permute-done.3.refs_2_), channel_id=1, source_target_pairs={{0,7},{1,0},{2,1},{3,2},{4,3},{5,4},{6,5},{7,6},{8,15},{9,8},{10,9... | collective-permute-start | bytes 1572872 | tf_op jit(solution)/shard_map/ppermute | solution.py:228
  37.0 0.0 collective-permute-done.2.refs_3_
  37.0 0.0 collective-permute-start.4
  37.0 3.9 %collective-permute-start.1 = (f32[8,128]{1,0:T(8,128)S(1)}, f32[8,128]{1,0:T(8,128)S(1)}, u32[]{:S(2)}, u32[]{:S(2)}) collective-permute-start(f32[8,128]{1,0:T(8,128)S(1)} %shard_map.70.a_ref), channel_id=1, source_target_pairs={{0,8},{8,0},{16,24},{24,16},{32,40},{40,32},{48,56},{56,48},{64,72... | collective-permute-start | bytes 12296 | tf_op jit(solution)/shard_map/ppermute | solution.py:246
  40.8 0.8 collective-permute-done.1.b_ref
  41.7 10.7 %all_to_all.21.parts_ref = f32[8,8,128]{2,1,0:T(8,128)S(1)} all-to-all(f32[8,8,128]{2,1,0:T(8,128)S(1)} %shard_map.71), channel_id=1, replica_groups=mesh['dp'=32,'mp'=8] {'mp'}, dimensions={0} | all-to-all | bytes 65536 | tf_op jit(solution)/shard_map/all_to_all | solution.py:217
  52.4 0.0 collective-permute-done.5.refs_4_
  52.4 0.5 collective-permute-start.6
  52.9 0.0 collective-permute-done.4.refs_5_
  52.9 1.0 %collective-permute-start.7 = (bf16[128,2048]{1,0:T(8,128)(2,1)S(1)}, bf16[128,2048]{1,0:T(8,128)(2,1)S(1)}, u32[]{:S(2)}, u32[]{:S(2)}) collective-permute-start(bf16[128,2048]{1,0:T(8,128)(2,1)S(1)} %collective-permute-done.4.refs_5_), channel_id=1, source_target_pairs={{0,1},{1,2},{2,3},{3,4},{4,5},{5,6},{6,7},{7,0},{8,9},{9,10},{10,1... | collective-permute-start | bytes 1572872 | tf_op jit(solution)/shard_map/ppermute | solution.py:225
  54.0 9.8 %all_to_all.22.parts_ref = f32[16,8,128]{2,1,0:T(8,128)S(1)} all-to-all(f32[16,8,128]{2,1,0:T(8,128)S(1)} %shard_map.72), channel_id=1, replica_groups={{0,16,32,48,64,80,96,112,128,144,160,176,192,208,224,240},{8,24,40,56,7..., dimensions={0} | all-to-all | bytes 131072 | tf_op jit(solution)/shard_map/all_to_all | solution.py:217
  63.7 0.3 collective-permute-done.6.refs_6_
  64.1 3.4 %shard_map.73 = (f32[8,2048]{1,0:T(8,128)S(1)}, f32[8,896]{1,0:T(8,128)S(1)}, f32[8,1024]{1,0:T(8,128)S(1)}, bf16[1024,2048]{1,0:T(8,128)(2,1)S(1)}, bf16[1024,8...) custom-call(f32[16,8,128]{2,1,0:T(8,128)S(1)} %all_to_all.22.parts_ref, bf16[2048,896]{1,0:T(8,128)(2,1)} %bitcast.3, ...), custom_call_target="tpu_custom_call" | custom-call | tf_op jit(solution)/shard_map/pallas_call | solution.py:59
  67.5 0.0 collective-permute-done.7.block_ref
  67.5 0.9 shard_map.74
  68.4 1.0 %collective-permute-start.10 = (f32[8,896]{1,0:T(8,128)S(1)}, f32[8,896]{1,0:T(8,128)S(1)}, u32[]{:S(2)}, u32[]{:S(2)}) collective-permute-start(f32[8,896]{1,0:T(8,128)S(1)} %get-tuple-element.51.own_ref), channel_id=1, source_target_pairs={{0,48},{8,56},{16,0},{24,8},{32,16},{40,24},{48,32},{56,40},{64,11... | collective-permute-start | bytes 86024 | tf_op jit(solution)/shard_map/ppermute | solution.py:286
  69.4 1.2 %collective-permute-start.8 = (f32[8,896]{1,0:T(8,128)S(1)}, f32[8,896]{1,0:T(8,128)S(1)}, u32[]{:S(2)}, u32[]{:S(2)}) collective-permute-start(f32[8,896]{1,0:T(8,128)S(1)} %get-tuple-element.51.own_ref), channel_id=1, source_target_pairs={{0,32},{8,40},{16,48},{24,56},{32,0},{40,8},{48,16},{56,24},{64,96... | collective-permute-start | bytes 86024 | tf_op jit(solution)/shard_map/ppermute | solution.py:286
  70.6 0.0 collective-permute-start.9
  70.6 1.3 %shard_map.76 = (f32[512,896]{1,0:T(8,128)S(1)}, bf16[512,48]{1,0:T(8,128)(2,1)S(1)}) custom-call(f32[8,2048]{1,0:T(8,128)S(1)} %get-tuple-element.61.p_ref, bf16[1024,2048]{1,0:T(8,128)(2,1)S(1)} %get-tuple-element.47.rows_ref, bf16[1024,896]{1,0:T(8,128)(2,1)S(1)} %get-tuple-element.43.grads_ref, bf16[2048,896]{1,0:T(8,128)(2,1)S(1)} %get-tuple-element.48.err_ref), custom_call_target="tpu_custom_call" | custom-call | tf_op jit(solution)/shard_map/pallas_call | solution.py:59
  71.9 1.3 %shard_map.75 = (f32[512,896]{1,0:T(8,128)S(1)}, bf16[512,48]{1,0:T(8,128)(2,1)S(1)}) custom-call(f32[8,2048]{1,0:T(8,128)S(1)} %get-tuple-element.61.p_ref, bf16[1024,2048]{1,0:T(8,128)(2,1)S(1)} %get-tuple-element.47.rows_ref, bf16[1024,896]{1,0:T(8,128)(2,1)S(1)} %get-tuple-element.43.grads_ref, bf16[2048,896]{1,0:T(8,128)(2,1)S(1)} %get-tuple-element.48.err_ref), custom_call_target="tpu_custom_call" | custom-call | tf_op jit(solution)/shard_map/pallas_call | solution.py:59
  73.2 0.0 collective-permute-done.10.other_ref
  73.2 0.4 collective-permute-done.8.across_ref
  73.6 0.9 collective-permute-done.9.one_ref
  74.5 1.2 %collective-permute-start.11 = (f32[8,896]{1,0:T(8,128)S(1)}, f32[8,896]{1,0:T(8,128)S(1)}, u32[]{:S(2)}, u32[]{:S(2)}) collective-permute-start(f32[8,896]{1,0:T(8,128)S(1)} %shard_map.77.own_ref), channel_id=1, source_target_pairs={{0,128},{8,136},{16,144},{24,152},{32,160},{40,168},{48,176},{56,1... | collective-permute-start | bytes 86024 | tf_op jit(solution)/shard_map/ppermute | solution.py:286
  75.7 0.3 collective-permute-start.12
  76.0 2.4 %collective-permute-start.13 = (f32[8,896]{1,0:T(8,128)S(1)}, f32[8,896]{1,0:T(8,128)S(1)}, u32[]{:S(2)}, u32[]{:S(2)}) collective-permute-start(f32[8,896]{1,0:T(8,128)S(1)} %shard_map.77.own_ref), channel_id=1, source_target_pairs={{0,192},{8,200},{16,208},{24,216},{32,224},{40,232},{48,240},{56,2... | collective-permute-start | bytes 86024 | tf_op jit(solution)/shard_map/ppermute | solution.py:286
  78.4 1.3 %shard_map.79 = (f32[512,896]{1,0:T(8,128)S(1)}, bf16[512,48]{1,0:T(8,128)(2,1)S(1)}) custom-call(f32[8,2048]{1,0:T(8,128)S(1)} %get-tuple-element.61.p_ref, bf16[1024,2048]{1,0:T(8,128)(2,1)S(1)} %get-tuple-element.47.rows_ref, bf16[1024,896]{1,0:T(8,128)(2,1)S(1)} %get-tuple-element.43.grads_ref, bf16[2048,896]{1,0:T(8,128)(2,1)S(1)} %get-tuple-element.48.err_ref), custom_call_target="tpu_custom_call" | custom-call | tf_op jit(solution)/shard_map/pallas_call | solution.py:59
  79.7 1.3 %shard_map.78 = (f32[512,896]{1,0:T(8,128)S(1)}, bf16[512,48]{1,0:T(8,128)(2,1)S(1)}) custom-call(f32[8,2048]{1,0:T(8,128)S(1)} %get-tuple-element.61.p_ref, bf16[1024,2048]{1,0:T(8,128)(2,1)S(1)} %get-tuple-element.47.rows_ref, bf16[1024,896]{1,0:T(8,128)(2,1)S(1)} %get-tuple-element.43.grads_ref, bf16[2048,896]{1,0:T(8,128)(2,1)S(1)} %get-tuple-element.48.err_ref), custom_call_target="tpu_custom_call" | custom-call | tf_op jit(solution)/shard_map/pallas_call | solution.py:59
  81.0 0.0 collective-permute-done.11.across_ref
  81.0 0.0 collective-permute-done.12.one_ref
  81.1 0.0 collective-permute-done.13.other_ref
  81.1 5.5 %collective-permute-start.14 = (f32[8,896]{1,0:T(8,128)S(1)}, f32[8,896]{1,0:T(8,128)S(1)}, u32[]{:S(2)}, u32[]{:S(2)}) collective-permute-start(f32[8,896]{1,0:T(8,128)S(1)} %shard_map.80.mine_ref), channel_id=1, source_target_pairs={{0,8},{8,0},{16,24},{24,16},{32,40},{40,32},{48,56},{56,48},{64,72... | collective-permute-start | bytes 86024 | tf_op jit(solution)/shard_map/ppermute | solution.py:288
  86.6 0.6 copy.9
  87.2 0.2 collective-permute-done.14.other_ref
  87.4 2.9 %shard_map.81 = (bf16[2048,896]{1,0:T(8,128)(2,1)}, f32[8,896]{1,0:T(8,128)}) custom-call(f32[8,896]{1,0:T(8,128)S(1)} %shard_map.80.mine_ref, f32[8,896]{1,0:T(8,128)S(1)} %collective-permute-done.14.other_ref, f32[512,896]{1,0:T(8,128)S(1)} %get-tuple-element.49.refs_0_, f32[512,896]{1,0:T(8,128)S(1)} %get-tuple-element.50.refs_1_, ...), custom_call_target="tpu_custom_call" | custom-call | tf_op jit(solution)/shard_map/pallas_call | solution.py:289
  (5 shorter events, 0.1 us)
Async XLA Ops:
  0.6 12.5 %copy-start = (bf16[128,2048]{1,0:T(8,128)(2,1)S(1)}, bf16[128,2048]{1,0:T(8,128)(2,1)}, u32[]{:S(2)}) copy-start(bf16[128,2048]{1,0:T(8,128)(2,1)} %refs_0_.1) | copy-start | bytes 1572868
  0.6 20.4 %collective-permute-start = (bf16[128,2048]{1,0:T(8,128)(2,1)}, bf16[128,2048]{1,0:T(8,128)(2,1)S(1)}, u32[]{:S(2)}, u32[]{:S(2)}) collective-permute-start(bf16[128,2048]{1,0:T(8,128)(2,1)} %refs_0_.1), channel_id=1, source_target_pairs={{0,1},{1,2},{2,3},{3,4},{4,5},{5,6},{6,7},{7,0},{8,9},{9,10},{10,1... | collective-permute-start | bytes 1572872 | tf_op jit(solution)/shard_map/ppermute | solution.py:225
  5.8 15.0 %all-to-all-start = ((f32[8,8,128]{2,1,0:T(8,128)}), f32[8,8,128]{2,1,0:T(8,128)S(1)}, u32[]{:S(2)}, u32[]{:S(2)}) async-start(f32[8,8,128]{2,1,0:T(8,128)} %shard_map.67), calls=%async_computation | async-start | bytes 65536 | tf_op jit(solution)/shard_map/all_to_all | solution.py:217
  13.1 21.1 %collective-permute-start.3 = (bf16[128,2048]{1,0:T(8,128)(2,1)S(1)}, bf16[128,2048]{1,0:T(8,128)(2,1)S(1)}, u32[]{:S(2)}, u32[]{:S(2)}) collective-permute-start(bf16[128,2048]{1,0:T(8,128)(2,1)S(1)} %copy-done), channel_id=1, source_target_pairs={{0,7},{1,0},{2,1},{3,2},{4,3},{5,4},{6,5},{7,6},{8,15},{9,8},{10,9... | collective-permute-start | bytes 1572872 | tf_op jit(solution)/shard_map/ppermute | solution.py:228
  21.0 15.9 %collective-permute-start.2 = (bf16[128,2048]{1,0:T(8,128)(2,1)S(1)}, bf16[128,2048]{1,0:T(8,128)(2,1)S(1)}, u32[]{:S(2)}, u32[]{:S(2)}) collective-permute-start(bf16[128,2048]{1,0:T(8,128)(2,1)S(1)} %collective-permute-done.refs_1_), channel_id=1, source_target_pairs={{0,1},{1,2},{2,3},{3,4},{4,5},{5,6},{6,7},{7,0},{8,9},{9,10},{10,1... | collective-permute-start | bytes 1572872 | tf_op jit(solution)/shard_map/ppermute | solution.py:225
  34.2 18.2 %collective-permute-start.5 = (bf16[128,2048]{1,0:T(8,128)(2,1)S(1)}, bf16[128,2048]{1,0:T(8,128)(2,1)S(1)}, u32[]{:S(2)}, u32[]{:S(2)}) collective-permute-start(bf16[128,2048]{1,0:T(8,128)(2,1)S(1)} %collective-permute-done.3.refs_2_), channel_id=1, source_target_pairs={{0,7},{1,0},{2,1},{3,2},{4,3},{5,4},{6,5},{7,6},{8,15},{9,8},{10,9... | collective-permute-start | bytes 1572872 | tf_op jit(solution)/shard_map/ppermute | solution.py:228
  37.0 16.0 %collective-permute-start.4 = (bf16[128,2048]{1,0:T(8,128)(2,1)S(1)}, bf16[128,2048]{1,0:T(8,128)(2,1)S(1)}, u32[]{:S(2)}, u32[]{:S(2)}) collective-permute-start(bf16[128,2048]{1,0:T(8,128)(2,1)S(1)} %collective-permute-done.2.refs_3_), channel_id=1, source_target_pairs={{0,1},{1,2},{2,3},{3,4},{4,5},{5,6},{6,7},{7,0},{8,9},{9,10},{10,1... | collective-permute-start | bytes 1572872 | tf_op jit(solution)/shard_map/ppermute | solution.py:225
  37.0 4.7 %collective-permute-start.1 = (f32[8,128]{1,0:T(8,128)S(1)}, f32[8,128]{1,0:T(8,128)S(1)}, u32[]{:S(2)}, u32[]{:S(2)}) collective-permute-start(f32[8,128]{1,0:T(8,128)S(1)} %shard_map.70.a_ref), channel_id=1, source_target_pairs={{0,8},{8,0},{16,24},{24,16},{32,40},{40,32},{48,56},{56,48},{64,72... | collective-permute-start | bytes 12296 | tf_op jit(solution)/shard_map/ppermute | solution.py:246
  52.4 11.6 %collective-permute-start.6 = (bf16[128,2048]{1,0:T(8,128)(2,1)S(1)}, bf16[128,2048]{1,0:T(8,128)(2,1)S(1)}, u32[]{:S(2)}, u32[]{:S(2)}) collective-permute-start(bf16[128,2048]{1,0:T(8,128)(2,1)S(1)} %collective-permute-done.5.refs_4_), channel_id=1, source_target_pairs={{0,7},{1,0},{2,1},{3,2},{4,3},{5,4},{6,5},{7,6},{8,15},{9,8},{10,9... | collective-permute-start | bytes 1572872 | tf_op jit(solution)/shard_map/ppermute | solution.py:228
  52.9 14.5 %collective-permute-start.7 = (bf16[128,2048]{1,0:T(8,128)(2,1)S(1)}, bf16[128,2048]{1,0:T(8,128)(2,1)S(1)}, u32[]{:S(2)}, u32[]{:S(2)}) collective-permute-start(bf16[128,2048]{1,0:T(8,128)(2,1)S(1)} %collective-permute-done.4.refs_5_), channel_id=1, source_target_pairs={{0,1},{1,2},{2,3},{3,4},{4,5},{5,6},{6,7},{7,0},{8,9},{9,10},{10,1... | collective-permute-start | bytes 1572872 | tf_op jit(solution)/shard_map/ppermute | solution.py:225
  68.4 4.8 %collective-permute-start.10 = (f32[8,896]{1,0:T(8,128)S(1)}, f32[8,896]{1,0:T(8,128)S(1)}, u32[]{:S(2)}, u32[]{:S(2)}) collective-permute-start(f32[8,896]{1,0:T(8,128)S(1)} %get-tuple-element.51.own_ref), channel_id=1, source_target_pairs={{0,48},{8,56},{16,0},{24,8},{32,16},{40,24},{48,32},{56,40},{64,11... | collective-permute-start | bytes 86024 | tf_op jit(solution)/shard_map/ppermute | solution.py:286
  69.4 4.2 %collective-permute-start.8 = (f32[8,896]{1,0:T(8,128)S(1)}, f32[8,896]{1,0:T(8,128)S(1)}, u32[]{:S(2)}, u32[]{:S(2)}) collective-permute-start(f32[8,896]{1,0:T(8,128)S(1)} %get-tuple-element.51.own_ref), channel_id=1, source_target_pairs={{0,32},{8,40},{16,48},{24,56},{32,0},{40,8},{48,16},{56,24},{64,96... | collective-permute-start | bytes 86024 | tf_op jit(solution)/shard_map/ppermute | solution.py:286
  70.6 3.9 %collective-permute-start.9 = (f32[8,896]{1,0:T(8,128)S(1)}, f32[8,896]{1,0:T(8,128)S(1)}, u32[]{:S(2)}, u32[]{:S(2)}) collective-permute-start(f32[8,896]{1,0:T(8,128)S(1)} %get-tuple-element.51.own_ref), channel_id=1, source_target_pairs={{0,16},{8,24},{16,32},{24,40},{32,48},{40,56},{48,0},{56,8},{64,80... | collective-permute-start | bytes 86024 | tf_op jit(solution)/shard_map/ppermute | solution.py:286
  74.5 6.5 %collective-permute-start.11 = (f32[8,896]{1,0:T(8,128)S(1)}, f32[8,896]{1,0:T(8,128)S(1)}, u32[]{:S(2)}, u32[]{:S(2)}) collective-permute-start(f32[8,896]{1,0:T(8,128)S(1)} %shard_map.77.own_ref), channel_id=1, source_target_pairs={{0,128},{8,136},{16,144},{24,152},{32,160},{40,168},{48,176},{56,1... | collective-permute-start | bytes 86024 | tf_op jit(solution)/shard_map/ppermute | solution.py:286
  75.7 5.3 %collective-permute-start.12 = (f32[8,896]{1,0:T(8,128)S(1)}, f32[8,896]{1,0:T(8,128)S(1)}, u32[]{:S(2)}, u32[]{:S(2)}) collective-permute-start(f32[8,896]{1,0:T(8,128)S(1)} %shard_map.77.own_ref), channel_id=1, source_target_pairs={{0,64},{8,72},{16,80},{24,88},{32,96},{40,104},{48,112},{56,120},{... | collective-permute-start | bytes 86024 | tf_op jit(solution)/shard_map/ppermute | solution.py:286
  76.0 5.0 %collective-permute-start.13 = (f32[8,896]{1,0:T(8,128)S(1)}, f32[8,896]{1,0:T(8,128)S(1)}, u32[]{:S(2)}, u32[]{:S(2)}) collective-permute-start(f32[8,896]{1,0:T(8,128)S(1)} %shard_map.77.own_ref), channel_id=1, source_target_pairs={{0,192},{8,200},{16,208},{24,216},{32,224},{40,232},{48,240},{56,2... | collective-permute-start | bytes 86024 | tf_op jit(solution)/shard_map/ppermute | solution.py:286
  81.1 6.3 %collective-permute-start.14 = (f32[8,896]{1,0:T(8,128)S(1)}, f32[8,896]{1,0:T(8,128)S(1)}, u32[]{:S(2)}, u32[]{:S(2)}) collective-permute-start(f32[8,896]{1,0:T(8,128)S(1)} %shard_map.80.mine_ref), channel_id=1, source_target_pairs={{0,8},{8,0},{16,24},{24,16},{32,40},{40,32},{48,56},{56,48},{64,72... | collective-permute-start | bytes 86024 | tf_op jit(solution)/shard_map/ppermute | solution.py:288

commit v6 on v5

--- a/solution.py
+++ b/solution.py
@@ -11,7 +11,8 @@
 DP = 32
 R = 8
 TOKENS = 1024
-CHUNK = 512
+CHUNK = 1024
+PIECE = 512
 F32 = jnp.float32
 BF16 = jnp.bfloat16
 VMEM = pltpu.MemorySpace.VMEM
@@ -198,16 +199,17 @@
 
 
 def residue_kernel(mine_ref, other_ref, *refs):
-    merged, lefts, (out_ref, q_ref, held, sems) = refs[:4], refs[4:8], refs[8:]
+    merged, lefts, (out_ref, q_ref, held, sems) = refs[:2], refs[2:4], refs[4:]
     q = (mine_ref[...] + other_ref[...]) / DP
     q_ref[...] = q
     a, b, c = terms(q)
     right = jnp.concatenate([a, b, c, a, b, a], axis=0).astype(BF16)
     copies = []
-    for i, (part, left) in enumerate(zip(merged, lefts)):
-        at = pl.ds(i * CHUNK, CHUNK)
-        held[i] = (part[...] - dot(left[...], right, 1, 0)).astype(BF16)
-        copies.append(pltpu.make_async_copy(held.at[i], out_ref.at[at], sems.at[i]))
+    for i in range(held.shape[0]):
+        part, left = merged[i * PIECE // CHUNK], lefts[i * PIECE // CHUNK]
+        inside = pl.ds(i * PIECE % CHUNK, PIECE)
+        held[i] = (part[inside] - dot(left[inside], right, 1, 0)).astype(BF16)
+        copies.append(pltpu.make_async_copy(held.at[i], out_ref.at[pl.ds(i * PIECE, PIECE)], sems.at[i]))
         copies[-1].start()
     for copy in copies:
         copy.wait()
@@ -281,8 +283,8 @@
     )
     rows = kept(rows)
     out = (pltpu.VMEM((CHUNK, columns), F32), pltpu.VMEM((CHUNK, 6 * R), BF16))
-    merged, lefts = zip(*[local(functools.partial(merged_kernel, i), out, p, rows, grads, near) for i in range(depth // CHUNK)])
-    for base, beside in ((2, merged[:2]), (8, merged[2:])):
+    merged, lefts = zip(*[local(functools.partial(merged_kernel, i), out, p, rows, grads, near, mib=20) for i in range(depth // CHUNK)])
+    for base, beside in ((2, merged[:1]), (8, merged[1:])):
         one, other, across = (lax.ppermute(mine, "dp", along(base, 4, step)) for step in (1, 3, 2))
         mine = local(add4_kernel, shape(R, columns), after(mine, *beside), across, one, other)
     other = lax.ppermute(mine, "dp", CORES)
@@ -291,7 +293,7 @@
         out_shape=(shape(depth, columns, dtype=BF16), shape(R, columns)),
         in_specs=[pl.BlockSpec(memory_space=VMEM)] * (2 + 2 * len(merged)),
         out_specs=(pl.BlockSpec(memory_space=hbm), pl.BlockSpec(memory_space=VMEM)),
-        scratch_shapes=[pltpu.VMEM((len(merged), CHUNK, columns), BF16), dma((len(merged),))],
+        scratch_shapes=[pltpu.VMEM((depth // PIECE, PIECE, columns), BF16), dma((depth // PIECE,))],
         compiler_params=pltpu.CompilerParams(vmem_limit_bytes=12 << 20),
     )(mine, other, *[kept(part) for part in merged + lefts])
     return (p_factor, q_factor, new_error[None])

time: 90.8 us -> 90.5 us (level)
    pallas_call x14 -> x12, Pallas kernels: 15.2 us -> 14.7 us  [local(): pl.pallas_call(kernel, out_shape=out, in_specs=[pl.BlockSpec(memory_space...]
  transfers between devices with their start and end apart: 16 -> 16, of which waited for: 6 -> 6; matrix products, arithmetic and copies ran while one was open for 1% -> 1% of each run, Pallas kernels for 16% -> 15%
where the time goes in v6:
time: 90.5 us; the launch traced here: 90.2 us
  blocking collectives  33.6 us (37%)
  starting transfers between devices  32 us (35%)
  Pallas kernels  17.6 us (19%)
  waiting for transfers between devices  5.5 us (6%)
  between operations  0.95 us (1%)
    all_to_all x3, blocking collectives, exchange(): return lax.all_to_all(x, axis, 0, 0, axis_index_groups=groups)  33.6 us
    pallas_call x12, Pallas kernels, local(): pl.pallas_call(kernel, out_shape=out, in_specs=[pl.BlockSpec(memory_space...  14.7 us
    all_to_all x1, starting transfers between devices, exchange(): return lax.all_to_all(x, axis, 0, 0, axis_index_groups=groups)  7.3 us
    ppermute x6, starting transfers between devices, on_device(): lax.ppermute(mine, 'dp', along(base, 4, step))  5.81 us
    ppermute x3, starting transfers between devices, leftward(): return lax.ppermute(x, 'mp', shift(MP, -1))  5.76 us
    ppermute x1, starting transfers between devices, on_device(): other = lax.ppermute(mine, 'dp', CORES)  5.44 us
    ppermute x1, starting transfers between devices, on_device(): lax.ppermute(part, 'dp', CORES)  3.87 us
    ppermute x4, starting transfers between devices, rightward(): return lax.ppermute(x, 'mp', shift(MP, 1))  3.81 us
  transfers between devices with their start and end apart: 16, of which 6 were waited for; matrix products, arithmetic and copies ran while one was open for 1% of the time, Pallas kernels for 15%

profile of v6, /device:TPU:1, one launch (start us, length us, event | category | flops | bytes accessed | tf_op | source)
XLA Modules:
  0.0 90.2 jit_solution(10873285048834592311)
XLA Ops:
  0.6 0.0 copy-start
  0.6 2.5 %collective-permute-start = (bf16[128,2048]{1,0:T(8,128)(2,1)}, bf16[128,2048]{1,0:T(8,128)(2,1)S(1)}, u32[]{:S(2)}, u32[]{:S(2)}) collective-permute-start(bf16[128,2048]{1,0:T(8,128)(2,1)} %refs_0_.1), channel_id=1, source_target_pairs={{0,1},{1,2},{2,3},{3,4},{4,5},{5,6},{6,7},{7,0},{8,9},{9,10},{10,1... | collective-permute-start | bytes 1572872 | tf_op jit(solution)/shard_map/ppermute | solution.py:227
  3.2 2.6 %shard_map.67 = f32[8,8,128]{2,1,0:T(8,128)} custom-call(f32[8,896]{1,0:T(8,128)} %q_ref.3, bf16[1024,896]{1,0:T(8,128)(2,1)} %g_ref.3), custom_call_target="tpu_custom_call" | custom-call | tf_op jit(solution)/shard_map/pallas_call | solution.py:60
  5.8 7.3 %all-to-all-start = ((f32[8,8,128]{2,1,0:T(8,128)}), f32[8,8,128]{2,1,0:T(8,128)S(1)}, u32[]{:S(2)}, u32[]{:S(2)}) async-start(f32[8,8,128]{2,1,0:T(8,128)} %shard_map.67), calls=%async_computation | async-start | bytes 65536 | tf_op jit(solution)/shard_map/all_to_all | solution.py:219
  13.1 2.7 %collective-permute-start.3 = (bf16[128,2048]{1,0:T(8,128)(2,1)}, bf16[128,2048]{1,0:T(8,128)(2,1)S(1)}, u32[]{:S(2)}, u32[]{:S(2)}) collective-permute-start(bf16[128,2048]{1,0:T(8,128)(2,1)} %refs_0_.1), channel_id=1, source_target_pairs={{0,7},{1,0},{2,1},{3,2},{4,3},{5,4},{6,5},{7,6},{8,15},{9,8},{10,9... | collective-permute-start | bytes 1572872 | tf_op jit(solution)/shard_map/ppermute | solution.py:230
  15.8 2.8 %shard_map.68.more_ref = f32[8,2048]{1,0:T(8,128)S(1)} custom-call(f32[8,896]{1,0:T(8,128)} %q_ref.3, bf16[2048,896]{1,0:T(8,128)(2,1)} %bitcast.2), custom_call_target="tpu_custom_call" | custom-call | tf_op jit(solution)/shard_map/pallas_call | solution.py:60
  18.6 2.3 %all-to-all-done.parts_ref = f32[8,8,128]{2,1,0:T(8,128)S(1)} async-done(((f32[8,8,128]{2,1,0:T(8,128)}), f32[8,8,128]{2,1,0:T(8,128)S(1)}, u32[]{:S(2)}, u32[]{:S(2)}) %all-to-all-start) | async-done | bytes 32800 | tf_op jit(solution)/shard_map/all_to_all | solution.py:219
  20.8 0.0 copy-done
  20.8 0.2 shard_map.69
  21.0 0.0 collective-permute-done.refs_1_
  21.1 0.1 collective-permute-start.2
  21.1 13.1 %all_to_all.20.parts_ref = f32[16,8,128]{2,1,0:T(8,128)S(1)} all-to-all(f32[16,8,128]{2,1,0:T(8,128)S(1)} %shard_map.69), channel_id=1, replica_groups={{0,16,32,48,64,80,96,112,128,144,160,176,192,208,224,240},{8,24,40,56,7..., dimensions={0} | all-to-all | bytes 131072 | tf_op jit(solution)/shard_map/all_to_all | solution.py:219
  34.2 0.0 collective-permute-done.3.refs_2_
  34.2 2.7 %collective-permute-start.5 = (bf16[128,2048]{1,0:T(8,128)(2,1)S(1)}, bf16[128,2048]{1,0:T(8,128)(2,1)S(1)}, u32[]{:S(2)}, u32[]{:S(2)}) collective-permute-start(bf16[128,2048]{1,0:T(8,128)(2,1)S(1)} %collective-permute-done.3.refs_2_), channel_id=1, source_target_pairs={{0,7},{1,0},{2,1},{3,2},{4,3},{5,4},{6,5},{7,6},{8,15},{9,8},{10,9... | collective-permute-start | bytes 1572872 | tf_op jit(solution)/shard_map/ppermute | solution.py:230
  37.0 0.0 collective-permute-done.2.refs_3_
  37.0 0.0 collective-permute-start.4
  37.0 3.9 %collective-permute-start.1 = (f32[8,128]{1,0:T(8,128)S(1)}, f32[8,128]{1,0:T(8,128)S(1)}, u32[]{:S(2)}, u32[]{:S(2)}) collective-permute-start(f32[8,128]{1,0:T(8,128)S(1)} %shard_map.70.a_ref), channel_id=1, source_target_pairs={{0,8},{8,0},{16,24},{24,16},{32,40},{40,32},{48,56},{56,48},{64,72... | collective-permute-start | bytes 12296 | tf_op jit(solution)/shard_map/ppermute | solution.py:248
  40.8 0.8 collective-permute-done.1.b_ref
  41.7 10.9 %all_to_all.21.parts_ref = f32[8,8,128]{2,1,0:T(8,128)S(1)} all-to-all(f32[8,8,128]{2,1,0:T(8,128)S(1)} %shard_map.71), channel_id=1, replica_groups=mesh['dp'=32,'mp'=8] {'mp'}, dimensions={0} | all-to-all | bytes 65536 | tf_op jit(solution)/shard_map/all_to_all | solution.py:219
  52.6 0.0 collective-permute-done.5.refs_4_
  52.6 0.4 collective-permute-start.6
  52.9 0.0 collective-permute-done.4.refs_5_
  52.9 1.2 %collective-permute-start.7 = (bf16[128,2048]{1,0:T(8,128)(2,1)S(1)}, bf16[128,2048]{1,0:T(8,128)(2,1)S(1)}, u32[]{:S(2)}, u32[]{:S(2)}) collective-permute-start(bf16[128,2048]{1,0:T(8,128)(2,1)S(1)} %collective-permute-done.4.refs_5_), channel_id=1, source_target_pairs={{0,1},{1,2},{2,3},{3,4},{4,5},{5,6},{6,7},{7,0},{8,9},{9,10},{10,1... | collective-permute-start | bytes 1572872 | tf_op jit(solution)/shard_map/ppermute | solution.py:227
  54.1 9.6 %all_to_all.22.parts_ref = f32[16,8,128]{2,1,0:T(8,128)S(1)} all-to-all(f32[16,8,128]{2,1,0:T(8,128)S(1)} %shard_map.72), channel_id=1, replica_groups={{0,16,32,48,64,80,96,112,128,144,160,176,192,208,224,240},{8,24,40,56,7..., dimensions={0} | all-to-all | bytes 131072 | tf_op jit(solution)/shard_map/all_to_all | solution.py:219
  63.7 0.6 collective-permute-done.6.refs_6_
  64.4 3.4 %shard_map.73 = (f32[8,2048]{1,0:T(8,128)S(1)}, f32[8,896]{1,0:T(8,128)S(1)}, f32[8,1024]{1,0:T(8,128)S(1)}, bf16[1024,2048]{1,0:T(8,128)(2,1)S(1)}, bf16[1024,8...) custom-call(f32[16,8,128]{2,1,0:T(8,128)S(1)} %all_to_all.22.parts_ref, bf16[2048,896]{1,0:T(8,128)(2,1)} %bitcast.3, ...), custom_call_target="tpu_custom_call" | custom-call | tf_op jit(solution)/shard_map/pallas_call | solution.py:60
  67.8 0.0 collective-permute-done.7.block_ref
  67.8 0.9 shard_map.74
  68.7 1.0 %collective-permute-start.10 = (f32[8,896]{1,0:T(8,128)S(1)}, f32[8,896]{1,0:T(8,128)S(1)}, u32[]{:S(2)}, u32[]{:S(2)}) collective-permute-start(f32[8,896]{1,0:T(8,128)S(1)} %get-tuple-element.46.own_ref), channel_id=1, source_target_pairs={{0,48},{8,56},{16,0},{24,8},{32,16},{40,24},{48,32},{56,40},{64,11... | collective-permute-start | bytes 86024 | tf_op jit(solution)/shard_map/ppermute | solution.py:288
  69.7 1.2 %collective-permute-start.8 = (f32[8,896]{1,0:T(8,128)S(1)}, f32[8,896]{1,0:T(8,128)S(1)}, u32[]{:S(2)}, u32[]{:S(2)}) collective-permute-start(f32[8,896]{1,0:T(8,128)S(1)} %get-tuple-element.46.own_ref), channel_id=1, source_target_pairs={{0,32},{8,40},{16,48},{24,56},{32,0},{40,8},{48,16},{56,24},{64,96... | collective-permute-start | bytes 86024 | tf_op jit(solution)/shard_map/ppermute | solution.py:288
  70.9 0.0 collective-permute-start.9
  70.9 2.4 %shard_map.75 = (f32[1024,896]{1,0:T(8,128)S(1)}, bf16[1024,48]{1,0:T(8,128)(2,1)S(1)}) custom-call(f32[8,2048]{1,0:T(8,128)S(1)} %get-tuple-element.53.p_ref, bf16[1024,2048]{1,0:T(8,128)(2,1)S(1)} %get-tuple-element.43.rows_ref, bf16[1024,896]{1,0:T(8,128)(2,1)S(1)} %get-tuple-element.39.grads_ref, bf16[2048,896]{1,0:T(8,128)(2,1)S(1)} %get-tuple-element.44.err_ref), custom_call_target="tpu_custom_call" | custom-call | tf_op jit(solution)/shard_map/pallas_call | solution.py:60
  73.2 0.0 collective-permute-done.10.other_ref
  73.3 0.6 collective-permute-done.8.across_ref
  73.9 0.9 collective-permute-done.9.one_ref
  74.8 1.0 %collective-permute-start.11 = (f32[8,896]{1,0:T(8,128)S(1)}, f32[8,896]{1,0:T(8,128)S(1)}, u32[]{:S(2)}, u32[]{:S(2)}) collective-permute-start(f32[8,896]{1,0:T(8,128)S(1)} %shard_map.76.own_ref), channel_id=1, source_target_pairs={{0,128},{8,136},{16,144},{24,152},{32,160},{40,168},{48,176},{56,1... | collective-permute-start | bytes 86024 | tf_op jit(solution)/shard_map/ppermute | solution.py:288
  75.8 0.5 collective-permute-start.12
  76.3 2.1 %collective-permute-start.13 = (f32[8,896]{1,0:T(8,128)S(1)}, f32[8,896]{1,0:T(8,128)S(1)}, u32[]{:S(2)}, u32[]{:S(2)}) collective-permute-start(f32[8,896]{1,0:T(8,128)S(1)} %shard_map.76.own_ref), channel_id=1, source_target_pairs={{0,192},{8,200},{16,208},{24,216},{32,224},{40,232},{48,240},{56,2... | collective-permute-start | bytes 86024 | tf_op jit(solution)/shard_map/ppermute | solution.py:288
  78.5 2.4 %shard_map.77 = (f32[1024,896]{1,0:T(8,128)S(1)}, bf16[1024,48]{1,0:T(8,128)(2,1)S(1)}) custom-call(f32[8,2048]{1,0:T(8,128)S(1)} %get-tuple-element.53.p_ref, bf16[1024,2048]{1,0:T(8,128)(2,1)S(1)} %get-tuple-element.43.rows_ref, bf16[1024,896]{1,0:T(8,128)(2,1)S(1)} %get-tuple-element.39.grads_ref, bf16[2048,896]{1,0:T(8,128)(2,1)S(1)} %get-tuple-element.44.err_ref), custom_call_target="tpu_custom_call" | custom-call | tf_op jit(solution)/shard_map/pallas_call | solution.py:60
  80.8 0.0 collective-permute-done.11.across_ref
  80.9 0.0 collective-permute-done.12.one_ref
  80.9 0.0 collective-permute-done.13.other_ref
  80.9 5.4 %collective-permute-start.14 = (f32[8,896]{1,0:T(8,128)S(1)}, f32[8,896]{1,0:T(8,128)S(1)}, u32[]{:S(2)}, u32[]{:S(2)}) collective-permute-start(f32[8,896]{1,0:T(8,128)S(1)} %shard_map.78.mine_ref), channel_id=1, source_target_pairs={{0,8},{8,0},{16,24},{24,16},{32,40},{40,32},{48,56},{56,48},{64,72... | collective-permute-start | bytes 86024 | tf_op jit(solution)/shard_map/ppermute | solution.py:290
  86.3 0.6 copy.9
  87.0 0.2 collective-permute-done.14.other_ref
  87.2 2.9 %shard_map.79 = (bf16[2048,896]{1,0:T(8,128)(2,1)}, f32[8,896]{1,0:T(8,128)}) custom-call(f32[8,896]{1,0:T(8,128)S(1)} %shard_map.78.mine_ref, f32[8,896]{1,0:T(8,128)S(1)} %collective-permute-done.14.other_ref, f32[1024,896]{1,0:T(8,128)S(1)} %get-tuple-element.45.refs_0_, f32[1024,896]{1,0:T(8,128)S(1)} %get-tuple-element.47.refs_1_, ...), custom_call_target="tpu_custom_call" | custom-call | tf_op jit(solution)/shard_map/pallas_call | solution.py:291
  (5 shorter events, 0.1 us)
Async XLA Ops:
  0.6 20.2 %copy-start = (bf16[128,2048]{1,0:T(8,128)(2,1)S(1)}, bf16[128,2048]{1,0:T(8,128)(2,1)}, u32[]{:S(2)}) copy-start(bf16[128,2048]{1,0:T(8,128)(2,1)} %refs_0_.1) | copy-start | bytes 1572868
  0.6 20.4 %collective-permute-start = (bf16[128,2048]{1,0:T(8,128)(2,1)}, bf16[128,2048]{1,0:T(8,128)(2,1)S(1)}, u32[]{:S(2)}, u32[]{:S(2)}) collective-permute-start(bf16[128,2048]{1,0:T(8,128)(2,1)} %refs_0_.1), channel_id=1, source_target_pairs={{0,1},{1,2},{2,3},{3,4},{4,5},{5,6},{6,7},{7,0},{8,9},{9,10},{10,1... | collective-permute-start | bytes 1572872 | tf_op jit(solution)/shard_map/ppermute | solution.py:227
  5.8 15.0 %all-to-all-start = ((f32[8,8,128]{2,1,0:T(8,128)}), f32[8,8,128]{2,1,0:T(8,128)S(1)}, u32[]{:S(2)}, u32[]{:S(2)}) async-start(f32[8,8,128]{2,1,0:T(8,128)} %shard_map.67), calls=%async_computation | async-start | bytes 65536 | tf_op jit(solution)/shard_map/all_to_all | solution.py:219
  13.1 21.1 %collective-permute-start.3 = (bf16[128,2048]{1,0:T(8,128)(2,1)}, bf16[128,2048]{1,0:T(8,128)(2,1)S(1)}, u32[]{:S(2)}, u32[]{:S(2)}) collective-permute-start(bf16[128,2048]{1,0:T(8,128)(2,1)} %refs_0_.1), channel_id=1, source_target_pairs={{0,7},{1,0},{2,1},{3,2},{4,3},{5,4},{6,5},{7,6},{8,15},{9,8},{10,9... | collective-permute-start | bytes 1572872 | tf_op jit(solution)/shard_map/ppermute | solution.py:230
  21.1 15.9 %collective-permute-start.2 = (bf16[128,2048]{1,0:T(8,128)(2,1)S(1)}, bf16[128,2048]{1,0:T(8,128)(2,1)S(1)}, u32[]{:S(2)}, u32[]{:S(2)}) collective-permute-start(bf16[128,2048]{1,0:T(8,128)(2,1)S(1)} %collective-permute-done.refs_1_), channel_id=1, source_target_pairs={{0,1},{1,2},{2,3},{3,4},{4,5},{5,6},{6,7},{7,0},{8,9},{9,10},{10,1... | collective-permute-start | bytes 1572872 | tf_op jit(solution)/shard_map/ppermute | solution.py:227
  34.2 18.3 %collective-permute-start.5 = (bf16[128,2048]{1,0:T(8,128)(2,1)S(1)}, bf16[128,2048]{1,0:T(8,128)(2,1)S(1)}, u32[]{:S(2)}, u32[]{:S(2)}) collective-permute-start(bf16[128,2048]{1,0:T(8,128)(2,1)S(1)} %collective-permute-done.3.refs_2_), channel_id=1, source_target_pairs={{0,7},{1,0},{2,1},{3,2},{4,3},{5,4},{6,5},{7,6},{8,15},{9,8},{10,9... | collective-permute-start | bytes 1572872 | tf_op jit(solution)/shard_map/ppermute | solution.py:230
  37.0 16.0 %collective-permute-start.4 = (bf16[128,2048]{1,0:T(8,128)(2,1)S(1)}, bf16[128,2048]{1,0:T(8,128)(2,1)S(1)}, u32[]{:S(2)}, u32[]{:S(2)}) collective-permute-start(bf16[128,2048]{1,0:T(8,128)(2,1)S(1)} %collective-permute-done.2.refs_3_), channel_id=1, source_target_pairs={{0,1},{1,2},{2,3},{3,4},{4,5},{5,6},{6,7},{7,0},{8,9},{9,10},{10,1... | collective-permute-start | bytes 1572872 | tf_op jit(solution)/shard_map/ppermute | solution.py:227
  37.0 4.7 %collective-permute-start.1 = (f32[8,128]{1,0:T(8,128)S(1)}, f32[8,128]{1,0:T(8,128)S(1)}, u32[]{:S(2)}, u32[]{:S(2)}) collective-permute-start(f32[8,128]{1,0:T(8,128)S(1)} %shard_map.70.a_ref), channel_id=1, source_target_pairs={{0,8},{8,0},{16,24},{24,16},{32,40},{40,32},{48,56},{56,48},{64,72... | collective-permute-start | bytes 12296 | tf_op jit(solution)/shard_map/ppermute | solution.py:248
  52.6 11.8 %collective-permute-start.6 = (bf16[128,2048]{1,0:T(8,128)(2,1)S(1)}, bf16[128,2048]{1,0:T(8,128)(2,1)S(1)}, u32[]{:S(2)}, u32[]{:S(2)}) collective-permute-start(bf16[128,2048]{1,0:T(8,128)(2,1)S(1)} %collective-permute-done.5.refs_4_), channel_id=1, source_target_pairs={{0,7},{1,0},{2,1},{3,2},{4,3},{5,4},{6,5},{7,6},{8,15},{9,8},{10,9... | collective-permute-start | bytes 1572872 | tf_op jit(solution)/shard_map/ppermute | solution.py:230
  52.9 14.8 %collective-permute-start.7 = (bf16[128,2048]{1,0:T(8,128)(2,1)S(1)}, bf16[128,2048]{1,0:T(8,128)(2,1)S(1)}, u32[]{:S(2)}, u32[]{:S(2)}) collective-permute-start(bf16[128,2048]{1,0:T(8,128)(2,1)S(1)} %collective-permute-done.4.refs_5_), channel_id=1, source_target_pairs={{0,1},{1,2},{2,3},{3,4},{4,5},{5,6},{6,7},{7,0},{8,9},{9,10},{10,1... | collective-permute-start | bytes 1572872 | tf_op jit(solution)/shard_map/ppermute | solution.py:227
  68.7 4.5 %collective-permute-start.10 = (f32[8,896]{1,0:T(8,128)S(1)}, f32[8,896]{1,0:T(8,128)S(1)}, u32[]{:S(2)}, u32[]{:S(2)}) collective-permute-start(f32[8,896]{1,0:T(8,128)S(1)} %get-tuple-element.46.own_ref), channel_id=1, source_target_pairs={{0,48},{8,56},{16,0},{24,8},{32,16},{40,24},{48,32},{56,40},{64,11... | collective-permute-start | bytes 86024 | tf_op jit(solution)/shard_map/ppermute | solution.py:288
  69.7 4.2 %collective-permute-start.8 = (f32[8,896]{1,0:T(8,128)S(1)}, f32[8,896]{1,0:T(8,128)S(1)}, u32[]{:S(2)}, u32[]{:S(2)}) collective-permute-start(f32[8,896]{1,0:T(8,128)S(1)} %get-tuple-element.46.own_ref), channel_id=1, source_target_pairs={{0,32},{8,40},{16,48},{24,56},{32,0},{40,8},{48,16},{56,24},{64,96... | collective-permute-start | bytes 86024 | tf_op jit(solution)/shard_map/ppermute | solution.py:288
  70.9 3.9 %collective-permute-start.9 = (f32[8,896]{1,0:T(8,128)S(1)}, f32[8,896]{1,0:T(8,128)S(1)}, u32[]{:S(2)}, u32[]{:S(2)}) collective-permute-start(f32[8,896]{1,0:T(8,128)S(1)} %get-tuple-element.46.own_ref), channel_id=1, source_target_pairs={{0,16},{8,24},{16,32},{24,40},{32,48},{40,56},{48,0},{56,8},{64,80... | collective-permute-start | bytes 86024 | tf_op jit(solution)/shard_map/ppermute | solution.py:288
  74.8 6.0 %collective-permute-start.11 = (f32[8,896]{1,0:T(8,128)S(1)}, f32[8,896]{1,0:T(8,128)S(1)}, u32[]{:S(2)}, u32[]{:S(2)}) collective-permute-start(f32[8,896]{1,0:T(8,128)S(1)} %shard_map.76.own_ref), channel_id=1, source_target_pairs={{0,128},{8,136},{16,144},{24,152},{32,160},{40,168},{48,176},{56,1... | collective-permute-start | bytes 86024 | tf_op jit(solution)/shard_map/ppermute | solution.py:288
  75.8 5.1 %collective-permute-start.12 = (f32[8,896]{1,0:T(8,128)S(1)}, f32[8,896]{1,0:T(8,128)S(1)}, u32[]{:S(2)}, u32[]{:S(2)}) collective-permute-start(f32[8,896]{1,0:T(8,128)S(1)} %shard_map.76.own_ref), channel_id=1, source_target_pairs={{0,64},{8,72},{16,80},{24,88},{32,96},{40,104},{48,112},{56,120},{... | collective-permute-start | bytes 86024 | tf_op jit(solution)/shard_map/ppermute | solution.py:288
  76.3 4.6 %collective-permute-start.13 = (f32[8,896]{1,0:T(8,128)S(1)}, f32[8,896]{1,0:T(8,128)S(1)}, u32[]{:S(2)}, u32[]{:S(2)}) collective-permute-start(f32[8,896]{1,0:T(8,128)S(1)} %shard_map.76.own_ref), channel_id=1, source_target_pairs={{0,192},{8,200},{16,208},{24,216},{32,224},{40,232},{48,240},{56,2... | collective-permute-start | bytes 86024 | tf_op jit(solution)/shard_map/ppermute | solution.py:288
  80.9 6.3 %collective-permute-start.14 = (f32[8,896]{1,0:T(8,128)S(1)}, f32[8,896]{1,0:T(8,128)S(1)}, u32[]{:S(2)}, u32[]{:S(2)}) collective-permute-start(f32[8,896]{1,0:T(8,128)S(1)} %shard_map.78.mine_ref), channel_id=1, source_target_pairs={{0,8},{8,0},{16,24},{24,16},{32,40},{40,32},{48,56},{56,48},{64,72... | collective-permute-start | bytes 86024 | tf_op jit(solution)/shard_map/ppermute | solution.py:290

commit v7 on v5

--- a/solution.py
+++ b/solution.py
@@ -167,12 +167,12 @@
     p = gram_schmidt(jnp.concatenate([parts_ref[i] for i in range(parts_ref.shape[0])], axis=1))
     p_ref[...] = p
     left = split3(p)
-    for copy in copies[:7]:
-        copy.wait()
-    projected_ref[...] = fold3(dot(left, rows_ref[...], 1, 1))
+    for block, start in zip(blocks, starts_of()):
+        projected_ref[:, pl.ds(start, 128)] = fold3(dot(left, block[...], 1, 1))
     copies[7].wait()
     value_ref[...] = fold3(dot(left, held_ref[...], 1, 0))
-    copies[8].wait()
+    for copy in copies[:7] + copies[8:]:
+        copy.wait()
 
 
 def right_last_kernel(p_ref, value_ref, projected_ref, grads_ref, block_ref, old_ref, out_ref, rows_ref, total, sem):
@@ -263,7 +263,7 @@
         far(err),
         far(out_grad),
         *blocks,
-        spaces=[VMEM, hbm, hbm] + [pl.ANY] * 7,
+        spaces=[VMEM, hbm, hbm] + [VMEM] * 7,
         scratch=[dma((9,))],
     )
     p, grads, near = kept(p_factor), kept(grads), kept(near)

time: 90.8 us -> 92.1 us (1.014)
  Pallas kernels: 18.1 us -> 19.4 us
    pallas_call x14, Pallas kernels: 15.2 us -> 16.5 us  [local(): pl.pallas_call(kernel, out_shape=out, in_specs=[pl.BlockSpec(memory_space...]
  transfers between devices with their start and end apart: 16 -> 16, of which waited for: 6 -> 6; matrix products, arithmetic and copies ran while one was open for 1% -> 1% of each run, Pallas kernels for 16% -> 17%
where the time goes in v7:
time: 92.1 us; the launch traced here: 91.8 us
  blocking collectives  33.6 us (36%)
  starting transfers between devices  32.3 us (35%)
  Pallas kernels  19.4 us (21%)
  waiting for transfers between devices  4.97 us (5%)
  between operations  0.96 us (1%)
    all_to_all x3, blocking collectives, exchange(): return lax.all_to_all(x, axis, 0, 0, axis_index_groups=groups)  33.6 us
    pallas_call x14, Pallas kernels, local(): pl.pallas_call(kernel, out_shape=out, in_specs=[pl.BlockSpec(memory_space...  16.5 us
    all_to_all x1, starting transfers between devices, exchange(): return lax.all_to_all(x, axis, 0, 0, axis_index_groups=groups)  7.3 us
    ppermute x6, starting transfers between devices, on_device(): lax.ppermute(mine, 'dp', along(base, 4, step))  6.07 us
    ppermute x3, starting transfers between devices, leftward(): return lax.ppermute(x, 'mp', shift(MP, -1))  5.91 us
    ppermute x1, starting transfers between devices, on_device(): other = lax.ppermute(mine, 'dp', CORES)  5.47 us
    ppermute x1, starting transfers between devices, on_device(): lax.ppermute(part, 'dp', CORES)  3.87 us
    ppermute x4, starting transfers between devices, rightward(): return lax.ppermute(x, 'mp', shift(MP, 1))  3.66 us
  transfers between devices with their start and end apart: 16, of which 6 were waited for; matrix products, arithmetic and copies ran while one was open for 1% of the time, Pallas kernels for 17%

profile of v7, /device:TPU:1, one launch (start us, length us, event | category | flops | bytes accessed | tf_op | source)
XLA Modules:
  0.0 91.8 jit_solution(7668045726875570044)
XLA Ops:
  0.6 0.0 copy-start
  0.6 2.5 %collective-permute-start = (bf16[128,2048]{1,0:T(8,128)(2,1)}, bf16[128,2048]{1,0:T(8,128)(2,1)S(1)}, u32[]{:S(2)}, u32[]{:S(2)}) collective-permute-start(bf16[128,2048]{1,0:T(8,128)(2,1)} %refs_0_.1), channel_id=1, source_target_pairs={{0,1},{1,2},{2,3},{3,4},{4,5},{5,6},{6,7},{7,0},{8,9},{9,10},{10,1... | collective-permute-start | bytes 1572872 | tf_op jit(solution)/shard_map/ppermute | solution.py:225
  3.2 2.6 %shard_map.67 = f32[8,8,128]{2,1,0:T(8,128)} custom-call(f32[8,896]{1,0:T(8,128)} %q_ref.3, bf16[1024,896]{1,0:T(8,128)(2,1)} %g_ref.3), custom_call_target="tpu_custom_call" | custom-call | tf_op jit(solution)/shard_map/pallas_call | solution.py:59
  5.8 7.3 %all-to-all-start = ((f32[8,8,128]{2,1,0:T(8,128)}), f32[8,8,128]{2,1,0:T(8,128)S(1)}, u32[]{:S(2)}, u32[]{:S(2)}) async-start(f32[8,8,128]{2,1,0:T(8,128)} %shard_map.67), calls=%async_computation | async-start | bytes 65536 | tf_op jit(solution)/shard_map/all_to_all | solution.py:217
  13.1 0.0 copy-done
  13.1 2.7 %collective-permute-start.3 = (bf16[128,2048]{1,0:T(8,128)(2,1)S(1)}, bf16[128,2048]{1,0:T(8,128)(2,1)S(1)}, u32[]{:S(2)}, u32[]{:S(2)}) collective-permute-start(bf16[128,2048]{1,0:T(8,128)(2,1)S(1)} %copy-done), channel_id=1, source_target_pairs={{0,7},{1,0},{2,1},{3,2},{4,3},{5,4},{6,5},{7,6},{8,15},{9,8},{10,9... | collective-permute-start | bytes 1572872 | tf_op jit(solution)/shard_map/ppermute | solution.py:228
  15.8 2.8 %shard_map.68.more_ref = f32[8,2048]{1,0:T(8,128)S(1)} custom-call(f32[8,896]{1,0:T(8,128)} %q_ref.3, bf16[2048,896]{1,0:T(8,128)(2,1)} %bitcast.2), custom_call_target="tpu_custom_call" | custom-call | tf_op jit(solution)/shard_map/pallas_call | solution.py:59
  18.6 2.3 %all-to-all-done.parts_ref = f32[8,8,128]{2,1,0:T(8,128)S(1)} async-done(((f32[8,8,128]{2,1,0:T(8,128)}), f32[8,8,128]{2,1,0:T(8,128)S(1)}, u32[]{:S(2)}, u32[]{:S(2)}) %all-to-all-start) | async-done | bytes 32800 | tf_op jit(solution)/shard_map/all_to_all | solution.py:217
  20.8 0.2 shard_map.69
  21.0 0.0 collective-permute-done.refs_1_
  21.0 0.1 collective-permute-start.2
  21.1 13.1 %all_to_all.20.parts_ref = f32[16,8,128]{2,1,0:T(8,128)S(1)} all-to-all(f32[16,8,128]{2,1,0:T(8,128)S(1)} %shard_map.69), channel_id=1, replica_groups={{0,16,32,48,64,80,96,112,128,144,160,176,192,208,224,240},{8,24,40,56,7..., dimensions={0} | all-to-all | bytes 131072 | tf_op jit(solution)/shard_map/all_to_all | solution.py:217
  34.2 0.0 collective-permute-done.3.refs_2_
  34.2 2.7 %collective-permute-start.5 = (bf16[128,2048]{1,0:T(8,128)(2,1)S(1)}, bf16[128,2048]{1,0:T(8,128)(2,1)S(1)}, u32[]{:S(2)}, u32[]{:S(2)}) collective-permute-start(bf16[128,2048]{1,0:T(8,128)(2,1)S(1)} %collective-permute-done.3.refs_2_), channel_id=1, source_target_pairs={{0,7},{1,0},{2,1},{3,2},{4,3},{5,4},{6,5},{7,6},{8,15},{9,8},{10,9... | collective-permute-start | bytes 1572872 | tf_op jit(solution)/shard_map/ppermute | solution.py:228
  37.0 0.0 collective-permute-done.2.refs_3_
  37.0 0.0 collective-permute-start.4
  37.0 3.9 %collective-permute-start.1 = (f32[8,128]{1,0:T(8,128)S(1)}, f32[8,128]{1,0:T(8,128)S(1)}, u32[]{:S(2)}, u32[]{:S(2)}) collective-permute-start(f32[8,128]{1,0:T(8,128)S(1)} %shard_map.70.a_ref), channel_id=1, source_target_pairs={{0,8},{8,0},{16,24},{24,16},{32,40},{40,32},{48,56},{56,48},{64,72... | collective-permute-start | bytes 12296 | tf_op jit(solution)/shard_map/ppermute | solution.py:246
  40.8 0.8 collective-permute-done.1.b_ref
  41.7 10.7 %all_to_all.21.parts_ref = f32[8,8,128]{2,1,0:T(8,128)S(1)} all-to-all(f32[8,8,128]{2,1,0:T(8,128)S(1)} %shard_map.71), channel_id=1, replica_groups=mesh['dp'=32,'mp'=8] {'mp'}, dimensions={0} | all-to-all | bytes 65536 | tf_op jit(solution)/shard_map/all_to_all | solution.py:217
  52.4 0.0 collective-permute-done.5.refs_4_
  52.4 0.5 collective-permute-start.6
  52.9 0.0 collective-permute-done.4.refs_5_
  52.9 1.0 %collective-permute-start.7 = (bf16[128,2048]{1,0:T(8,128)(2,1)S(1)}, bf16[128,2048]{1,0:T(8,128)(2,1)S(1)}, u32[]{:S(2)}, u32[]{:S(2)}) collective-permute-start(bf16[128,2048]{1,0:T(8,128)(2,1)S(1)} %collective-permute-done.4.refs_5_), channel_id=1, source_target_pairs={{0,1},{1,2},{2,3},{3,4},{4,5},{5,6},{6,7},{7,0},{8,9},{9,10},{10,1... | collective-permute-start | bytes 1572872 | tf_op jit(solution)/shard_map/ppermute | solution.py:225
  54.0 9.8 %all_to_all.22.parts_ref = f32[16,8,128]{2,1,0:T(8,128)S(1)} all-to-all(f32[16,8,128]{2,1,0:T(8,128)S(1)} %shard_map.72), channel_id=1, replica_groups={{0,16,32,48,64,80,96,112,128,144,160,176,192,208,224,240},{8,24,40,56,7..., dimensions={0} | all-to-all | bytes 131072 | tf_op jit(solution)/shard_map/all_to_all | solution.py:217
  63.7 0.3 collective-permute-done.6.refs_6_
  64.1 4.8 %shard_map.73 = (f32[8,2048]{1,0:T(8,128)S(1)}, f32[8,896]{1,0:T(8,128)S(1)}, f32[8,1024]{1,0:T(8,128)S(1)}, bf16[1024,2048]{1,0:T(8,128)(2,1)S(1)}, bf16[1024,8...) custom-call(f32[16,8,128]{2,1,0:T(8,128)S(1)} %all_to_all.22.parts_ref, bf16[2048,896]{1,0:T(8,128)(2,1)} %bitcast.3, ...), custom_call_target="tpu_custom_call" | custom-call | tf_op jit(solution)/shard_map/pallas_call | solution.py:59
  68.8 0.0 collective-permute-done.7.block_ref
  68.8 0.9 shard_map.74
  69.7 1.0 %collective-permute-start.10 = (f32[8,896]{1,0:T(8,128)S(1)}, f32[8,896]{1,0:T(8,128)S(1)}, u32[]{:S(2)}, u32[]{:S(2)}) collective-permute-start(f32[8,896]{1,0:T(8,128)S(1)} %get-tuple-element.51.own_ref), channel_id=1, source_target_pairs={{0,48},{8,56},{16,0},{24,8},{32,16},{40,24},{48,32},{56,40},{64,11... | collective-permute-start | bytes 86024 | tf_op jit(solution)/shard_map/ppermute | solution.py:286
  70.7 1.2 %collective-permute-start.8 = (f32[8,896]{1,0:T(8,128)S(1)}, f32[8,896]{1,0:T(8,128)S(1)}, u32[]{:S(2)}, u32[]{:S(2)}) collective-permute-start(f32[8,896]{1,0:T(8,128)S(1)} %get-tuple-element.51.own_ref), channel_id=1, source_target_pairs={{0,32},{8,40},{16,48},{24,56},{32,0},{40,8},{48,16},{56,24},{64,96... | collective-permute-start | bytes 86024 | tf_op jit(solution)/shard_map/ppermute | solution.py:286
  71.9 0.0 collective-permute-start.9
  71.9 1.3 %shard_map.76 = (f32[512,896]{1,0:T(8,128)S(1)}, bf16[512,48]{1,0:T(8,128)(2,1)S(1)}) custom-call(f32[8,2048]{1,0:T(8,128)S(1)} %get-tuple-element.61.p_ref, bf16[1024,2048]{1,0:T(8,128)(2,1)S(1)} %get-tuple-element.47.rows_ref, bf16[1024,896]{1,0:T(8,128)(2,1)S(1)} %get-tuple-element.43.grads_ref, bf16[2048,896]{1,0:T(8,128)(2,1)S(1)} %get-tuple-element.48.err_ref), custom_call_target="tpu_custom_call" | custom-call | tf_op jit(solution)/shard_map/pallas_call | solution.py:59
  73.2 1.3 %shard_map.75 = (f32[512,896]{1,0:T(8,128)S(1)}, bf16[512,48]{1,0:T(8,128)(2,1)S(1)}) custom-call(f32[8,2048]{1,0:T(8,128)S(1)} %get-tuple-element.61.p_ref, bf16[1024,2048]{1,0:T(8,128)(2,1)S(1)} %get-tuple-element.47.rows_ref, bf16[1024,896]{1,0:T(8,128)(2,1)S(1)} %get-tuple-element.43.grads_ref, bf16[2048,896]{1,0:T(8,128)(2,1)S(1)} %get-tuple-element.48.err_ref), custom_call_target="tpu_custom_call" | custom-call | tf_op jit(solution)/shard_map/pallas_call | solution.py:59
  74.5 0.0 collective-permute-done.10.other_ref
  74.5 0.4 collective-permute-done.8.across_ref
  74.9 0.9 collective-permute-done.9.one_ref
  75.9 1.2 %collective-permute-start.11 = (f32[8,896]{1,0:T(8,128)S(1)}, f32[8,896]{1,0:T(8,128)S(1)}, u32[]{:S(2)}, u32[]{:S(2)}) collective-permute-start(f32[8,896]{1,0:T(8,128)S(1)} %shard_map.77.own_ref), channel_id=1, source_target_pairs={{0,128},{8,136},{16,144},{24,152},{32,160},{40,168},{48,176},{56,1... | collective-permute-start | bytes 86024 | tf_op jit(solution)/shard_map/ppermute | solution.py:286
  77.1 0.3 collective-permute-start.12
  77.4 2.4 %collective-permute-start.13 = (f32[8,896]{1,0:T(8,128)S(1)}, f32[8,896]{1,0:T(8,128)S(1)}, u32[]{:S(2)}, u32[]{:S(2)}) collective-permute-start(f32[8,896]{1,0:T(8,128)S(1)} %shard_map.77.own_ref), channel_id=1, source_target_pairs={{0,192},{8,200},{16,208},{24,216},{32,224},{40,232},{48,240},{56,2... | collective-permute-start | bytes 86024 | tf_op jit(solution)/shard_map/ppermute | solution.py:286
  79.8 1.3 %shard_map.79 = (f32[512,896]{1,0:T(8,128)S(1)}, bf16[512,48]{1,0:T(8,128)(2,1)S(1)}) custom-call(f32[8,2048]{1,0:T(8,128)S(1)} %get-tuple-element.61.p_ref, bf16[1024,2048]{1,0:T(8,128)(2,1)S(1)} %get-tuple-element.47.rows_ref, bf16[1024,896]{1,0:T(8,128)(2,1)S(1)} %get-tuple-element.43.grads_ref, bf16[2048,896]{1,0:T(8,128)(2,1)S(1)} %get-tuple-element.48.err_ref), custom_call_target="tpu_custom_call" | custom-call | tf_op jit(solution)/shard_map/pallas_call | solution.py:59
  81.1 1.3 %shard_map.78 = (f32[512,896]{1,0:T(8,128)S(1)}, bf16[512,48]{1,0:T(8,128)(2,1)S(1)}) custom-call(f32[8,2048]{1,0:T(8,128)S(1)} %get-tuple-element.61.p_ref, bf16[1024,2048]{1,0:T(8,128)(2,1)S(1)} %get-tuple-element.47.rows_ref, bf16[1024,896]{1,0:T(8,128)(2,1)S(1)} %get-tuple-element.43.grads_ref, bf16[2048,896]{1,0:T(8,128)(2,1)S(1)} %get-tuple-element.48.err_ref), custom_call_target="tpu_custom_call" | custom-call | tf_op jit(solution)/shard_map/pallas_call | solution.py:59
  82.4 0.0 collective-permute-done.11.across_ref
  82.4 0.0 collective-permute-done.12.one_ref
  82.4 0.0 collective-permute-done.13.other_ref
  82.4 5.5 %collective-permute-start.14 = (f32[8,896]{1,0:T(8,128)S(1)}, f32[8,896]{1,0:T(8,128)S(1)}, u32[]{:S(2)}, u32[]{:S(2)}) collective-permute-start(f32[8,896]{1,0:T(8,128)S(1)} %shard_map.80.mine_ref), channel_id=1, source_target_pairs={{0,8},{8,0},{16,24},{24,16},{32,40},{40,32},{48,56},{56,48},{64,72... | collective-permute-start | bytes 86024 | tf_op jit(solution)/shard_map/ppermute | solution.py:288
  87.9 0.6 copy.9
  88.5 0.2 collective-permute-done.14.other_ref
  88.8 2.9 %shard_map.81 = (bf16[2048,896]{1,0:T(8,128)(2,1)}, f32[8,896]{1,0:T(8,128)}) custom-call(f32[8,896]{1,0:T(8,128)S(1)} %shard_map.80.mine_ref, f32[8,896]{1,0:T(8,128)S(1)} %collective-permute-done.14.other_ref, f32[512,896]{1,0:T(8,128)S(1)} %get-tuple-element.49.refs_0_, f32[512,896]{1,0:T(8,128)S(1)} %get-tuple-element.50.refs_1_, ...), custom_call_target="tpu_custom_call" | custom-call | tf_op jit(solution)/shard_map/pallas_call | solution.py:289
  (5 shorter events, 0.1 us)
Async XLA Ops:
  0.6 12.5 %copy-start = (bf16[128,2048]{1,0:T(8,128)(2,1)S(1)}, bf16[128,2048]{1,0:T(8,128)(2,1)}, u32[]{:S(2)}) copy-start(bf16[128,2048]{1,0:T(8,128)(2,1)} %refs_0_.1) | copy-start | bytes 1572868
  0.6 20.4 %collective-permute-start = (bf16[128,2048]{1,0:T(8,128)(2,1)}, bf16[128,2048]{1,0:T(8,128)(2,1)S(1)}, u32[]{:S(2)}, u32[]{:S(2)}) collective-permute-start(bf16[128,2048]{1,0:T(8,128)(2,1)} %refs_0_.1), channel_id=1, source_target_pairs={{0,1},{1,2},{2,3},{3,4},{4,5},{5,6},{6,7},{7,0},{8,9},{9,10},{10,1... | collective-permute-start | bytes 1572872 | tf_op jit(solution)/shard_map/ppermute | solution.py:225
  5.8 15.0 %all-to-all-start = ((f32[8,8,128]{2,1,0:T(8,128)}), f32[8,8,128]{2,1,0:T(8,128)S(1)}, u32[]{:S(2)}, u32[]{:S(2)}) async-start(f32[8,8,128]{2,1,0:T(8,128)} %shard_map.67), calls=%async_computation | async-start | bytes 65536 | tf_op jit(solution)/shard_map/all_to_all | solution.py:217
  13.1 21.1 %collective-permute-start.3 = (bf16[128,2048]{1,0:T(8,128)(2,1)S(1)}, bf16[128,2048]{1,0:T(8,128)(2,1)S(1)}, u32[]{:S(2)}, u32[]{:S(2)}) collective-permute-start(bf16[128,2048]{1,0:T(8,128)(2,1)S(1)} %copy-done), channel_id=1, source_target_pairs={{0,7},{1,0},{2,1},{3,2},{4,3},{5,4},{6,5},{7,6},{8,15},{9,8},{10,9... | collective-permute-start | bytes 1572872 | tf_op jit(solution)/shard_map/ppermute | solution.py:228
  21.0 15.9 %collective-permute-start.2 = (bf16[128,2048]{1,0:T(8,128)(2,1)S(1)}, bf16[128,2048]{1,0:T(8,128)(2,1)S(1)}, u32[]{:S(2)}, u32[]{:S(2)}) collective-permute-start(bf16[128,2048]{1,0:T(8,128)(2,1)S(1)} %collective-permute-done.refs_1_), channel_id=1, source_target_pairs={{0,1},{1,2},{2,3},{3,4},{4,5},{5,6},{6,7},{7,0},{8,9},{9,10},{10,1... | collective-permute-start | bytes 1572872 | tf_op jit(solution)/shard_map/ppermute | solution.py:225
  34.2 18.2 %collective-permute-start.5 = (bf16[128,2048]{1,0:T(8,128)(2,1)S(1)}, bf16[128,2048]{1,0:T(8,128)(2,1)S(1)}, u32[]{:S(2)}, u32[]{:S(2)}) collective-permute-start(bf16[128,2048]{1,0:T(8,128)(2,1)S(1)} %collective-permute-done.3.refs_2_), channel_id=1, source_target_pairs={{0,7},{1,0},{2,1},{3,2},{4,3},{5,4},{6,5},{7,6},{8,15},{9,8},{10,9... | collective-permute-start | bytes 1572872 | tf_op jit(solution)/shard_map/ppermute | solution.py:228
  37.0 16.0 %collective-permute-start.4 = (bf16[128,2048]{1,0:T(8,128)(2,1)S(1)}, bf16[128,2048]{1,0:T(8,128)(2,1)S(1)}, u32[]{:S(2)}, u32[]{:S(2)}) collective-permute-start(bf16[128,2048]{1,0:T(8,128)(2,1)S(1)} %collective-permute-done.2.refs_3_), channel_id=1, source_target_pairs={{0,1},{1,2},{2,3},{3,4},{4,5},{5,6},{6,7},{7,0},{8,9},{9,10},{10,1... | collective-permute-start | bytes 1572872 | tf_op jit(solution)/shard_map/ppermute | solution.py:225
  37.0 4.7 %collective-permute-start.1 = (f32[8,128]{1,0:T(8,128)S(1)}, f32[8,128]{1,0:T(8,128)S(1)}, u32[]{:S(2)}, u32[]{:S(2)}) collective-permute-start(f32[8,128]{1,0:T(8,128)S(1)} %shard_map.70.a_ref), channel_id=1, source_target_pairs={{0,8},{8,0},{16,24},{24,16},{32,40},{40,32},{48,56},{56,48},{64,72... | collective-permute-start | bytes 12296 | tf_op jit(solution)/shard_map/ppermute | solution.py:246
  52.4 11.6 %collective-permute-start.6 = (bf16[128,2048]{1,0:T(8,128)(2,1)S(1)}, bf16[128,2048]{1,0:T(8,128)(2,1)S(1)}, u32[]{:S(2)}, u32[]{:S(2)}) collective-permute-start(bf16[128,2048]{1,0:T(8,128)(2,1)S(1)} %collective-permute-done.5.refs_4_), channel_id=1, source_target_pairs={{0,7},{1,0},{2,1},{3,2},{4,3},{5,4},{6,5},{7,6},{8,15},{9,8},{10,9... | collective-permute-start | bytes 1572872 | tf_op jit(solution)/shard_map/ppermute | solution.py:228
  52.9 15.9 %collective-permute-start.7 = (bf16[128,2048]{1,0:T(8,128)(2,1)S(1)}, bf16[128,2048]{1,0:T(8,128)(2,1)S(1)}, u32[]{:S(2)}, u32[]{:S(2)}) collective-permute-start(bf16[128,2048]{1,0:T(8,128)(2,1)S(1)} %collective-permute-done.4.refs_5_), channel_id=1, source_target_pairs={{0,1},{1,2},{2,3},{3,4},{4,5},{5,6},{6,7},{7,0},{8,9},{9,10},{10,1... | collective-permute-start | bytes 1572872 | tf_op jit(solution)/shard_map/ppermute | solution.py:225
  69.7 4.8 %collective-permute-start.10 = (f32[8,896]{1,0:T(8,128)S(1)}, f32[8,896]{1,0:T(8,128)S(1)}, u32[]{:S(2)}, u32[]{:S(2)}) collective-permute-start(f32[8,896]{1,0:T(8,128)S(1)} %get-tuple-element.51.own_ref), channel_id=1, source_target_pairs={{0,48},{8,56},{16,0},{24,8},{32,16},{40,24},{48,32},{56,40},{64,11... | collective-permute-start | bytes 86024 | tf_op jit(solution)/shard_map/ppermute | solution.py:286
  70.7 4.2 %collective-permute-start.8 = (f32[8,896]{1,0:T(8,128)S(1)}, f32[8,896]{1,0:T(8,128)S(1)}, u32[]{:S(2)}, u32[]{:S(2)}) collective-permute-start(f32[8,896]{1,0:T(8,128)S(1)} %get-tuple-element.51.own_ref), channel_id=1, source_target_pairs={{0,32},{8,40},{16,48},{24,56},{32,0},{40,8},{48,16},{56,24},{64,96... | collective-permute-start | bytes 86024 | tf_op jit(solution)/shard_map/ppermute | solution.py:286
  71.9 3.9 %collective-permute-start.9 = (f32[8,896]{1,0:T(8,128)S(1)}, f32[8,896]{1,0:T(8,128)S(1)}, u32[]{:S(2)}, u32[]{:S(2)}) collective-permute-start(f32[8,896]{1,0:T(8,128)S(1)} %get-tuple-element.51.own_ref), channel_id=1, source_target_pairs={{0,16},{8,24},{16,32},{24,40},{32,48},{40,56},{48,0},{56,8},{64,80... | collective-permute-start | bytes 86024 | tf_op jit(solution)/shard_map/ppermute | solution.py:286
  75.9 6.5 %collective-permute-start.11 = (f32[8,896]{1,0:T(8,128)S(1)}, f32[8,896]{1,0:T(8,128)S(1)}, u32[]{:S(2)}, u32[]{:S(2)}) collective-permute-start(f32[8,896]{1,0:T(8,128)S(1)} %shard_map.77.own_ref), channel_id=1, source_target_pairs={{0,128},{8,136},{16,144},{24,152},{32,160},{40,168},{48,176},{56,1... | collective-permute-start | bytes 86024 | tf_op jit(solution)/shard_map/ppermute | solution.py:286
  77.1 5.3 %collective-permute-start.12 = (f32[8,896]{1,0:T(8,128)S(1)}, f32[8,896]{1,0:T(8,128)S(1)}, u32[]{:S(2)}, u32[]{:S(2)}) collective-permute-start(f32[8,896]{1,0:T(8,128)S(1)} %shard_map.77.own_ref), channel_id=1, source_target_pairs={{0,64},{8,72},{16,80},{24,88},{32,96},{40,104},{48,112},{56,120},{... | collective-permute-start | bytes 86024 | tf_op jit(solution)/shard_map/ppermute | solution.py:286
  77.4 5.0 %collective-permute-start.13 = (f32[8,896]{1,0:T(8,128)S(1)}, f32[8,896]{1,0:T(8,128)S(1)}, u32[]{:S(2)}, u32[]{:S(2)}) collective-permute-start(f32[8,896]{1,0:T(8,128)S(1)} %shard_map.77.own_ref), channel_id=1, source_target_pairs={{0,192},{8,200},{16,208},{24,216},{32,224},{40,232},{48,240},{56,2... | collective-permute-start | bytes 86024 | tf_op jit(solution)/shard_map/ppermute | solution.py:286
  82.4 6.3 %collective-permute-start.14 = (f32[8,896]{1,0:T(8,128)S(1)}, f32[8,896]{1,0:T(8,128)S(1)}, u32[]{:S(2)}, u32[]{:S(2)}) collective-permute-start(f32[8,896]{1,0:T(8,128)S(1)} %shard_map.80.mine_ref), channel_id=1, source_target_pairs={{0,8},{8,0},{16,24},{24,16},{32,40},{40,32},{48,56},{56,48},{64,72... | collective-permute-start | bytes 86024 | tf_op jit(solution)/shard_map/ppermute | solution.py:288
